TPU v7x, 32 devices: a whole 2x2x4 slice. The times are simulated.
32 devices in a mesh: group: 2 (over x), gx: 4 (over y, core), gy: 4 (over z).
Axes of the slice: x: 2, y: 2, z: 4, core: 2. Of those that a mesh axis runs over, the one named last changes fastest.
Arguments:
- wave_now: float32 [4, 64, 32, 512], P('group', None, 'gx', 'gy'), parts along dimension 0, may hold values from -6 to 46
- wave_before: float32 [4, 64, 32, 512], P('group', None, 'gx', 'gy'), parts along dimension 0, may hold values from -6 to 86
- courant: float32 [128, 32, 512], P('group', 'gx', 'gy'), parts along dimension 0, may hold values from 0.03 to 0.15
- records: bfloat16 [512, 2, 4096], P(('group', 'gx', 'gy')), parts along dimension 0, may hold values from -0.59765625 to 0.59765625
- signs: int32 [4, 256], P('group', ('gx', 'gy')), parts along dimension 0, may hold values from -1 to 1
- source_x: int32 [512], P(('group', 'gx', 'gy')), parts along dimension 0, may hold values from 0 to 31
- source_y: int32 [512], P(('group', 'gx', 'gy')), parts along dimension 0, may hold values from 0 to 511
- receiver_cell: int32 [8192], P('group'), parts along dimension 0, may hold values from 0 to 1023, as said below
Outputs:
- wave_after: float32 [4, 64, 32, 512], P('group', None, 'gx', 'gy'), parts along dimension 0
- wave_middle: float32 [4, 64, 32, 512], P('group', None, 'gx', 'gy'), parts along dimension 0
There are 2 independent parts, one for each index of `group`. A program takes and returns all parts, laid end to end along the dimension named above; each array names one. Nothing has to cross between parts.
Inputs may be any that keep to these rules, and one draw needn't show every extreme that they name: `receiver_cell`: receivers of one tile may share a cell.
All inputs are finite; a program needn't handle non-finite values.
Results may differ from a plain program's by a relative error of at most 0.0003.
Values sent between devices are 32-bit elements; how exact they have to be, the bound alone decides.
No kernel may reach another device: no remote copies, remote signals or barrier semaphores. Data moves between devices by JAX's collectives and lax.ppermute only.
A program may use at most 192 MiB of HBM per device.

v0:
```python
import jax
import jax.numpy as jnp
from jax import lax
from jax.sharding import PartitionSpec as P

REC_DEV = 256
RDEPTH = 2


coef_zero = -205.0 / 72.0
coef_rest = (8.0 / 5.0, -1.0 / 5.0, 8.0 / 315.0, -1.0 / 560.0)


def with_halo(cells, sides, width):
    for axis, dim in sides:
        count = lax.axis_size(axis)
        ends = count - 1
        head = lax.slice_in_dim(cells, 0, width, axis=dim)
        tail = lax.slice_in_dim(cells, cells.shape[dim] - width, cells.shape[dim], axis=dim)
        cells = jnp.concatenate(
            [
                lax.ppermute(tail, axis, [(i, (i + 1) % count) for i in range(ends)]),
                cells,
                lax.ppermute(head, axis, [((i + 1) % count, i) for i in range(ends)]),
            ],
            axis=dim,
        )
    return cells


def laplace(ext, margin):
    depth = ext.shape[1]
    wide_x = ext.shape[2] - 2 * margin
    wide_y = ext.shape[3] - 2 * margin
    padded = jnp.pad(ext, ((0, 0), (4, 4), (0, 0), (0, 0)))
    center = ext[:, :, margin : margin + wide_x, margin : margin + wide_y]
    total = 3.0 * coef_zero * center
    for step in range(1, 5):
        near = padded[
            :, 4 + step : 4 + step + depth, margin : margin + wide_x, margin : margin + wide_y
        ]
        near = (
            near
            + padded[
                :, 4 - step : 4 - step + depth, margin : margin + wide_x, margin : margin + wide_y
            ]
        )
        near = near + ext[:, :, margin + step : margin + step + wide_x, margin : margin + wide_y]
        near = near + ext[:, :, margin - step : margin - step + wide_x, margin : margin + wide_y]
        near = near + ext[:, :, margin : margin + wide_x, margin + step : margin + step + wide_y]
        near = near + ext[:, :, margin : margin + wide_x, margin - step : margin - step + wide_y]
        total = total + coef_rest[step - 1] * near
    return total


def face_layers(field):
    return with_halo(field, (("gx", 2), ("gy", 3)), 4)


def on_device(wave_now, wave_before, courant, records, signs, source_x, source_y, receiver_cell):
    cells_x = wave_now.shape[2]
    cells_y = wave_now.shape[3]
    tiles_y = lax.axis_size("gy")
    total_recv = receiver_cell.shape[0]
    owner = jnp.arange(total_recv, dtype=jnp.int32) // REC_DEV
    gpos_x = owner // tiles_y * cells_x + receiver_cell // cells_y
    gpos_y = owner % tiles_y * cells_y + receiver_cell % cells_y
    span = (cells_x * lax.axis_size("gx") + cells_y * tiles_y) // 4
    radius_sq = jnp.float32(span * span)
    dx = (gpos_x[None, :] - source_x[:, None]).astype(jnp.float32)
    dy = (gpos_y[None, :] - source_y[:, None]).astype(jnp.float32)
    dist = dx * dx + dy * dy
    taper = dist / (dist + radius_sq)
    taped = records.astype(jnp.float32) * taper[:, None, :]
    shot_count = taped.shape[0]
    flat_taped = taped.reshape(shot_count, 2 * total_recv)
    partial_res = jnp.dot(
        signs.astype(jnp.float32),
        flat_taped,
        precision=lax.Precision.HIGHEST,
        preferred_element_type=jnp.float32,
    ).reshape(2, 2, total_recv)
    residual = lax.psum_scatter(partial_res, ("gx", "gy"), scatter_dimension=2, tiled=True)
    tile = lax.axis_index("gx") * tiles_y + lax.axis_index("gy")
    own_cells = lax.dynamic_slice_in_dim(receiver_cell, tile * REC_DEV, REC_DEV, 0)
    layer = jnp.zeros((2, 2, cells_x * cells_y), jnp.float32).at[:, :, own_cells].add(residual)
    layer = layer.reshape(2, 2, cells_x, cells_y)
    ext_now = face_layers(wave_now)
    wave_middle = 2.0 * wave_now - wave_before + courant * laplace(ext_now, 4)
    wave_middle = wave_middle.at[:, RDEPTH].add(layer[:, 0])
    ext_middle = face_layers(wave_middle)
    wave_after = 2.0 * wave_middle - wave_now + courant * laplace(ext_middle, 4)
    wave_after = wave_after.at[:, RDEPTH].add(layer[:, 1])
    return (wave_after, wave_middle)


def solution(mesh):
    return jax.shard_map(
        on_device,
        mesh=mesh,
        in_specs=(
            P("group", None, "gx", "gy"),
            P("group", None, "gx", "gy"),
            P("group", "gx", "gy"),
            P(("group", "gx", "gy"), None, None),
            P("group", ("gx", "gy")),
            P(("group", "gx", "gy")),
            P(("group", "gx", "gy")),
            P("group"),
        ),
        out_specs=(P("group", None, "gx", "gy"), P("group", None, "gx", "gy")),
        check_vma=False,
    )
```

profile of v0, /device:TPU:0, one launch (start us, length us, event | category | flops | bytes accessed | tf_op | source)
XLA Modules:
  0.0 252.3 jit_solution(12016462765928305005)
XLA Ops:
  7.2 1.3 fusion.78
  8.6 2.4 collective-permute-start
  11.0 0.7 copy.93
  11.7 1.3 collective-permute-start.1
  13.0 0.7 fusion.62
  13.7 0.8 add_divide_fusion
  14.6 0.3 convert_multiply_fusion
  14.9 0.3 copy.96
  15.2 0.4 convolution_bitcast_fusion
  15.7 4.4 %copy.80 = f32[2,2,4096]{1,0,2:T(2,128)} copy(f32[2,2,4096]{2,1,0:T(2,128)S(1)} %reshape.135) | data formatting | bytes 131072 | tf_op jit(solution)/shard_map/reshape | solution.py:82
  20.1 0.9 compare_select_fusion
  21.1 0.4 copy.67
  21.6 1.0 copy.69
  22.6 1.4 copy.68
  24.0 0.6 dynamic-slice.14
  25.2 111.1 %all-reduce.5.cloned.1.call-done = f32[2,2,4096]{1,0,2:T(2,128)} async-done(((f32[2,2,4096]{1,0,2:T(2,128)}), f32[2,2,4096]{1,0,2:T(2,128)}) %all-reduce.5.cloned.1.call-update) | async-done | bytes 65552
  136.3 1.0 dynamic-slice_bitcast_fusion
  137.3 0.3 broadcast_in_dim.4
  137.6 8.3 %scatter_fusion = f32[2,2,1024]{1,0,2:T(2,128)S(1)} fusion(f32[2,2,1024]{1,0,2:T(2,128)S(1)} %broadcast_in_dim.4, s32[256]{0:T(256)S(1)} %compare_select_fusion, f32[256,2,2]{2,1,0:T(2,128)S(1)} %dynamic-slice_bitcast_fusion), kind=kCustom, calls=%fused_computation | custom fusion | flops 1024 | bytes 13312 | tf_op jit(solution)/shard_map/scatter-add | solution.py:86
  145.9 0.2 copy.73
  146.2 0.2 copy.75
  146.5 3.1 %collective-permute-start.2 = (f32[2,64,16,4]{1,2,3,0:T(8,128)S(1)}, f32[2,64,16,4]{1,2,3,0:T(8,128)S(1)}, u32[]{:S(2)}, u32[]{:S(2)}) collective-permute-start(f32[2,64,16,4]{1,2,3,0:T(8,128)S(1)} %get-tuple-element.39), channel_id=1, source_target_pairs={{0,1},{1,2},{2,3},{4,5},{5,6},{6,7},{8,9},{9,10},{10,11},{12,13},{... | collective-permute-start | bytes 98312 | tf_op jit(solution)/shard_map/ppermute | solution.py:22
  149.6 1.3 collective-permute-start.3
  150.9 2.5 fusion.76
  153.3 2.4 collective-permute-done.3
  155.7 2.5 pad_maximum_fusion
  158.2 1.2 select_maximum_fusion.4
  159.4 8.7 %fusion.36 = f32[2,64,8,128]{1,2,3,0:T(8,128)S(1)} fusion(f32[2,64,8,128]{1,2,3,0:T(8,128)S(1)} %copy.67, f32[2,64,4,128]{1,2,3,0:T(4,128)S(1)} %copy.73, f32[2,64,4,128]{1,2,3,0:T(4,128)S(1)} %copy.75, f32[2,64,16,132]{1,2,3,0:T(8,128)} %get-tuple-element.37, f32[2,64,16,132]{1,2,3,0:T(8,128)} %get-tuple-element.36, ...), kind=kLoop, calls=%fused_computation.76 | loop fusion | flops 5373952 | bytes 10747904 | tf_op jit(solution)/shard_map/add | solution.py:89
  168.2 1.9 slice_add_fusion.7
  170.1 21.0 %scatter-add.18 = f32[2,64,8,128]{1,2,3,0:T(8,128)S(1)} dynamic-update-slice(f32[2,64,8,128]{1,2,3,0:T(8,128)S(1)} %fusion.36, f32[2,1,8,128]{1,2,3,0:T(8,128)S(1)} %slice_add_fusion.7, s32[]{:T(128)} %constant.128.clone.1, s32[]{:T(128)} %constant.136.clone.1, s32[]{:T(128)} %constant.128.clone.1, s32[]{:T(128)} %constant.128.clone.1) | dynamic-update-slice | bytes 16388 | tf_op jit(solution)/shard_map/scatter-add | solution.py:90
  191.1 0.2 fusion.77
  191.2 0.2 copy.83
  191.4 1.3 collective-permute-start.4
  192.7 0.2 copy.84
  192.9 1.3 collective-permute-start.5
  194.2 0.2 copy.85
  194.5 3.2 %collective-permute-done.5 = f32[2,64,4,128]{3,1,2,0:T(8,128)} collective-permute-done((f32[2,64,4,128]{3,1,2,0:T(8,128)S(1)}, f32[2,64,4,128]{3,1,2,0:T(8,128)}, u32[]{:S(2)}, u32[]{:S(2)}) %collective-permute-start.5) | collective-permute-done | bytes 262176 | tf_op jit(solution)/shard_map/ppermute | solution.py:24
  197.6 1.2 copy.86
  198.9 3.1 %collective-permute-start.6 = (f32[2,64,16,4]{1,2,3,0:T(8,128)S(1)}, f32[2,64,16,4]{1,2,3,0:T(8,128)S(1)}, u32[]{:S(2)}, u32[]{:S(2)}) collective-permute-start(f32[2,64,16,4]{1,2,3,0:T(8,128)S(1)} %get-tuple-element.35), channel_id=1, source_target_pairs={{0,1},{1,2},{2,3},{4,5},{5,6},{6,7},{8,9},{9,10},{10,11},{12,13},{... | collective-permute-start | bytes 98312 | tf_op jit(solution)/shard_map/ppermute | solution.py:22
  202.0 1.3 collective-permute-start.7
  203.3 1.2 copy.91
  204.4 3.7 %collective-permute-done.7 = f32[2,64,16,4]{1,2,3,0:T(8,128)S(1)} collective-permute-done((f32[2,64,16,4]{1,2,3,0:T(8,128)S(1)}, f32[2,64,16,4]{1,2,3,0:T(8,128)S(1)}, u32[]{:S(2)}, u32[]{:S(2)}) %collective-permute-start.7) | collective-permute-done | bytes 32800 | tf_op jit(solution)/shard_map/ppermute | solution.py:24
  208.1 1.2 select_maximum_fusion
  209.3 2.5 pad_maximum_fusion.1
  211.8 9.1 %fusion.9 = f32[2,64,8,128]{1,2,3,0:T(8,128)} fusion(f32[2,64,8,128]{1,2,3,0:T(8,128)S(1)} %scatter-add.18, f32[2,64,4,128]{1,2,3,0:T(4,128)S(1)} %copy.85, f32[2,64,4,128]{1,2,3,0:T(4,128)S(1)} %copy.86, f32[2,64,16,132]{1,2,3,0:T(8,128)} %get-tuple-element.33, f32[2,64,16,132]{1,2,3,0:T(8,128)} %get-tuple-element.32, ...), kind=kLoop, calls=%fused_computation.49 | loop fusion | flops 5373952 | bytes 10747904 | tf_op jit(solution)/shard_map/add | solution.py:92
  220.9 2.3 slice_add_fusion
  223.3 21.0 %scatter-add.19 = f32[2,64,8,128]{1,2,3,0:T(8,128)S(1)} dynamic-update-slice(f32[2,64,8,128]{1,2,3,0:T(8,128)S(1)} %copy-done, f32[2,1,8,128]{1,2,3,0:T(8,128)S(1)} %slice_add_fusion, s32[]{:T(128)} %constant.128.clone.1, s32[]{:T(128)} %constant.136.clone.1, s32[]{:T(128)} %constant.128.clone.1, s32[]{:T(128)} %constant.128.clone.1) | dynamic-update-slice | bytes 16388 | tf_op jit(solution)/shard_map/scatter-add | solution.py:93
  244.3 1.2 copy.90
  (29 shorter events, 0.4 us)
Async XLA Ops:
  7.2 7.4 %copy-start.6 = (bf16[16,2,4096]{2,1,0:T(2,128)(2,1)S(1)}, bf16[16,2,4096]{2,1,0:T(2,128)(2,1)}, u32[]{:S(2)}) copy-start(bf16[16,2,4096]{2,1,0:T(2,128)(2,1)} %param.15) | copy-start | bytes 786436
  7.2 8.0 %copy-start.7 = (s32[2,16]{1,0:T(2,128)S(1)}, s32[2,16]{1,0:T(2,128)}, u32[]{:S(2)}) copy-start(s32[2,16]{1,0:T(2,128)} %param.16) | copy-start | bytes 388
  7.2 129.2 %all-reduce.5.cloned.1.call-start = ((), (), s32[]{:S(2)}) async-start(), calls=%async_computation | async-start | bytes 8388608
  8.6 137.3 %collective-permute-start = (f32[2,64,4,128]{3,1,2,0:T(8,128)S(1)}, f32[2,64,4,128]{3,1,2,0:T(8,128)S(1)}, u32[]{:S(2)}, u32[]{:S(2)}) collective-permute-start(f32[2,64,4,128]{3,1,2,0:T(8,128)S(1)} %copy.92), channel_id=1, source_target_pairs={{0,4},{4,8},{8,12},{1,5},{5,9},{9,13},{2,6},{6,10},{10,14},{3,7},{... | collective-permute-start | bytes 786440 | tf_op jit(solution)/shard_map/ppermute | solution.py:22
  11.7 134.5 %collective-permute-start.1 = (f32[2,64,4,128]{3,1,2,0:T(8,128)}, f32[2,64,4,128]{3,1,2,0:T(8,128)S(1)}, u32[]{:S(2)}, u32[]{:S(2)}) collective-permute-start(f32[2,64,4,128]{3,1,2,0:T(8,128)} %copy.93), channel_id=1, source_target_pairs={{4,0},{8,4},{12,8},{5,1},{9,5},{13,9},{6,2},{10,6},{14,10},{7,3},{... | collective-permute-start | bytes 786440 | tf_op jit(solution)/shard_map/ppermute | solution.py:24
  20.1 1.1 copy-start.3
  20.1 1.5 copy-start.5
  20.1 2.5 copy-start.4
  20.1 3.9 %copy-start.8 = (u32[32]{0:T(128)S(1)}, u32[32]{0:T(128)}, u32[]{:S(2)}) copy-start(u32[32]{0:T(128)} %constant.150) | copy-start | bytes 388
  146.5 6.9 %collective-permute-start.2 = (f32[2,64,16,4]{1,2,3,0:T(8,128)S(1)}, f32[2,64,16,4]{1,2,3,0:T(8,128)S(1)}, u32[]{:S(2)}, u32[]{:S(2)}) collective-permute-start(f32[2,64,16,4]{1,2,3,0:T(8,128)S(1)} %get-tuple-element.39), channel_id=1, source_target_pairs={{0,1},{1,2},{2,3},{4,5},{5,6},{6,7},{8,9},{9,10},{10,11},{12,13},{... | collective-permute-start | bytes 98312 | tf_op jit(solution)/shard_map/ppermute | solution.py:22
  149.6 6.2 %collective-permute-start.3 = (f32[2,64,16,4]{1,2,3,0:T(8,128)S(1)}, f32[2,64,16,4]{1,2,3,0:T(8,128)S(1)}, u32[]{:S(2)}, u32[]{:S(2)}) collective-permute-start(f32[2,64,16,4]{1,2,3,0:T(8,128)S(1)} %get-tuple-element.38), channel_id=1, source_target_pairs={{1,0},{2,1},{3,2},{5,4},{6,5},{7,6},{9,8},{10,9},{11,10},{13,12},{... | collective-permute-start | bytes 98312 | tf_op jit(solution)/shard_map/ppermute | solution.py:24
  158.2 1.2 copy-start.1
  191.4 2.8 %collective-permute-start.4 = (f32[2,64,4,128]{3,1,2,0:T(8,128)S(1)}, f32[2,64,4,128]{3,1,2,0:T(8,128)S(1)}, u32[]{:S(2)}, u32[]{:S(2)}) collective-permute-start(f32[2,64,4,128]{3,1,2,0:T(8,128)S(1)} %copy.83), channel_id=1, source_target_pairs={{0,4},{4,8},{8,12},{1,5},{5,9},{9,13},{2,6},{6,10},{10,14},{3,7},{... | collective-permute-start | bytes 786440 | tf_op jit(solution)/shard_map/ppermute | solution.py:22
  192.9 4.7 %collective-permute-start.5 = (f32[2,64,4,128]{3,1,2,0:T(8,128)S(1)}, f32[2,64,4,128]{3,1,2,0:T(8,128)}, u32[]{:S(2)}, u32[]{:S(2)}) collective-permute-start(f32[2,64,4,128]{3,1,2,0:T(8,128)S(1)} %copy.84), channel_id=1, source_target_pairs={{4,0},{8,4},{12,8},{5,1},{9,5},{13,9},{6,2},{10,6},{14,10},{7,3},{... | collective-permute-start | bytes 786440 | tf_op jit(solution)/shard_map/ppermute | solution.py:24
  198.9 5.5 %collective-permute-start.6 = (f32[2,64,16,4]{1,2,3,0:T(8,128)S(1)}, f32[2,64,16,4]{1,2,3,0:T(8,128)S(1)}, u32[]{:S(2)}, u32[]{:S(2)}) collective-permute-start(f32[2,64,16,4]{1,2,3,0:T(8,128)S(1)} %get-tuple-element.35), channel_id=1, source_target_pairs={{0,1},{1,2},{2,3},{4,5},{5,6},{6,7},{8,9},{9,10},{10,11},{12,13},{... | collective-permute-start | bytes 98312 | tf_op jit(solution)/shard_map/ppermute | solution.py:22
  202.0 6.2 %collective-permute-start.7 = (f32[2,64,16,4]{1,2,3,0:T(8,128)S(1)}, f32[2,64,16,4]{1,2,3,0:T(8,128)S(1)}, u32[]{:S(2)}, u32[]{:S(2)}) collective-permute-start(f32[2,64,16,4]{1,2,3,0:T(8,128)S(1)} %get-tuple-element.34), channel_id=1, source_target_pairs={{1,0},{2,1},{3,2},{5,4},{6,5},{7,6},{9,8},{10,9},{11,10},{13,12},{... | collective-permute-start | bytes 98312 | tf_op jit(solution)/shard_map/ppermute | solution.py:24
  209.3 2.5 copy-start.2
  220.9 2.3 copy-start
Sparse Core Ops, SparseCore 0:
  20.2 116.0 all-reduce.4
where the time goes:
time: 256 us; the launch traced here: 252 us
  waiting for transfers between devices  120 us (47%)
  local copies, waits for them, and re-layouts  60.9 us (24%)
  other arithmetic  40.5 us (16%)
  starting transfers between devices  15 us (6%)
  between operations  15 us (6%)
    unnamed x2, waiting for transfers between devices  111 us
    scatter-add x1, local copies, waits for them, and re-layouts, on_device(): wave_middle = wave_middle.at[:, RDEPTH].add(layer[:, 0])  21 us
    scatter-add x1, local copies, waits for them, and re-layouts, on_device(): wave_after = wave_after.at[:, RDEPTH].add(layer[:, 1])  21 us
    ppermute x4, starting transfers between devices, with_halo(): lax.ppermute(tail, axis, [(i, (i + 1) % count) for i in range(ends)])  9.84 us
    ppermute x4, waiting for transfers between devices, with_halo(): lax.ppermute(head, axis, [((i + 1) % count, i) for i in range(ends)])  9.27 us
    add x1, other arithmetic, on_device(): wave_after = 2.0 * wave_middle - wave_now + courant * laplace(ext_middle, 4)  9.12 us
    add x1, other arithmetic, on_device(): wave_middle = 2.0 * wave_now - wave_before + courant * laplace(ext_now, 4)  8.73 us
    scatter-add x1, other arithmetic, on_device(): jnp.zeros((2, 2, cells_x * cells_y), jnp.float32).at[:, :, own_cells]  8.32 us
  transfers between devices with their start and end apart: 9, of which 4 were waited for; matrix products, arithmetic and copies ran while one was open for 10% of the time, Pallas kernels for 0%

commit v1 on v0

v1 whole, which is shorter than its diff:
```python
import functools

import jax
import jax.numpy as jnp
from jax import lax
from jax.experimental import pallas as pl
from jax.experimental.pallas import tpu as pltpu
from jax.sharding import PartitionSpec as P

REC_DEV = 256
RDEPTH = 2
HALO = 4
AXES = ("group", "gx", "gy")

coef_zero = -205.0 / 72.0
coef_rest = (8.0 / 5.0, -1.0 / 5.0, 8.0 / 315.0, -1.0 / 560.0)

VM = pl.BlockSpec(memory_space=pltpu.VMEM)
SM = pl.BlockSpec(memory_space=pltpu.SMEM)


def rows_of(shape):
    return lax.broadcasted_iota(jnp.int32, shape, len(shape) - 2)


def lanes_of(shape):
    return lax.broadcasted_iota(jnp.int32, shape, len(shape) - 1)


def head_rows(first, second):
    return jnp.where(rows_of(first.shape) < HALO, first, pltpu.roll(second, HALO, 0))


def tail_rows(first, second):
    return jnp.where(rows_of(first.shape) < HALO, pltpu.roll(first, HALO, 0), second)


def put_columns(cells, depth, tail_ref, head_ref, field):
    wide = cells.shape[-1]
    per = wide // HALO
    slot, part = lax.rem(depth, per), lax.div(depth, per)
    mine = lanes_of(cells.shape) // HALO == slot
    head = pltpu.roll(cells, slot * HALO, 1)
    tail = pltpu.roll(cells, lax.rem(slot * HALO + HALO, wide), 1)
    head_ref[field, part] = jnp.where(mine, head, head_ref[field, part])
    tail_ref[field, part] = jnp.where(mine, tail, tail_ref[field, part])


def side_columns(next_tile, prev_tile, depth):
    wide = next_tile.shape[-1]
    slot = lax.rem(depth, wide // HALO)
    after = pltpu.roll(next_tile, lax.rem(wide - slot * HALO, wide), 1)
    before = pltpu.roll(prev_tile, wide - HALO - slot * HALO, 1)
    return jnp.where(lanes_of(next_tile.shape) < HALO, after, before)


def shifted_pair(cells, beside, step, axis):
    size = cells.shape[axis]
    place = lax.broadcasted_iota(jnp.int32, cells.shape, axis)
    up = pltpu.roll(jnp.where(place < step, beside, cells), size - step, axis)
    down = pltpu.roll(jnp.where(place >= size - step, beside, cells), step, axis)
    return up + down


def laplace(ref, field, depth, static_depth, deep, beside_x, beside_y):
    cells = ref[field, depth]
    total = 3.0 * coef_zero * cells
    for step in range(1, HALO + 1):
        near = shifted_pair(cells, beside_x, step, 0) + shifted_pair(cells, beside_y, step, 1)
        if static_depth is None or static_depth + step < deep:
            near = near + ref[field, depth + step]
        if static_depth is None or static_depth >= step:
            near = near + ref[field, depth - step]
        total = total + coef_rest[step - 1] * near
    return cells, total


def over_depth(deep, body):
    for depth in range(HALO):
        body(depth, depth)

    def inner(depth, carry):
        body(depth, None)
        return carry

    lax.fori_loop(HALO, deep - HALO, inner, 0, unroll=4)
    for depth in range(deep - HALO, deep):
        body(depth, depth)


def pack_kernel(flag_ref, now_ref, xa_ref, xb_ref, ya_ref, yb_ref, tail_ref, head_ref):
    odd_x, odd_y = flag_ref[0] == 1, flag_ref[1] == 1
    deep = now_ref.shape[1]
    tail_ref[...] = jnp.zeros_like(tail_ref)
    head_ref[...] = jnp.zeros_like(head_ref)

    def body(depth, carry):
        first, second = now_ref[0, depth], now_ref[1, depth]
        head, tail = head_rows(first, second), tail_rows(first, second)
        xa_ref[depth] = jnp.where(odd_x, head, tail)
        xb_ref[depth] = jnp.where(odd_x, tail, head)
        put_columns(first, depth, tail_ref, head_ref, 0)
        put_columns(second, depth, tail_ref, head_ref, 1)
        return carry

    lax.fori_loop(0, deep, body, 0, unroll=4)
    ya_ref[...] = jnp.where(odd_y, head_ref[...], tail_ref[...])
    yb_ref[...] = jnp.where(odd_y, tail_ref[...], head_ref[...])


def residual_kernel(tiles_y, cells_x, cells_y, radius_sq, signs_ref, sx_ref, sy_ref, records_ref, cell_ref, out_ref):
    shots = records_ref.shape[0]
    lanes = cell_ref.shape[1]
    shape = (shots, lanes)
    place = rows_of(shape)
    source_x = jnp.zeros(shape, jnp.int32)
    source_y = jnp.zeros(shape, jnp.int32)
    for shot in range(shots):
        source_x = jnp.where(place == shot, sx_ref[shot], source_x)
        source_y = jnp.where(place == shot, sy_ref[shot], source_y)
    per = REC_DEV // lanes

    def tile_step(tile, carry):
        for part in range(per):
            row = tile * per + part
            cell = jnp.broadcast_to(cell_ref[pl.ds(row, 1), :], shape)
            pos_x = lax.div(tile, tiles_y) * cells_x + lax.shift_right_logical(cell, cells_y.bit_length() - 1)
            pos_y = lax.rem(tile, tiles_y) * cells_y + (cell & (cells_y - 1))
            dx = (pos_x - source_x).astype(jnp.float32)
            dy = (pos_y - source_y).astype(jnp.float32)
            dist = dx * dx + dy * dy
            taper = dist / (dist + radius_sq)
            sums = [jnp.zeros((2, lanes), jnp.float32) for _ in range(2)]
            start = pl.multiple_of(row * lanes, lanes)
            for shot in range(shots):
                taped = records_ref[shot, :, pl.ds(start, lanes)].astype(jnp.float32) * taper[shot : shot + 1, :]
                for code in range(2):
                    sums[code] = sums[code] + signs_ref[code, shot].astype(jnp.float32) * taped
            for code in range(2):
                out_ref[tile, 2 * code : 2 * code + 2, part * lanes : (part + 1) * lanes] = sums[code]
        return carry

    lax.fori_loop(0, out_ref.shape[0], tile_step, 0)


def inject_layers(res, cell_row, cells_x, cells_y):
    count = res.shape[1]
    row = lax.shift_right_logical(cell_row, cells_y.bit_length() - 1)
    column = cell_row & (cells_y - 1)
    in_row = rows_of((cells_x, count)) == row
    spread = jnp.concatenate([jnp.where(in_row, res[q : q + 1], 0.0) for q in range(res.shape[0])], axis=0)
    hot = (rows_of((cells_y, count)) == column).astype(jnp.float32)
    out = lax.dot_general(
        spread, hot, (((1,), (1,)), ((), ())),
        precision=lax.Precision.HIGHEST, preferred_element_type=jnp.float32,
    )
    return out


def sides_x(xa, xb, odd_x, no_next, no_prev):
    after = jnp.where(odd_x, xb, xa)
    before = jnp.where(odd_x, xa, xb)
    after = jnp.where(no_next, 0.0, after)
    before = jnp.where(no_prev, 0.0, before)
    low = rows_of(after.shape) < HALO
    first = jnp.where(low, after, pltpu.roll(before, HALO, 0))
    second = jnp.where(low, pltpu.roll(after, HALO, 0), before)
    return first, second


def middle_kernel(
    flag_ref, now_ref, old_ref, courant_ref, xa_ref, xb_ref, ya_ref, yb_ref, res_ref, cell_ref,
    mid_ref, layer_ref, xa_out, xb_out, ya_out, yb_out, tail_ref, head_ref, ny_ref, py_ref,
):
    odd_x, odd_y = flag_ref[0] == 1, flag_ref[1] == 1
    no_px, no_nx, no_py, no_ny = [flag_ref[i] == 1 for i in range(2, 6)]
    deep, cells_x, cells_y = now_ref.shape[1:]
    ny_ref[...] = jnp.where(no_ny, 0.0, jnp.where(odd_y, yb_ref[...], ya_ref[...]))
    py_ref[...] = jnp.where(no_py, 0.0, jnp.where(odd_y, ya_ref[...], yb_ref[...]))
    tail_ref[...] = jnp.zeros_like(tail_ref)
    head_ref[...] = jnp.zeros_like(head_ref)
    res = res_ref[0]
    for t in range(1, res_ref.shape[0]):
        res = res + res_ref[t]
    layers = inject_layers(res, cell_ref[...], cells_x, cells_y)
    for q in range(4):
        layer_ref[q] = layers[q * cells_x : (q + 1) * cells_x]

    def body(depth, static_depth):
        sides = sides_x(xa_ref[depth], xb_ref[depth], odd_x, no_nx, no_px)
        part = depth // (cells_y // HALO) if static_depth is not None else lax.div(depth, cells_y // HALO)
        fields = []
        for field in range(2):
            beside_y = side_columns(ny_ref[field, part], py_ref[field, part], depth)
            cells, total = laplace(now_ref, field, depth, static_depth, deep, sides[field], beside_y)
            fresh = 2.0 * cells - old_ref[field, depth] + courant_ref[depth] * total
            if static_depth == RDEPTH:
                fresh = fresh + layer_ref[2 * field]
            mid_ref[field, depth] = fresh
            put_columns(fresh, depth, tail_ref, head_ref, field)
            fields.append(fresh)
        head, tail = head_rows(*fields), tail_rows(*fields)
        xa_out[depth] = jnp.where(odd_x, head, tail)
        xb_out[depth] = jnp.where(odd_x, tail, head)

    over_depth(deep, body)
    ya_out[...] = jnp.where(odd_y, head_ref[...], tail_ref[...])
    yb_out[...] = jnp.where(odd_y, tail_ref[...], head_ref[...])


def after_kernel(
    flag_ref, mid_ref, now_ref, courant_ref, xa_ref, xb_ref, ya_ref, yb_ref, layer_ref,
    out_ref, ny_ref, py_ref,
):
    odd_x, odd_y = flag_ref[0] == 1, flag_ref[1] == 1
    no_px, no_nx, no_py, no_ny = [flag_ref[i] == 1 for i in range(2, 6)]
    deep, cells_x, cells_y = now_ref.shape[1:]
    ny_ref[...] = jnp.where(no_ny, 0.0, jnp.where(odd_y, yb_ref[...], ya_ref[...]))
    py_ref[...] = jnp.where(no_py, 0.0, jnp.where(odd_y, ya_ref[...], yb_ref[...]))

    def body(depth, static_depth):
        sides = sides_x(xa_ref[depth], xb_ref[depth], odd_x, no_nx, no_px)
        part = depth // (cells_y // HALO) if static_depth is not None else lax.div(depth, cells_y // HALO)
        for field in range(2):
            beside_y = side_columns(ny_ref[field, part], py_ref[field, part], depth)
            cells, total = laplace(mid_ref, field, depth, static_depth, deep, sides[field], beside_y)
            fresh = 2.0 * cells - now_ref[field, depth] + courant_ref[depth] * total
            if static_depth == RDEPTH:
                fresh = fresh + layer_ref[2 * field + 1]
            out_ref[field, depth] = fresh

    over_depth(deep, body)


def paired(groups, count_x, count_y, partner):
    index = lambda g, x, y: (g * count_x + x) * count_y + y
    return [
        (index(g, x, y), index(*partner(g, x, y)))
        for g in range(groups)
        for x in range(count_x)
        for y in range(count_y)
    ]


def on_device(wave_now, wave_before, courant, records, signs, source_x, source_y, receiver_cell):
    _, deep, cells_x, cells_y = wave_now.shape
    groups, tiles_x, tiles_y = [lax.axis_size(axis) for axis in AXES]
    total_recv = receiver_cell.shape[0]
    tiles = total_recv // REC_DEV
    span = (cells_x * tiles_x + cells_y * tiles_y) // 4
    at_x, at_y = lax.axis_index("gx"), lax.axis_index("gy")
    flags = jnp.stack([
        at_x % 2, at_y % 2,
        (at_x == 0).astype(jnp.int32), (at_x == tiles_x - 1).astype(jnp.int32),
        (at_y == 0).astype(jnp.int32), (at_y == tiles_y - 1).astype(jnp.int32),
    ]).astype(jnp.int32)

    perms = functools.partial(paired, groups, tiles_x, tiles_y)
    swap_xa = perms(lambda g, x, y: (g, x ^ 1, y))
    swap_ya = perms(lambda g, x, y: (g, x, y ^ 1))
    swap_xb = perms(
        lambda g, x, y: ((g + groups // 2) % groups, x, y) if x in (0, tiles_x - 1) else (g, ((x + 1) ^ 1) - 1, y)
    )
    swap_yb = perms(lambda g, x, y: (g, x ^ 1, y) if y in (0, tiles_y - 1) else (g, x, ((y + 1) ^ 1) - 1))

    f32 = jnp.float32
    parts = deep * HALO // cells_y
    face_x = jax.ShapeDtypeStruct((deep, cells_x, cells_y), f32)
    face_y = jax.ShapeDtypeStruct((2, parts, cells_x, cells_y), f32)
    face_scratch = pltpu.VMEM(face_y.shape, f32)

    xa, xb, ya, yb = pl.pallas_call(
        pack_kernel,
        out_shape=(face_x, face_x, face_y, face_y),
        in_specs=[SM, VM],
        out_specs=(VM,) * 4,
        scratch_shapes=[face_scratch] * 2,
        name="pack_now",
    )(flags, wave_now)
    send = lambda value, pairs: lax.ppermute(value, AXES, pairs)
    xb_in, ya_in, yb_in, xa_in = send(xb, swap_xb), send(ya, swap_ya), send(yb, swap_yb), send(xa, swap_xa)

    lanes = 128
    cell_rows = receiver_cell.reshape(total_recv // lanes, lanes)
    partial_res = pl.pallas_call(
        functools.partial(residual_kernel, tiles_y, cells_x, cells_y, float(span * span)),
        out_shape=jax.ShapeDtypeStruct((tiles, 4, REC_DEV), f32),
        in_specs=[SM, SM, SM, VM, VM],
        out_specs=VM,
        name="residual",
    )(signs, source_x, source_y, records, cell_rows)
    res_in = lax.all_to_all(partial_res, ("gx", "gy"), 0, 0, tiled=True)
    tile = at_x * tiles_y + at_y
    own_cells = lax.dynamic_slice_in_dim(receiver_cell, tile * REC_DEV, REC_DEV, 0).reshape(1, REC_DEV)

    wave = jax.ShapeDtypeStruct(wave_now.shape, f32)
    wave_middle, layers, xa, xb, ya, yb = pl.pallas_call(
        middle_kernel,
        out_shape=(wave, jax.ShapeDtypeStruct((4, cells_x, cells_y), f32), face_x, face_x, face_y, face_y),
        in_specs=[SM] + [VM] * 9,
        out_specs=(VM,) * 6,
        scratch_shapes=[face_scratch] * 4,
        name="middle",
    )(flags, wave_now, wave_before, courant, xa_in, xb_in, ya_in, yb_in, res_in, own_cells)
    xb_in, ya_in, yb_in, xa_in = send(xb, swap_xb), send(ya, swap_ya), send(yb, swap_yb), send(xa, swap_xa)
    wave_after = pl.pallas_call(
        after_kernel,
        out_shape=wave,
        in_specs=[SM] + [VM] * 8,
        out_specs=VM,
        scratch_shapes=[face_scratch] * 2,
        name="after",
    )(flags, wave_middle, wave_now, courant, xa_in, xb_in, ya_in, yb_in, layers)
    return (wave_after, wave_middle)


def solution(mesh):
    return jax.shard_map(
        on_device,
        mesh=mesh,
        in_specs=(
            P("group", None, "gx", "gy"),
            P("group", None, "gx", "gy"),
            P("group", "gx", "gy"),
            P(("group", "gx", "gy"), None, None),
            P("group", ("gx", "gy")),
            P(("group", "gx", "gy")),
            P(("group", "gx", "gy")),
            P("group"),
        ),
        out_specs=(P("group", None, "gx", "gy"), P("group", None, "gx", "gy")),
        check_vma=False,
    )
```

time: 256 us -> 44.2 us (0.17); the launches traced: 252 us -> 43.8 us
  waiting for transfers between devices: 120 us -> 8.8 us
  local copies, waits for them, and re-layouts: 60.9 us -> 3.4 us
  other arithmetic: 40.5 us -> 0 us
  Pallas kernels: 0 us -> 18.7 us
  between operations: 15 us -> 0.73 us
  starting transfers between devices: 15 us -> 12.2 us
    unnamed x2 -> x0, waiting for transfers between devices: 111 us -> none
    scatter-add x2 -> x0, local copies, waits for them, and re-layouts: 42 us -> none  [the longest x1 21 us: on_device(): wave_middle = wave_middle.at[:, RDEPTH].add(layer[:, 0])]
    add x5 -> x0, other arithmetic: 22.8 us -> none  [the longest x1 9.12 us: on_device(): wave_after = 2.0 * wave_middle - wave_now + courant * laplace(ext_middle, 4)]
    pallas_call x0 -> x4, Pallas kernels: none -> 18.7 us  [the longest x1 6.99 us: on_device(): pl.pallas_call(middle_kernel, out_shape=(wave, jax.ShapeDtypeStruct((4, c...]
    ppermute x8, starting transfers between devices: 15 us -> 6.29 us  [on_device(): send = lambda value, pairs: lax.ppermute(value, AXES, pairs)]
    scatter-add x1 -> x0, other arithmetic: 8.32 us -> none  [on_device(): jnp.zeros((2, 2, cells_x * cells_y), jnp.float32).at[:, :, own_cells]]
    concatenate x6 -> x0, other arithmetic: 7.43 us -> none  [with_halo(): jnp.concatenate([lax.ppermute(tail, axis, [(i, (i + 1) % count) for i in...]
    all_to_all x0 -> x1, starting transfers between devices: none -> 5.9 us  [on_device(): res_in = lax.all_to_all(partial_res, ('gx', 'gy'), 0, 0, tiled=True)]
  transfers between devices with their start and end apart: 9 -> 9, of which waited for: 4 -> 4; matrix products, arithmetic and copies ran while one was open for 10% -> 3% of each run, Pallas kernels for 0% -> 6%
where the time goes in v1:
time: 44.2 us; the launch traced here: 43.8 us
  Pallas kernels  18.7 us (42%)
  starting transfers between devices  12.2 us (28%)
  waiting for transfers between devices  8.8 us (20%)
  local copies, waits for them, and re-layouts  3.4 us (8%)
  between operations  0.73 us (2%)
    pallas_call x1, Pallas kernels, on_device(): pl.pallas_call(middle_kernel, out_shape=(wave, jax.ShapeDtypeStruct((4, c...  6.99 us
    ppermute x8, starting transfers between devices, on_device(): send = lambda value, pairs: lax.ppermute(value, AXES, pairs)  6.29 us
    ppermute x8, waiting for transfers between devices, on_device(): send = lambda value, pairs: lax.ppermute(value, AXES, pairs)  6.04 us
    all_to_all x1, starting transfers between devices, on_device(): res_in = lax.all_to_all(partial_res, ('gx', 'gy'), 0, 0, tiled=True)  5.9 us
    pallas_call x1, Pallas kernels, on_device(): pl.pallas_call(after_kernel, out_shape=wave, in_specs=[SM] + [VM] * 8, ou...  5.82 us
    pallas_call x1, Pallas kernels, on_device(): pl.pallas_call(pack_kernel, out_shape=(face_x, face_x, face_y, face_y), i...  3.35 us
    all_to_all x1, waiting for transfers between devices, on_device(): res_in = lax.all_to_all(partial_res, ('gx', 'gy'), 0, 0, tiled=True)  2.76 us
    pallas_call x1, Pallas kernels, on_device(): pl.pallas_call(functools.partial(residual_kernel, tiles_y, cells_x, cells...  2.52 us
  transfers between devices with their start and end apart: 9, of which 4 were waited for; matrix products, arithmetic and copies ran while one was open for 3% of the time, Pallas kernels for 6%

profile of v1, /device:TPU:0, one launch (start us, length us, event | category | flops | bytes accessed | tf_op | source)
XLA Modules:
  0.0 43.8 jit_solution(5012562152193837604)
XLA Ops:
  0.7 0.6 %stack.43.flag_ref = s32[6]{0:T(128)} concatenate(s32[1]{0:T(128)} %bitcast, s32[1]{0:T(128)} %bitcast.1, s32[1]{0:T(128)} %bitcast.2, s32[1]{0:T(128)} %bitcast.3, s32[1]{0:T(128)} %bitcast.4, s32[1]{0:T(128)} %bitcast.5), dimensions={0} | concatenate | bytes 48 | tf_op jit(solution)/shard_map/stack | solution.py:252
  1.3 3.3 %pack_now.1 = (f32[64,8,128]{2,1,0:T(8,128)}, f32[64,8,128]{2,1,0:T(8,128)}, f32[2,2,8,128]{3,2,1,0:T(8,128)}, f32[2,2,8,128]{3,2,1,0:T(8,128)}) custom-call(s32[6]{0:T(128)} %stack.43.flag_ref, f32[2,64,8,128]{3,2,1,0:T(8,128)} %now_ref.5), custom_call_target="tpu_custom_call" | custom-call | tf_op jit(solution)/shard_map/pack_now/pallas_call | solution.py:272
  4.6 0.5 %collective-permute-start = (f32[64,8,128]{2,1,0:T(8,128)}, f32[64,8,128]{2,1,0:T(8,128)S(1)}, u32[]{:S(2)}, u32[]{:S(2)}) collective-permute-start(f32[64,8,128]{2,1,0:T(8,128)} %get-tuple-element.12), channel_id=1, source_target_pairs={{0,4},{1,5},{2,6},{3,7},{4,0},{5,1},{6,2},{7,3},{8,12},{9,13},{10,... | collective-permute-start | bytes 786440 | tf_op jit(solution)/shard_map/ppermute | solution.py:280
  5.1 2.5 %collective-permute-start.1 = (f32[64,8,128]{2,1,0:T(8,128)}, f32[64,8,128]{2,1,0:T(8,128)S(1)}, u32[]{:S(2)}, u32[]{:S(2)}) collective-permute-start(f32[64,8,128]{2,1,0:T(8,128)} %get-tuple-element.13), channel_id=1, source_target_pairs={{0,16},{1,17},{2,18},{3,19},{4,8},{5,9},{6,10},{7,11},{8,4},{9,5},... | collective-permute-start | bytes 786440 | tf_op jit(solution)/shard_map/ppermute | solution.py:280
  7.6 2.5 %residual.1 = f32[16,4,256]{2,1,0:T(4,128)} custom-call(s32[2,16]{1,0:T(2,128)} %signs_ref.1, s32[16]{0:T(128)} %sx_ref.1, s32[16]{0:T(128)} %sy_ref.1, bf16[16,2,4096]{2,1,0:T(2,128)(2,1)} %records_ref.1, s32[32,128]{1,0:T(8,128)} %bitcast.8), custom_call_target="tpu_custom_call" | custom-call | tf_op jit(solution)/shard_map/residual/pallas_call | solution.py:285
  10.1 0.0 copy-start.10
  10.1 0.0 copy-start.9
  10.1 5.9 %all-to-all-start = ((f32[16,4,256]{2,1,0:T(4,128)}), f32[16,4,256]{2,1,0:T(4,128)S(1)}, u32[]{:S(2)}, u32[]{:S(2)}) async-start(f32[16,4,256]{2,1,0:T(4,128)} %residual.1), calls=%async_computation | async-start | bytes 131072 | tf_op jit(solution)/shard_map/all_to_all | solution.py:292
  16.0 0.0 copy-done.10
  16.0 2.0 %collective-permute-start.2 = (f32[2,2,8,128]{3,2,1,0:T(8,128)S(1)}, f32[2,2,8,128]{3,2,1,0:T(8,128)S(1)}, u32[]{:S(2)}, u32[]{:S(2)}) collective-permute-start(f32[2,2,8,128]{3,2,1,0:T(8,128)S(1)} %copy-done.10), channel_id=1, source_target_pairs={{0,1},{1,0},{2,3},{3,2},{4,5},{5,4},{6,7},{7,6},{8,9},{9,8},{10,11... | collective-permute-start | bytes 49160 | tf_op jit(solution)/shard_map/ppermute | solution.py:280
  18.0 0.0 copy-done.9
  18.0 0.0 collective-permute-start.3
  18.0 1.3 %dynamic_slice.3 = s32[256]{0:T(256)} dynamic-slice(s32[4096]{0:T(1024)} %param.15, s32[]{:T(128)S(6)} %select_n.16), dynamic_slice_sizes={256} | dynamic-slice | bytes 2052 | tf_op jit(solution)/shard_map/dynamic_slice | solution.py:294
  19.3 0.7 %collective-permute-done.2.ya_ref = f32[2,2,8,128]{3,2,1,0:T(8,128)S(1)} collective-permute-done((f32[2,2,8,128]{3,2,1,0:T(8,128)S(1)}, f32[2,2,8,128]{3,2,1,0:T(8,128)S(1)}, u32[]{:S(2)}, u32[]{:S(2)}) %collective-permute-start.2) | collective-permute-done | bytes 16416 | tf_op jit(solution)/shard_map/ppermute | solution.py:280
  20.0 0.0 copy-start.5
  20.0 0.0 collective-permute-done.3.yb_ref
  20.0 0.0 copy-start.6
  20.0 2.8 %all-to-all-done.res_ref = f32[16,4,256]{2,1,0:T(4,128)S(1)} async-done(((f32[16,4,256]{2,1,0:T(4,128)}), f32[16,4,256]{2,1,0:T(4,128)S(1)}, u32[]{:S(2)}, u32[]{:S(2)}) %all-to-all-start) | async-done | bytes 65568 | tf_op jit(solution)/shard_map/all_to_all | solution.py:292
  22.8 0.0 copy-start
  22.8 0.0 collective-permute-done.xa_ref
  22.8 0.0 copy-start.1
  22.8 0.0 collective-permute-done.1.xb_ref
  22.8 0.0 copy-start.2
  22.8 0.0 copy-done.5
  22.8 0.0 copy-done.6
  22.8 0.6 %copy-done = f32[16,4,256]{2,1,0:T(4,128)} copy-done((f32[16,4,256]{2,1,0:T(4,128)}, f32[16,4,256]{2,1,0:T(4,128)S(1)}, u32[]{:S(2)}) %copy-start) | copy-done | bytes 65560
  23.4 0.1 copy-done.1
  23.5 0.1 copy-done.2
  23.6 7.0 %middle.1 = (f32[2,64,8,128]{3,2,1,0:T(8,128)}, f32[4,8,128]{2,1,0:T(8,128)}, f32[64,8,128]{2,1,0:T(8,128)}, f32[64,8,128]{2,1,0:T(8,128)}, f32[2,2,8,128]{3,2,1,0:T(8,128)}, /*index=5*/f32[2,2,8,128]{3,2,1,0:T(8,128)}) custom-call(s32[6]{0:T(128)} %stack.43.flag_ref, f32[2,64,8,128]{3,2,1,0:T(8,128)} %now_ref.5, f32[2,64,8,128]{3,2,1,0:T(8,128)} %old_ref.1, ...), custom_call_target="tpu_custom_call" | custom-call | tf_op jit(solution)/shard_map/middle/pallas_call | solution.py:297
  30.6 0.1 collective-permute-start.4
  30.7 0.8 %collective-permute-start.5 = (f32[64,8,128]{2,1,0:T(8,128)}, f32[64,8,128]{2,1,0:T(8,128)S(1)}, u32[]{:S(2)}, u32[]{:S(2)}) collective-permute-start(f32[64,8,128]{2,1,0:T(8,128)} %get-tuple-element.18), channel_id=1, source_target_pairs={{0,16},{1,17},{2,18},{3,19},{4,8},{5,9},{6,10},{7,11},{8,4},{9,5},... | collective-permute-start | bytes 786440 | tf_op jit(solution)/shard_map/ppermute | solution.py:280
  31.5 0.2 collective-permute-start.6
  31.7 0.3 collective-permute-start.7
  32.0 3.5 %collective-permute-done.6.ya_ref = f32[2,2,8,128]{3,2,1,0:T(8,128)S(1)} collective-permute-done((f32[2,2,8,128]{3,2,1,0:T(8,128)}, f32[2,2,8,128]{3,2,1,0:T(8,128)S(1)}, u32[]{:S(2)}, u32[]{:S(2)}) %collective-permute-start.6) | collective-permute-done | bytes 16416 | tf_op jit(solution)/shard_map/ppermute | solution.py:280
  35.4 0.0 copy-start.7
  35.4 0.0 collective-permute-done.7.yb_ref
  35.4 0.0 copy-start.8
  35.5 0.0 collective-permute-done.4.xa_ref
  35.5 0.0 copy-start.3
  35.5 1.8 %collective-permute-done.5.xb_ref = f32[64,8,128]{2,1,0:T(8,128)S(1)} collective-permute-done((f32[64,8,128]{2,1,0:T(8,128)}, f32[64,8,128]{2,1,0:T(8,128)S(1)}, u32[]{:S(2)}, u32[]{:S(2)}) %collective-permute-start.5) | collective-permute-done | bytes 262176 | tf_op jit(solution)/shard_map/ppermute | solution.py:280
  37.3 0.0 copy-start.4
  37.3 0.0 copy-done.7
  37.3 0.0 copy-done.8
  37.3 0.0 copy-done.3
  37.3 0.7 %copy-done.4 = f32[64,8,128]{2,1,0:T(8,128)} copy-done((f32[64,8,128]{2,1,0:T(8,128)}, f32[64,8,128]{2,1,0:T(8,128)S(1)}, u32[]{:S(2)}) %copy-start.4) | copy-done | bytes 262168
  38.0 5.8 %after.1 = f32[2,64,8,128]{3,2,1,0:T(8,128)} custom-call(s32[6]{0:T(128)} %stack.43.flag_ref, f32[2,64,8,128]{3,2,1,0:T(8,128)} %get-tuple-element.11.mid_ref, f32[2,64,8,128]{3,2,1,0:T(8,128)} %now_ref.5, f32[64,8,128]{2,1,0:T(8,128)} %courant_ref.3, f32[64,8,128]{2,1,0:T(8,128)} %copy-done.3, f32[64,8,128]{2,1,0:T(8,128)} %copy-done.4, ...), custom_call_target="tpu_custom_call" | custom-call | tf_op jit(solution)/shard_map/after/pallas_call | solution.py:306
Async XLA Ops:
  4.6 18.2 %collective-permute-start = (f32[64,8,128]{2,1,0:T(8,128)}, f32[64,8,128]{2,1,0:T(8,128)S(1)}, u32[]{:S(2)}, u32[]{:S(2)}) collective-permute-start(f32[64,8,128]{2,1,0:T(8,128)} %get-tuple-element.12), channel_id=1, source_target_pairs={{0,4},{1,5},{2,6},{3,7},{4,0},{5,1},{6,2},{7,3},{8,12},{9,13},{10,... | collective-permute-start | bytes 786440 | tf_op jit(solution)/shard_map/ppermute | solution.py:280
  5.1 17.7 %collective-permute-start.1 = (f32[64,8,128]{2,1,0:T(8,128)}, f32[64,8,128]{2,1,0:T(8,128)S(1)}, u32[]{:S(2)}, u32[]{:S(2)}) collective-permute-start(f32[64,8,128]{2,1,0:T(8,128)} %get-tuple-element.13), channel_id=1, source_target_pairs={{0,16},{1,17},{2,18},{3,19},{4,8},{5,9},{6,10},{7,11},{8,4},{9,5},... | collective-permute-start | bytes 786440 | tf_op jit(solution)/shard_map/ppermute | solution.py:280
  10.1 5.9 %copy-start.10 = (f32[2,2,8,128]{3,2,1,0:T(8,128)S(1)}, f32[2,2,8,128]{3,2,1,0:T(8,128)}, u32[]{:S(2)}) copy-start(f32[2,2,8,128]{3,2,1,0:T(8,128)} %get-tuple-element.14) | copy-start | bytes 49156
  10.1 7.9 %copy-start.9 = (f32[2,2,8,128]{3,2,1,0:T(8,128)S(1)}, f32[2,2,8,128]{3,2,1,0:T(8,128)}, u32[]{:S(2)}) copy-start(f32[2,2,8,128]{3,2,1,0:T(8,128)} %get-tuple-element.15) | copy-start | bytes 49156
  10.1 12.7 %all-to-all-start = ((f32[16,4,256]{2,1,0:T(4,128)}), f32[16,4,256]{2,1,0:T(4,128)S(1)}, u32[]{:S(2)}, u32[]{:S(2)}) async-start(f32[16,4,256]{2,1,0:T(4,128)} %residual.1), calls=%async_computation | async-start | bytes 131072 | tf_op jit(solution)/shard_map/all_to_all | solution.py:292
  16.0 4.0 %collective-permute-start.2 = (f32[2,2,8,128]{3,2,1,0:T(8,128)S(1)}, f32[2,2,8,128]{3,2,1,0:T(8,128)S(1)}, u32[]{:S(2)}, u32[]{:S(2)}) collective-permute-start(f32[2,2,8,128]{3,2,1,0:T(8,128)S(1)} %copy-done.10), channel_id=1, source_target_pairs={{0,1},{1,0},{2,3},{3,2},{4,5},{5,4},{6,7},{7,6},{8,9},{9,8},{10,11... | collective-permute-start | bytes 49160 | tf_op jit(solution)/shard_map/ppermute | solution.py:280
  18.0 2.0 %collective-permute-start.3 = (f32[2,2,8,128]{3,2,1,0:T(8,128)S(1)}, f32[2,2,8,128]{3,2,1,0:T(8,128)S(1)}, u32[]{:S(2)}, u32[]{:S(2)}) collective-permute-start(f32[2,2,8,128]{3,2,1,0:T(8,128)S(1)} %copy-done.9), channel_id=1, source_target_pairs={{0,4},{1,2},{2,1},{3,7},{4,0},{5,6},{6,5},{7,3},{8,12},{9,10},{10,... | collective-permute-start | bytes 49160 | tf_op jit(solution)/shard_map/ppermute | solution.py:280
  20.0 2.8 %copy-start.5 = (f32[2,2,8,128]{3,2,1,0:T(8,128)}, f32[2,2,8,128]{3,2,1,0:T(8,128)S(1)}, u32[]{:S(2)}) copy-start(f32[2,2,8,128]{3,2,1,0:T(8,128)S(1)} %collective-permute-done.2.ya_ref) | copy-start | bytes 49156
  20.0 2.8 %copy-start.6 = (f32[2,2,8,128]{3,2,1,0:T(8,128)}, f32[2,2,8,128]{3,2,1,0:T(8,128)S(1)}, u32[]{:S(2)}) copy-start(f32[2,2,8,128]{3,2,1,0:T(8,128)S(1)} %collective-permute-done.3.yb_ref) | copy-start | bytes 49156
  22.8 0.6 %copy-start = (f32[16,4,256]{2,1,0:T(4,128)}, f32[16,4,256]{2,1,0:T(4,128)S(1)}, u32[]{:S(2)}) copy-start(f32[16,4,256]{2,1,0:T(4,128)S(1)} %all-to-all-done.res_ref) | copy-start | bytes 196612
  22.8 0.7 %copy-start.1 = (f32[64,8,128]{2,1,0:T(8,128)}, f32[64,8,128]{2,1,0:T(8,128)S(1)}, u32[]{:S(2)}) copy-start(f32[64,8,128]{2,1,0:T(8,128)S(1)} %collective-permute-done.xa_ref) | copy-start | bytes 786436
  22.8 0.8 %copy-start.2 = (f32[64,8,128]{2,1,0:T(8,128)}, f32[64,8,128]{2,1,0:T(8,128)S(1)}, u32[]{:S(2)}) copy-start(f32[64,8,128]{2,1,0:T(8,128)S(1)} %collective-permute-done.1.xb_ref) | copy-start | bytes 786436
  30.6 4.9 %collective-permute-start.4 = (f32[64,8,128]{2,1,0:T(8,128)}, f32[64,8,128]{2,1,0:T(8,128)S(1)}, u32[]{:S(2)}, u32[]{:S(2)}) collective-permute-start(f32[64,8,128]{2,1,0:T(8,128)} %get-tuple-element.17), channel_id=1, source_target_pairs={{0,4},{1,5},{2,6},{3,7},{4,0},{5,1},{6,2},{7,3},{8,12},{9,13},{10,... | collective-permute-start | bytes 786440 | tf_op jit(solution)/shard_map/ppermute | solution.py:280
  30.7 6.6 %collective-permute-start.5 = (f32[64,8,128]{2,1,0:T(8,128)}, f32[64,8,128]{2,1,0:T(8,128)S(1)}, u32[]{:S(2)}, u32[]{:S(2)}) collective-permute-start(f32[64,8,128]{2,1,0:T(8,128)} %get-tuple-element.18), channel_id=1, source_target_pairs={{0,16},{1,17},{2,18},{3,19},{4,8},{5,9},{6,10},{7,11},{8,4},{9,5},... | collective-permute-start | bytes 786440 | tf_op jit(solution)/shard_map/ppermute | solution.py:280
  31.5 3.9 %collective-permute-start.6 = (f32[2,2,8,128]{3,2,1,0:T(8,128)}, f32[2,2,8,128]{3,2,1,0:T(8,128)S(1)}, u32[]{:S(2)}, u32[]{:S(2)}) collective-permute-start(f32[2,2,8,128]{3,2,1,0:T(8,128)} %get-tuple-element.19), channel_id=1, source_target_pairs={{0,1},{1,0},{2,3},{3,2},{4,5},{5,4},{6,7},{7,6},{8,9},{9,8},{10,11... | collective-permute-start | bytes 49160 | tf_op jit(solution)/shard_map/ppermute | solution.py:280
  31.7 3.8 %collective-permute-start.7 = (f32[2,2,8,128]{3,2,1,0:T(8,128)}, f32[2,2,8,128]{3,2,1,0:T(8,128)S(1)}, u32[]{:S(2)}, u32[]{:S(2)}) collective-permute-start(f32[2,2,8,128]{3,2,1,0:T(8,128)} %get-tuple-element.20), channel_id=1, source_target_pairs={{0,4},{1,2},{2,1},{3,7},{4,0},{5,6},{6,5},{7,3},{8,12},{9,10},{10,... | collective-permute-start | bytes 49160 | tf_op jit(solution)/shard_map/ppermute | solution.py:280
  35.4 1.8 %copy-start.7 = (f32[2,2,8,128]{3,2,1,0:T(8,128)}, f32[2,2,8,128]{3,2,1,0:T(8,128)S(1)}, u32[]{:S(2)}) copy-start(f32[2,2,8,128]{3,2,1,0:T(8,128)S(1)} %collective-permute-done.6.ya_ref) | copy-start | bytes 49156
  35.4 1.8 %copy-start.8 = (f32[2,2,8,128]{3,2,1,0:T(8,128)}, f32[2,2,8,128]{3,2,1,0:T(8,128)S(1)}, u32[]{:S(2)}) copy-start(f32[2,2,8,128]{3,2,1,0:T(8,128)S(1)} %collective-permute-done.7.yb_ref) | copy-start | bytes 49156
  35.5 1.8 %copy-start.3 = (f32[64,8,128]{2,1,0:T(8,128)}, f32[64,8,128]{2,1,0:T(8,128)S(1)}, u32[]{:S(2)}) copy-start(f32[64,8,128]{2,1,0:T(8,128)S(1)} %collective-permute-done.4.xa_ref) | copy-start | bytes 786436
  37.3 0.7 %copy-start.4 = (f32[64,8,128]{2,1,0:T(8,128)}, f32[64,8,128]{2,1,0:T(8,128)S(1)}, u32[]{:S(2)}) copy-start(f32[64,8,128]{2,1,0:T(8,128)S(1)} %collective-permute-done.5.xb_ref) | copy-start | bytes 786436

commit v2 on v0

v2 whole, which is shorter than its diff:
```python
import functools

import jax
import jax.numpy as jnp
import ml_dtypes
import numpy as np
from jax import lax
from jax.experimental import pallas as pl
from jax.experimental.pallas import tpu as pltpu
from jax.sharding import PartitionSpec as P

REC_DEV = 256
RDEPTH = 2
HALO = 4
LANES = 128
SUB = 8
GROUP = 16
AXES = ("group", "gx", "gy")
F32, BF16 = jnp.float32, jnp.bfloat16

coef_zero = -205.0 / 72.0
coef_rest = (8.0 / 5.0, -1.0 / 5.0, 8.0 / 315.0, -1.0 / 560.0)
coef_high = [float(np.float32(c).astype(ml_dtypes.bfloat16)) for c in coef_rest]
coef_low = [float(np.float32(c - h).astype(ml_dtypes.bfloat16)) for c, h in zip(coef_rest, coef_high)]

VM = pl.BlockSpec(memory_space=pltpu.VMEM)
SM = pl.BlockSpec(memory_space=pltpu.SMEM)
PARAMS = pltpu.CompilerParams(vmem_limit_bytes=16 * 1024 * 1024)


def near_memory(value):
    return pltpu.with_memory_space_constraint(value, pltpu.VMEM)


def rows_of(shape):
    return lax.broadcasted_iota(jnp.int32, shape, len(shape) - 2)


def lanes_of(shape):
    return lax.broadcasted_iota(jnp.int32, shape, len(shape) - 1)


def dot(left, right):
    return jnp.dot(left, right, preferred_element_type=F32)


def split(value):
    first = value.astype(BF16)
    rest = value - first.astype(F32)
    second = rest.astype(BF16)
    return first, second, (rest - second.astype(F32)).astype(BF16)


def pick(step, coefs):
    out = jnp.zeros(step.shape, F32)
    for m in range(1, HALO + 1):
        out = jnp.where(step == m, coefs[m - 1], out)
    return out.astype(BF16)


def band(coefs):
    shape = (LANES, LANES)
    return pick(jnp.abs(rows_of(shape) - lanes_of(shape)), coefs)


def side(coefs):
    shape = (LANES, LANES)
    c = rows_of(shape) & 7
    j = lanes_of(shape)
    return pick(jnp.where(c < HALO, LANES + c - j, j + 8 - c), coefs)


def chooser():
    shape = (LANES, LANES)
    c = lanes_of(shape) & 7
    return (rows_of(shape) == jnp.where(c < HALO, c, LANES - 8 + c)).astype(F32).astype(BF16)


def pack_columns(ref, out_ref):
    choose = chooser()
    choose_both = jnp.concatenate([choose, choose], axis=0)
    groups = ref.shape[1] // GROUP

    def step(i, carry):
        field, group = lax.div(i, groups), lax.rem(i, groups)
        cells = ref[field, pl.ds(group * GROUP, GROUP)].reshape(GROUP * SUB, LANES)
        first, second, third = split(cells)
        wide = dot(jnp.concatenate([first, second], axis=1), choose_both) + dot(third, choose)
        lane_group = lanes_of((SUB, LANES)) >> 3
        tile = wide[:SUB]
        for q in range(1, GROUP):
            tile = jnp.where(lane_group == q, wide[q * SUB : (q + 1) * SUB], tile)
        out_ref[field, group] = tile
        return carry

    lax.fori_loop(0, 2 * groups, step, 0, unroll=2)


def sides_y(ya, yb, odd, no_next, no_prev):
    after = jnp.where(no_next, 0.0, jnp.where(odd, yb, ya))
    before = jnp.where(no_prev, 0.0, jnp.where(odd, ya, yb))
    return jnp.where((lanes_of(ya.shape) & 7) < HALO, after, before)


def along_y(ref, ya_ref, yb_ref, place, out_ref):
    high, low, side_high, side_low = band(coef_high), band(coef_low), side(coef_high), side(coef_low)
    high, side_high = [jnp.concatenate([m, m], axis=0) for m in (high, side_high)]
    low = jnp.concatenate([low, side_low], axis=0)
    groups = ref.shape[1] // GROUP
    _, odd, _, _, no_next, no_prev = place

    def step(i, carry):
        field, group = lax.div(i, groups), lax.rem(i, groups)
        cells = ref[field, pl.ds(group * GROUP, GROUP)].reshape(GROUP * SUB, LANES)
        first, second, _ = split(cells)
        beside = sides_y(ya_ref[field, group], yb_ref[field, group], odd, no_next, no_prev)
        lane_group = lanes_of((SUB, LANES)) >> 3
        beside = jnp.concatenate([jnp.where(lane_group == q, beside, 0.0) for q in range(GROUP)], axis=0)
        beside_first, beside_second, _ = split(beside)
        total = dot(jnp.concatenate([first, second], axis=1), high)
        total = total + dot(jnp.concatenate([beside_first, beside_second], axis=1), side_high)
        total = total + dot(jnp.concatenate([first, beside_first], axis=1), low)
        out_ref[field, pl.ds(group * GROUP, GROUP)] = total.reshape(GROUP, SUB, LANES)
        return carry

    lax.fori_loop(0, 2 * groups, step, 0, unroll=2)


def where_am_i(counts):
    at_x, at_y = lax.axis_index("gx"), lax.axis_index("gy")
    return (
        lax.rem(at_x, 2) == 1, lax.rem(at_y, 2) == 1,
        at_x == counts[0] - 1, at_x == 0, at_y == counts[1] - 1, at_y == 0,
    )


def head_rows(first, second):
    return jnp.where(rows_of(first.shape) < HALO, first, pltpu.roll(second, HALO, 0))


def tail_rows(first, second):
    return jnp.where(rows_of(first.shape) < HALO, pltpu.roll(first, HALO, 0), second)


def sides_x(xa, xb, place):
    odd, _, no_next, no_prev, _, _ = place
    after = jnp.where(no_next, 0.0, jnp.where(odd, xb, xa))
    before = jnp.where(no_prev, 0.0, jnp.where(odd, xa, xb))
    low = rows_of(after.shape) < HALO
    return jnp.where(low, after, pltpu.roll(before, HALO, 0)), jnp.where(low, pltpu.roll(after, HALO, 0), before)


def shifted_pair(cells, beside, step):
    row = rows_of(cells.shape)
    up = pltpu.roll(jnp.where(row < step, beside, cells), SUB - step, 0)
    down = pltpu.roll(jnp.where(row >= SUB - step, beside, cells), step, 0)
    return up + down


def laplace(ref, field, depth, static_depth, beside_x, part_y):
    deep = ref.shape[1]
    cells = ref[field, depth]
    total = 3.0 * coef_zero * cells + part_y
    for step in range(1, HALO + 1):
        near = shifted_pair(cells, beside_x, step)
        if static_depth is None or static_depth + step < deep:
            near = near + ref[field, depth + step]
        if static_depth is None or static_depth >= step:
            near = near + ref[field, depth - step]
        total = total + coef_rest[step - 1] * near
    return cells, total


def over_depth(deep, body, after_part=None):
    parts = 4
    size = deep // parts
    for part in range(parts):
        start, stop = part * size, (part + 1) * size
        if part == 0:
            for depth in range(HALO):
                body(depth, depth)
            start = HALO
        if part == parts - 1:
            stop = deep - HALO

        def inner(depth, carry):
            body(depth, None)
            return carry

        lax.fori_loop(start, stop, inner, 0, unroll=4)
        if part == parts - 1:
            for depth in range(deep - HALO, deep):
                body(depth, depth)
        if after_part is not None:
            after_part(part, part * size, size)


def pack_xb_kernel(counts, now_ref, xb_ref):
    odd = where_am_i(counts)[0]

    def body(depth, carry):
        first, second = now_ref[0, depth], now_ref[1, depth]
        xb_ref[depth] = jnp.where(odd, tail_rows(first, second), head_rows(first, second))
        return carry

    lax.fori_loop(0, now_ref.shape[1], body, 0, unroll=8)


def pack_rest_kernel(counts, now_ref, xa_ref, y_ref):
    odd = where_am_i(counts)[0]
    pack_columns(now_ref, y_ref)

    def body(depth, carry):
        first, second = now_ref[0, depth], now_ref[1, depth]
        xa_ref[depth] = jnp.where(odd, head_rows(first, second), tail_rows(first, second))
        return carry

    lax.fori_loop(0, now_ref.shape[1], body, 0, unroll=8)


def residual_kernel(tiles_y, cells_x, cells_y, radius_sq, signs_ref, sx_ref, sy_ref, records_ref, cell_ref, out_ref):
    shots, rows, _ = records_ref.shape
    chunk = min(rows, 64)
    per = 2 * REC_DEV // LANES
    twice = (rows_of((chunk, chunk // 2)) >> 1 == lanes_of((chunk, chunk // 2))).astype(F32).astype(BF16)

    def chunk_step(c, carry):
        cell = cell_ref[pl.ds(pl.multiple_of(c * (chunk // 2), chunk // 2), chunk // 2), :]
        row, column = lax.shift_right_logical(cell, cells_y.bit_length() - 1), cell & (cells_y - 1)
        row, column = [dot(twice, v.astype(F32).astype(BF16)) for v in (row, column)]
        tile = c * (chunk // per) + rows_of((chunk, LANES)) // per
        tile_x, tile_y = tile // tiles_y, tile % tiles_y
        pos_x = (tile_x * cells_x).astype(F32) + row
        pos_y = (tile_y * cells_y).astype(F32) + column
        sums = [jnp.zeros((chunk, LANES), F32) for _ in range(2)]
        start = pl.multiple_of(c * chunk, chunk)
        for shot in range(shots):
            dx = pos_x - sx_ref[shot].astype(F32)
            dy = pos_y - sy_ref[shot].astype(F32)
            dist = dx * dx + dy * dy
            taped = records_ref[shot, pl.ds(start, chunk), :].astype(F32) * (dist / (dist + radius_sq))
            for code in range(2):
                sums[code] = sums[code] + signs_ref[code, shot].astype(F32) * taped
        for t in range(chunk // per):
            both = [s[t * per : (t + 1) * per] for s in sums]
            out_ref[c * (chunk // per) + t] = jnp.concatenate(both, axis=0)
        return carry

    lax.fori_loop(0, rows // chunk, chunk_step, 0)


def inject_layers(res, cells, cells_x, cells_y):
    out = None
    for half in range(REC_DEV // LANES):
        row = lax.shift_right_logical(cells[half], cells_y.bit_length() - 1)
        column = cells[half] & (cells_y - 1)
        in_row = rows_of((cells_x, LANES)) == row
        spread = jnp.concatenate(
            [
                jnp.where(in_row, res[code * 4 + half * 2 + sample][None, :], 0.0)
                for code in range(2)
                for sample in range(2)
            ],
            axis=0,
        )
        hot = (rows_of((cells_y, LANES)) == column).astype(F32).astype(BF16)
        parts = jnp.concatenate(split(spread), axis=0)
        got = lax.dot_general(parts, hot, (((1,), (1,)), ((), ())), preferred_element_type=F32)
        out = got if out is None else out + got
    count = 4 * cells_x
    return out[:count] + out[count : 2 * count] + out[2 * count :]


def middle_kernel(
    counts, now_ref, old_ref, courant_ref, xa_ref, xb_ref, ya_ref, yb_ref, res_ref, cell_ref,
    mid_ref, layer_ref, xa_out, xb_out, y_out, part_y_ref,
):
    place = where_am_i(counts)
    deep, cells_x, cells_y = now_ref.shape[1:]
    along_y(now_ref, ya_ref, yb_ref, place, part_y_ref)
    res = res_ref[0]
    for t in range(1, res_ref.shape[0]):
        res = res + res_ref[t]
    halves = REC_DEV // LANES
    first_row = (lax.axis_index("gx") * counts[1] + lax.axis_index("gy")) * halves
    cells = [cell_ref[pl.ds(first_row + half, 1), :] for half in range(halves)]
    layers = inject_layers(res, cells, cells_x, cells_y)
    for q in range(4):
        layer_ref[q] = layers[q * cells_x : (q + 1) * cells_x]

    def body(depth, static_depth):
        sides = sides_x(xa_ref[depth], xb_ref[depth], place)
        fields = []
        for field in range(2):
            cells, total = laplace(now_ref, field, depth, static_depth, sides[field], part_y_ref[field, depth])
            fresh = 2.0 * cells - old_ref[field, depth] + courant_ref[depth] * total
            if static_depth == RDEPTH:
                fresh = fresh + layer_ref[2 * field]
            mid_ref[field, depth] = fresh
            fields.append(fresh)
        head, tail = head_rows(*fields), tail_rows(*fields)
        xa_out[depth] = jnp.where(place[0], head, tail)
        xb_out[depth] = jnp.where(place[0], tail, head)

    over_depth(deep, body)
    pack_columns(mid_ref, y_out)


def after_kernel(
    counts, mid_ref, now_ref, courant_ref, xa_ref, xb_ref, ya_ref, yb_ref, layer_ref,
    out_ref, part_y_ref, held_ref, sems,
):
    place = where_am_i(counts)
    deep = now_ref.shape[1]
    along_y(mid_ref, ya_ref, yb_ref, place, part_y_ref)

    def body(depth, static_depth):
        sides = sides_x(xa_ref[depth], xb_ref[depth], place)
        for field in range(2):
            cells, total = laplace(mid_ref, field, depth, static_depth, sides[field], part_y_ref[field, depth])
            fresh = 2.0 * cells - now_ref[field, depth] + courant_ref[depth] * total
            if static_depth == RDEPTH:
                fresh = fresh + layer_ref[2 * field + 1]
            held_ref[field, depth] = fresh

    copies = []

    def send_out(part, start, size):
        copy = pltpu.make_async_copy(
            held_ref.at[:, pl.ds(start, size)], out_ref.at[:, pl.ds(start, size)], sems.at[part]
        )
        copy.start()
        copies.append(copy)

    over_depth(deep, body, send_out)
    for copy in copies:
        copy.wait()


def paired(groups, count_x, count_y, partner):
    index = lambda g, x, y: (g * count_x + x) * count_y + y
    return [
        (index(g, x, y), index(*partner(g, x, y)))
        for g in range(groups)
        for x in range(count_x)
        for y in range(count_y)
    ]


def on_device(wave_now, wave_before, courant, records, signs, source_x, source_y, receiver_cell):
    _, deep, cells_x, cells_y = wave_now.shape
    groups, tiles_x, tiles_y = [lax.axis_size(axis) for axis in AXES]
    counts = (tiles_x, tiles_y)
    total_recv = receiver_cell.shape[0]
    tiles = total_recv // REC_DEV
    shots = records.shape[0]
    span = (cells_x * tiles_x + cells_y * tiles_y) // 4

    perms = functools.partial(paired, groups, tiles_x, tiles_y)
    swap_xa = perms(lambda g, x, y: (g, x ^ 1, y))
    swap_ya = perms(lambda g, x, y: (g, x, y ^ 1))
    swap_xb = perms(
        lambda g, x, y: ((g + groups // 2) % groups, x, y) if x in (0, tiles_x - 1) else (g, ((x + 1) ^ 1) - 1, y)
    )
    swap_yb = perms(lambda g, x, y: (g, x ^ 1, y) if y in (0, tiles_y - 1) else (g, x, ((y + 1) ^ 1) - 1))
    send = lambda value, pairs: lax.ppermute(value, AXES, pairs)

    face_x = pltpu.VMEM((deep, cells_x, cells_y), F32)
    face_y = pltpu.VMEM((2, deep // GROUP, cells_x, cells_y), F32)
    wave = wave_now.shape

    def kernel(body, outs, n_scalar, n_array, scratch=(), out_specs=None):
        name = body.__name__.removesuffix("_kernel")

        def call(*args):
            args = args[:n_scalar] + tuple(near_memory(a) for a in args[n_scalar:])
            return pl.pallas_call(
                functools.partial(body, counts),
                out_shape=outs,
                in_specs=[SM] * n_scalar + [VM] * n_array,
                out_specs=out_specs if out_specs is not None else jax.tree.map(lambda _: VM, outs),
                scratch_shapes=scratch,
                compiler_params=PARAMS,
                name=name,
            )(*args)

        return call

    xb = kernel(pack_xb_kernel, face_x, 0, 1)(wave_now)
    xb_in = send(xb, swap_xb)
    xa, y_face = kernel(pack_rest_kernel, (face_x, face_y), 0, 1)(wave_now)
    ya_in, yb_in, xa_in = send(y_face, swap_ya), send(y_face, swap_yb), send(xa, swap_xa)

    cell_rows = receiver_cell.reshape(total_recv // LANES, LANES)
    record_rows = records.reshape(shots, 2, total_recv // LANES, LANES).transpose(0, 2, 1, 3)
    record_rows = record_rows.reshape(shots, 2 * total_recv // LANES, LANES)
    partial_res = pl.pallas_call(
        functools.partial(residual_kernel, tiles_y, cells_x, cells_y, float(span * span)),
        out_shape=pltpu.VMEM((tiles, SUB, LANES), F32),
        in_specs=[SM, SM, SM, VM, VM],
        out_specs=VM,
        compiler_params=PARAMS,
        name="residual",
    )(signs, source_x, source_y, near_memory(record_rows), near_memory(cell_rows))
    res_in = lax.all_to_all(partial_res, ("gx", "gy"), 0, 0, tiled=True)

    part_y = pltpu.VMEM(wave, F32)
    wave_middle, layers, xa, xb, y_face = kernel(
        middle_kernel,
        (pltpu.VMEM(wave, F32), pltpu.VMEM((4, cells_x, cells_y), F32), face_x, face_x, face_y),
        0, 9, [part_y],
    )(wave_now, wave_before, courant, xa_in, xb_in, ya_in, yb_in, res_in, cell_rows)
    xb_in, ya_in, yb_in, xa_in = send(xb, swap_xb), send(y_face, swap_ya), send(y_face, swap_yb), send(xa, swap_xa)
    wave_after = kernel(
        after_kernel, jax.ShapeDtypeStruct(wave, F32), 0, 8,
        [part_y, part_y, pltpu.SemaphoreType.DMA((4,))],
        out_specs=pl.BlockSpec(memory_space=pl.ANY),
    )(wave_middle, wave_now, courant, xa_in, xb_in, ya_in, yb_in, layers)
    return (wave_after, wave_middle)


def solution(mesh):
    return jax.shard_map(
        on_device,
        mesh=mesh,
        in_specs=(
            P("group", None, "gx", "gy"),
            P("group", None, "gx", "gy"),
            P("group", "gx", "gy"),
            P(("group", "gx", "gy"), None, None),
            P("group", ("gx", "gy")),
            P(("group", "gx", "gy")),
            P(("group", "gx", "gy")),
            P("group"),
        ),
        out_specs=(P("group", None, "gx", "gy"), P("group", None, "gx", "gy")),
        check_vma=False,
    )
```

time: 256 us -> 32.3 us (0.13); the launches traced: 252 us -> 32 us
  waiting for transfers between devices: 120 us -> 6.68 us
  local copies, waits for them, and re-layouts: 60.9 us -> 1.87 us
  other arithmetic: 40.5 us -> 0 us
  between operations: 15 us -> 0.75 us
  Pallas kernels: 0 us -> 8.27 us
    unnamed x2 -> x0, waiting for transfers between devices: 111 us -> none
    scatter-add x2 -> x0, local copies, waits for them, and re-layouts: 42 us -> none  [the longest x1 21 us: on_device(): wave_middle = wave_middle.at[:, RDEPTH].add(layer[:, 0])]
    add x5 -> x0, other arithmetic: 22.8 us -> none  [the longest x1 9.12 us: on_device(): wave_after = 2.0 * wave_middle - wave_now + courant * laplace(ext_middle, 4)]
    scatter-add x1 -> x0, other arithmetic: 8.32 us -> none  [on_device(): jnp.zeros((2, 2, cells_x * cells_y), jnp.float32).at[:, :, own_cells]]
    pallas_call x0 -> x5, Pallas kernels: none -> 8.27 us  [the longest x4 6.71 us: call(): pl.pallas_call(functools.partial(body, counts), out_shape=outs, in_specs=...]
    concatenate x6 -> x0, other arithmetic: 7.43 us -> none  [with_halo(): jnp.concatenate([lax.ppermute(tail, axis, [(i, (i + 1) % count) for i in...]
    ppermute x8, starting transfers between devices: 15 us -> 9.12 us  [on_device(): send = lambda value, pairs: lax.ppermute(value, AXES, pairs)]
    all_to_all x0 -> x1, starting transfers between devices: none -> 5.35 us  [on_device(): res_in = lax.all_to_all(partial_res, ('gx', 'gy'), 0, 0, tiled=True)]
  transfers between devices with their start and end apart: 9 -> 9, of which waited for: 4 -> 4; matrix products, arithmetic and copies ran while one was open for 10% -> 2% of each run, Pallas kernels for 0% -> 8%
where the time goes in v2:
time: 32.3 us; the launch traced here: 32 us
  starting transfers between devices  14.5 us (45%)
  Pallas kernels  8.27 us (26%)
  waiting for transfers between devices  6.68 us (21%)
  local copies, waits for them, and re-layouts  1.87 us (6%)
  between operations  0.75 us (2%)
    ppermute x8, starting transfers between devices, on_device(): send = lambda value, pairs: lax.ppermute(value, AXES, pairs)  9.12 us
    pallas_call x4, Pallas kernels, call(): pl.pallas_call(functools.partial(body, counts), out_shape=outs, in_specs=...  6.71 us
    ppermute x8, waiting for transfers between devices, on_device(): send = lambda value, pairs: lax.ppermute(value, AXES, pairs)  5.36 us
    all_to_all x1, starting transfers between devices, on_device(): res_in = lax.all_to_all(partial_res, ('gx', 'gy'), 0, 0, tiled=True)  5.35 us
    unnamed x19, local copies, waits for them, and re-layouts  1.87 us
    pallas_call x1, Pallas kernels, on_device(): pl.pallas_call(functools.partial(residual_kernel, tiles_y, cells_x, cells...  1.57 us
    all_to_all x1, waiting for transfers between devices, on_device(): res_in = lax.all_to_all(partial_res, ('gx', 'gy'), 0, 0, tiled=True)  1.33 us
  transfers between devices with their start and end apart: 9, of which 4 were waited for; matrix products, arithmetic and copies ran while one was open for 2% of the time, Pallas kernels for 8%

profile of v2, /device:TPU:0, one launch (start us, length us, event | category | flops | bytes accessed | tf_op | source)
XLA Modules:
  0.0 32.0 jit_solution(14085503189209979495)
XLA Ops:
  0.6 0.0 copy-start
  0.6 1.0 %copy-done = f32[2,64,8,128]{3,2,1,0:T(8,128)S(1)} copy-done((f32[2,64,8,128]{3,2,1,0:T(8,128)S(1)}, f32[2,64,8,128]{3,2,1,0:T(8,128)}, u32[]{:S(2)}) %copy-start) | copy-done | bytes 524312
  1.7 0.0 copy-start.4
  1.7 0.0 copy-start.5
  1.7 0.0 copy-start.6
  1.7 0.0 copy-start.7
  1.7 0.0 copy-start.8
  1.7 0.0 copy-start.3
  1.7 0.1 pack_xb.1
  1.8 0.0 copy-start.1
  1.8 3.0 %collective-permute-start.1 = (f32[64,8,128]{2,1,0:T(8,128)S(1)}, f32[64,8,128]{2,1,0:T(8,128)S(1)}, u32[]{:S(2)}, u32[]{:S(2)}) collective-permute-start(f32[64,8,128]{2,1,0:T(8,128)S(1)} %pack_xb.1), channel_id=1, source_target_pairs={{0,16},{1,17},{2,18},{3,19},{4,8},{5,9},{6,10},{7,11},{8,4},{9,5},... | collective-permute-start | bytes 786440 | tf_op jit(solution)/shard_map/ppermute | solution.py:366
  4.8 0.9 %pack_rest.1 = (f32[64,8,128]{2,1,0:T(8,128)S(1)}, f32[2,4,8,128]{3,2,1,0:T(8,128)S(1)}) custom-call(f32[2,64,8,128]{3,2,1,0:T(8,128)S(1)} %copy-done), custom_call_target="tpu_custom_call" | custom-call | tf_op jit(solution)/shard_map/pack_rest/pallas_call | solution.py:377
  5.7 0.0 copy-start.2
  5.7 0.2 collective-permute-start
  5.9 0.0 copy-done.4
  5.9 0.0 copy-done.5
  5.9 0.0 copy-done.6
  5.9 0.0 copy-done.7
  5.9 0.0 copy-done.8
  6.0 1.6 %residual.1 = f32[16,8,128]{2,1,0:T(8,128)} custom-call(s32[2,16]{1,0:T(2,128)S(1)} %copy-done.6, s32[16]{0:T(128)S(1)} %copy-done.7, s32[16]{0:T(128)S(1)} %copy-done.8, bf16[16,64,128]{2,1,0:T(8,128)(2,1)S(1)} %bitcast.6, s32[32,128]{1,0:T(8,128)S(1)} %bitcast.7), custom_call_target="tpu_custom_call" | custom-call | tf_op jit(solution)/shard_map/residual/pallas_call | solution.py:397
  7.5 5.3 %all-to-all-start = ((f32[16,8,128]{2,1,0:T(8,128)}), f32[16,8,128]{2,1,0:T(8,128)S(1)}, u32[]{:S(2)}, u32[]{:S(2)}) async-start(f32[16,8,128]{2,1,0:T(8,128)} %residual.1), calls=%async_computation | async-start | bytes 131072 | tf_op jit(solution)/shard_map/all_to_all | solution.py:405
  12.9 0.4 %collective-permute-start.3 = (f32[2,4,8,128]{3,2,1,0:T(8,128)S(1)}, f32[2,4,8,128]{3,2,1,0:T(8,128)S(1)}, u32[]{:S(2)}, u32[]{:S(2)}) collective-permute-start(f32[2,4,8,128]{3,2,1,0:T(8,128)S(1)} %get-tuple-element.10), channel_id=1, source_target_pairs={{0,4},{1,2},{2,1},{3,7},{4,0},{5,6},{6,5},{7,3},{8,12},{9,10},{10,... | collective-permute-start | bytes 98312 | tf_op jit(solution)/shard_map/ppermute | solution.py:366
  13.3 3.0 %collective-permute-start.2 = (f32[2,4,8,128]{3,2,1,0:T(8,128)S(1)}, f32[2,4,8,128]{3,2,1,0:T(8,128)S(1)}, u32[]{:S(2)}, u32[]{:S(2)}) collective-permute-start(f32[2,4,8,128]{3,2,1,0:T(8,128)S(1)} %get-tuple-element.10), channel_id=1, source_target_pairs={{0,1},{1,0},{2,3},{3,2},{4,5},{5,4},{6,7},{7,6},{8,9},{9,8},{10,11... | collective-permute-start | bytes 98312 | tf_op jit(solution)/shard_map/ppermute | solution.py:366
  16.3 0.0 collective-permute-done.3.yb_ref
  16.3 2.1 %collective-permute-done.2.ya_ref = f32[2,4,8,128]{3,2,1,0:T(8,128)S(1)} collective-permute-done((f32[2,4,8,128]{3,2,1,0:T(8,128)S(1)}, f32[2,4,8,128]{3,2,1,0:T(8,128)S(1)}, u32[]{:S(2)}, u32[]{:S(2)}) %collective-permute-start.2) | collective-permute-done | bytes 32800 | tf_op jit(solution)/shard_map/ppermute | solution.py:366
  18.4 1.3 %all-to-all-done.res_ref = f32[16,8,128]{2,1,0:T(8,128)S(1)} async-done(((f32[16,8,128]{2,1,0:T(8,128)}), f32[16,8,128]{2,1,0:T(8,128)S(1)}, u32[]{:S(2)}, u32[]{:S(2)}) %all-to-all-start) | async-done | bytes 65568 | tf_op jit(solution)/shard_map/all_to_all | solution.py:405
  19.7 0.0 collective-permute-done.1.xb_ref
  19.7 0.0 collective-permute-done.xa_ref
  19.7 0.0 copy-done.3
  19.7 0.0 copy-done.1
  19.7 0.0 copy-done.2
  19.7 3.0 %middle.1 = (f32[2,64,8,128]{3,2,1,0:T(8,128)S(1)}, f32[4,8,128]{2,1,0:T(8,128)S(1)}, f32[64,8,128]{2,1,0:T(8,128)S(1)}, f32[64,8,128]{2,1,0:T(8,128)S(1)}, f32[2,4,8,128]{3,2,1,0:T(8,128)S(1)}) custom-call(f32[2,64,8,128]{3,2,1,0:T(8,128)S(1)} %copy-done.1, f32[2,64,8,128]{3,2,1,0:T(8,128)S(1)} %copy-done.3, f32[64,8,128]{2,1,0:T(8,128)S(1)} %copy-done.2, ...), custom_call_target="tpu_custom_call" | custom-call | tf_op jit(solution)/shard_map/middle/pallas_call | solution.py:377
  22.7 0.2 collective-permute-start.4
  22.9 1.1 %collective-permute-start.5 = (f32[64,8,128]{2,1,0:T(8,128)S(1)}, f32[64,8,128]{2,1,0:T(8,128)S(1)}, u32[]{:S(2)}, u32[]{:S(2)}) collective-permute-start(f32[64,8,128]{2,1,0:T(8,128)S(1)} %get-tuple-element.13), channel_id=1, source_target_pairs={{0,16},{1,17},{2,18},{3,19},{4,8},{5,9},{6,10},{7,11},{8,4},{9,5},... | collective-permute-start | bytes 786440 | tf_op jit(solution)/shard_map/ppermute | solution.py:366
  24.1 0.0 collective-permute-start.7
  24.1 1.2 %collective-permute-start.6 = (f32[2,4,8,128]{3,2,1,0:T(8,128)S(1)}, f32[2,4,8,128]{3,2,1,0:T(8,128)S(1)}, u32[]{:S(2)}, u32[]{:S(2)}) collective-permute-start(f32[2,4,8,128]{3,2,1,0:T(8,128)S(1)} %get-tuple-element.14), channel_id=1, source_target_pairs={{0,1},{1,0},{2,3},{3,2},{4,5},{5,4},{6,7},{7,6},{8,9},{9,8},{10,11... | collective-permute-start | bytes 98312 | tf_op jit(solution)/shard_map/ppermute | solution.py:366
  25.3 0.8 %copy.11 = f32[2,64,8,128]{3,2,1,0:T(8,128)} copy(f32[2,64,8,128]{3,2,1,0:T(8,128)S(1)} %get-tuple-element.17.mid_ref) | data formatting | bytes 1048576
  26.1 0.0 collective-permute-done.7.yb_ref
  26.1 1.9 %collective-permute-done.6.ya_ref = f32[2,4,8,128]{3,2,1,0:T(8,128)S(1)} collective-permute-done((f32[2,4,8,128]{3,2,1,0:T(8,128)S(1)}, f32[2,4,8,128]{3,2,1,0:T(8,128)S(1)}, u32[]{:S(2)}, u32[]{:S(2)}) %collective-permute-start.6) | collective-permute-done | bytes 32800 | tf_op jit(solution)/shard_map/ppermute | solution.py:366
  28.0 0.0 collective-permute-done.4.xa_ref
  28.0 1.3 %collective-permute-done.5.xb_ref = f32[64,8,128]{2,1,0:T(8,128)S(1)} collective-permute-done((f32[64,8,128]{2,1,0:T(8,128)S(1)}, f32[64,8,128]{2,1,0:T(8,128)S(1)}, u32[]{:S(2)}, u32[]{:S(2)}) %collective-permute-start.5) | collective-permute-done | bytes 262176 | tf_op jit(solution)/shard_map/ppermute | solution.py:366
  29.3 2.7 %after.1 = f32[2,64,8,128]{3,2,1,0:T(8,128)} custom-call(f32[2,64,8,128]{3,2,1,0:T(8,128)S(1)} %get-tuple-element.17.mid_ref, f32[2,64,8,128]{3,2,1,0:T(8,128)S(1)} %copy-done.1, f32[64,8,128]{2,1,0:T(8,128)S(1)} %copy-done.2, f32[64,8,128]{2,1,0:T(8,128)S(1)} %collective-permute-done.4.xa_ref, f32[64,8,128]{2,1,0:T(8,128)S(1)} %collective-permute-done.5.xb_ref, ...), custom_call_target="tpu_custom_call" | custom-call | tf_op jit(solution)/shard_map/after/pallas_call | solution.py:377
Async XLA Ops:
  0.6 1.0 %copy-start = (f32[2,64,8,128]{3,2,1,0:T(8,128)S(1)}, f32[2,64,8,128]{3,2,1,0:T(8,128)}, u32[]{:S(2)}) copy-start(f32[2,64,8,128]{3,2,1,0:T(8,128)} %now_ref.7) | copy-start | bytes 1572868
  1.7 4.3 %copy-start.4 = (bf16[16,2,4096]{2,1,0:T(2,128)(2,1)S(1)}, bf16[16,2,4096]{2,1,0:T(2,128)(2,1)}, u32[]{:S(2)}) copy-start(bf16[16,2,4096]{2,1,0:T(2,128)(2,1)} %param.11) | copy-start | bytes 786436
  1.7 4.3 %copy-start.5 = (s32[4096]{0:T(1024)S(1)}, s32[4096]{0:T(1024)}, u32[]{:S(2)}) copy-start(s32[4096]{0:T(1024)} %param.15) | copy-start | bytes 49156
  1.7 4.3 %copy-start.6 = (s32[2,16]{1,0:T(2,128)S(1)}, s32[2,16]{1,0:T(2,128)}, u32[]{:S(2)}) copy-start(s32[2,16]{1,0:T(2,128)} %signs_ref.1) | copy-start | bytes 388
  1.7 4.3 %copy-start.7 = (s32[16]{0:T(128)S(1)}, s32[16]{0:T(128)}, u32[]{:S(2)}) copy-start(s32[16]{0:T(128)} %sx_ref.1) | copy-start | bytes 196
  1.7 4.3 %copy-start.8 = (s32[16]{0:T(128)S(1)}, s32[16]{0:T(128)}, u32[]{:S(2)}) copy-start(s32[16]{0:T(128)} %sy_ref.1) | copy-start | bytes 196
  1.7 18.0 %copy-start.3 = (f32[2,64,8,128]{3,2,1,0:T(8,128)S(1)}, f32[2,64,8,128]{3,2,1,0:T(8,128)}, u32[]{:S(2)}) copy-start(f32[2,64,8,128]{3,2,1,0:T(8,128)} %old_ref.1) | copy-start | bytes 1572868
  1.8 17.9 %copy-start.1 = (f32[2,64,8,128]{3,2,1,0:T(8,128)S(1)}, f32[2,64,8,128]{3,2,1,0:T(8,128)}, u32[]{:S(2)}) copy-start(f32[2,64,8,128]{3,2,1,0:T(8,128)} %now_ref.7) | copy-start | bytes 1572868
  1.8 17.9 %collective-permute-start.1 = (f32[64,8,128]{2,1,0:T(8,128)S(1)}, f32[64,8,128]{2,1,0:T(8,128)S(1)}, u32[]{:S(2)}, u32[]{:S(2)}) collective-permute-start(f32[64,8,128]{2,1,0:T(8,128)S(1)} %pack_xb.1), channel_id=1, source_target_pairs={{0,16},{1,17},{2,18},{3,19},{4,8},{5,9},{6,10},{7,11},{8,4},{9,5},... | collective-permute-start | bytes 786440 | tf_op jit(solution)/shard_map/ppermute | solution.py:366
  5.7 14.0 %copy-start.2 = (f32[64,8,128]{2,1,0:T(8,128)S(1)}, f32[64,8,128]{2,1,0:T(8,128)}, u32[]{:S(2)}) copy-start(f32[64,8,128]{2,1,0:T(8,128)} %courant_ref.3) | copy-start | bytes 786436
  5.7 14.0 %collective-permute-start = (f32[64,8,128]{2,1,0:T(8,128)S(1)}, f32[64,8,128]{2,1,0:T(8,128)S(1)}, u32[]{:S(2)}, u32[]{:S(2)}) collective-permute-start(f32[64,8,128]{2,1,0:T(8,128)S(1)} %get-tuple-element.9), channel_id=1, source_target_pairs={{0,4},{1,5},{2,6},{3,7},{4,0},{5,1},{6,2},{7,3},{8,12},{9,13},{10,... | collective-permute-start | bytes 786440 | tf_op jit(solution)/shard_map/ppermute | solution.py:366
  7.5 12.2 %all-to-all-start = ((f32[16,8,128]{2,1,0:T(8,128)}), f32[16,8,128]{2,1,0:T(8,128)S(1)}, u32[]{:S(2)}, u32[]{:S(2)}) async-start(f32[16,8,128]{2,1,0:T(8,128)} %residual.1), calls=%async_computation | async-start | bytes 131072 | tf_op jit(solution)/shard_map/all_to_all | solution.py:405
  12.9 3.4 %collective-permute-start.3 = (f32[2,4,8,128]{3,2,1,0:T(8,128)S(1)}, f32[2,4,8,128]{3,2,1,0:T(8,128)S(1)}, u32[]{:S(2)}, u32[]{:S(2)}) collective-permute-start(f32[2,4,8,128]{3,2,1,0:T(8,128)S(1)} %get-tuple-element.10), channel_id=1, source_target_pairs={{0,4},{1,2},{2,1},{3,7},{4,0},{5,6},{6,5},{7,3},{8,12},{9,10},{10,... | collective-permute-start | bytes 98312 | tf_op jit(solution)/shard_map/ppermute | solution.py:366
  13.3 5.1 %collective-permute-start.2 = (f32[2,4,8,128]{3,2,1,0:T(8,128)S(1)}, f32[2,4,8,128]{3,2,1,0:T(8,128)S(1)}, u32[]{:S(2)}, u32[]{:S(2)}) collective-permute-start(f32[2,4,8,128]{3,2,1,0:T(8,128)S(1)} %get-tuple-element.10), channel_id=1, source_target_pairs={{0,1},{1,0},{2,3},{3,2},{4,5},{5,4},{6,7},{7,6},{8,9},{9,8},{10,11... | collective-permute-start | bytes 98312 | tf_op jit(solution)/shard_map/ppermute | solution.py:366
  22.7 5.2 %collective-permute-start.4 = (f32[64,8,128]{2,1,0:T(8,128)S(1)}, f32[64,8,128]{2,1,0:T(8,128)S(1)}, u32[]{:S(2)}, u32[]{:S(2)}) collective-permute-start(f32[64,8,128]{2,1,0:T(8,128)S(1)} %get-tuple-element.12), channel_id=1, source_target_pairs={{0,4},{1,5},{2,6},{3,7},{4,0},{5,1},{6,2},{7,3},{8,12},{9,13},{10,... | collective-permute-start | bytes 786440 | tf_op jit(solution)/shard_map/ppermute | solution.py:366
  22.9 6.4 %collective-permute-start.5 = (f32[64,8,128]{2,1,0:T(8,128)S(1)}, f32[64,8,128]{2,1,0:T(8,128)S(1)}, u32[]{:S(2)}, u32[]{:S(2)}) collective-permute-start(f32[64,8,128]{2,1,0:T(8,128)S(1)} %get-tuple-element.13), channel_id=1, source_target_pairs={{0,16},{1,17},{2,18},{3,19},{4,8},{5,9},{6,10},{7,11},{8,4},{9,5},... | collective-permute-start | bytes 786440 | tf_op jit(solution)/shard_map/ppermute | solution.py:366
  24.1 2.0 %collective-permute-start.7 = (f32[2,4,8,128]{3,2,1,0:T(8,128)S(1)}, f32[2,4,8,128]{3,2,1,0:T(8,128)S(1)}, u32[]{:S(2)}, u32[]{:S(2)}) collective-permute-start(f32[2,4,8,128]{3,2,1,0:T(8,128)S(1)} %get-tuple-element.14), channel_id=1, source_target_pairs={{0,4},{1,2},{2,1},{3,7},{4,0},{5,6},{6,5},{7,3},{8,12},{9,10},{10,... | collective-permute-start | bytes 98312 | tf_op jit(solution)/shard_map/ppermute | solution.py:366
  24.1 3.9 %collective-permute-start.6 = (f32[2,4,8,128]{3,2,1,0:T(8,128)S(1)}, f32[2,4,8,128]{3,2,1,0:T(8,128)S(1)}, u32[]{:S(2)}, u32[]{:S(2)}) collective-permute-start(f32[2,4,8,128]{3,2,1,0:T(8,128)S(1)} %get-tuple-element.14), channel_id=1, source_target_pairs={{0,1},{1,0},{2,3},{3,2},{4,5},{5,4},{6,7},{7,6},{8,9},{9,8},{10,11... | collective-permute-start | bytes 98312 | tf_op jit(solution)/shard_map/ppermute | solution.py:366

commit v3 on v2

v3 whole, which is shorter than its diff:
```python
import functools

import jax
import jax.numpy as jnp
import ml_dtypes
import numpy as np
from jax import lax
from jax.experimental import pallas as pl
from jax.experimental.pallas import tpu as pltpu
from jax.sharding import PartitionSpec as P

REC_DEV = 256
RDEPTH = 2
HALO = 4
LANES = 128
SUB = 8
GROUP = 16
AXES = ("group", "gx", "gy")
F32, BF16 = jnp.float32, jnp.bfloat16

coef_zero = -205.0 / 72.0
coef_rest = (8.0 / 5.0, -1.0 / 5.0, 8.0 / 315.0, -1.0 / 560.0)
coef_high = [float(np.float32(c).astype(ml_dtypes.bfloat16)) for c in coef_rest]
coef_low = [float(np.float32(c - h).astype(ml_dtypes.bfloat16)) for c, h in zip(coef_rest, coef_high)]

VM = pl.BlockSpec(memory_space=pltpu.VMEM)
SM = pl.BlockSpec(memory_space=pltpu.SMEM)
PARAMS = pltpu.CompilerParams(vmem_limit_bytes=16 * 1024 * 1024)


def near_memory(value):
    return pltpu.with_memory_space_constraint(value, pltpu.VMEM)


def rows_of(shape):
    return lax.broadcasted_iota(jnp.int32, shape, len(shape) - 2)


def lanes_of(shape):
    return lax.broadcasted_iota(jnp.int32, shape, len(shape) - 1)


def dot(left, right):
    return jnp.dot(left, right, preferred_element_type=F32)


def split(value):
    first = value.astype(BF16)
    rest = value - first.astype(F32)
    second = rest.astype(BF16)
    return first, second, (rest - second.astype(F32)).astype(BF16)


def pick(step, coefs):
    out = jnp.zeros(step.shape, F32)
    for m in range(1, HALO + 1):
        out = jnp.where(step == m, coefs[m - 1], out)
    return out.astype(BF16)


def band(coefs):
    shape = (LANES, LANES)
    return pick(jnp.abs(rows_of(shape) - lanes_of(shape)), coefs)


def side(coefs):
    shape = (LANES, LANES)
    c = rows_of(shape) & 7
    j = lanes_of(shape)
    return pick(jnp.where(c < HALO, j + HALO - c, LANES + c - HALO - j), coefs)


def pack_columns(ref, odd, ya_ref, yb_ref):
    lane_group = lanes_of((SUB, LANES)) >> 3
    low = (lanes_of((SUB, LANES)) & 7) < HALO
    pairs = ref.shape[1] // GROUP // 2

    def step(pair, carry):
        for field in range(2):
            both = []
            for group in range(2):
                tile = None
                for q in range(GROUP):
                    cells = ref[field, (pair * 2 + group) * GROUP + q]
                    turned = pltpu.roll(cells, (q * 2 * HALO + HALO) % LANES, 1)
                    tile = turned if tile is None else jnp.where(lane_group == q, turned, tile)
                both.append(tile)
            last = jnp.where(low, both[0], pltpu.roll(both[1], HALO, 1))
            first = jnp.where(low, pltpu.roll(both[0], LANES - HALO, 1), both[1])
            ya_ref[field * pairs + pair] = jnp.where(odd, first, last)
            yb_ref[field * pairs + pair] = jnp.where(odd, last, first)
        return carry

    lax.fori_loop(0, pairs, step, 0)


def sides_y(ya, yb, odd, no_next, no_prev):
    after = jnp.where(no_next, 0.0, jnp.where(odd, yb, ya))
    before = jnp.where(no_prev, 0.0, jnp.where(odd, ya, yb))
    low = (lanes_of(ya.shape) & 7) < HALO
    return (
        jnp.where(low, before, pltpu.roll(after, HALO, 1)),
        jnp.where(low, pltpu.roll(before, LANES - HALO, 1), after),
    )


def local_y(cells, high, low):
    first, second, _ = split(cells)
    return dot(jnp.concatenate([first, second, first], axis=1), jnp.concatenate([high, high, low], axis=0))


def halo_y(ya_ref, yb_ref, place, out_ref):
    high, low = side(coef_high), side(coef_low)
    weights = jnp.concatenate([high, high, low], axis=0)
    _, odd, _, _, no_next, no_prev = place
    groups = out_ref.shape[1] // GROUP
    lane_group = lanes_of((SUB, LANES)) >> 3
    for field in range(2):
        firsts, seconds = [], []
        for pair in range(groups // 2):
            at = field * (groups // 2) + pair
            for beside in sides_y(ya_ref[at], yb_ref[at], odd, no_next, no_prev):
                first = beside.astype(BF16).astype(F32)
                second = beside - first
                firsts += [jnp.where(lane_group == q, first, 0.0) for q in range(GROUP)]
                seconds += [jnp.where(lane_group == q, second, 0.0) for q in range(GROUP)]
        first, second = [jnp.concatenate(v, axis=0).astype(BF16) for v in (firsts, seconds)]
        total = dot(jnp.concatenate([first, second, first], axis=1), weights)
        out_ref[field] = total.reshape(groups * GROUP, SUB, LANES)


def where_am_i(counts):
    at_x, at_y = lax.axis_index("gx"), lax.axis_index("gy")
    return (
        lax.rem(at_x, 2) == 1, lax.rem(at_y, 2) == 1,
        at_x == counts[0] - 1, at_x == 0, at_y == counts[1] - 1, at_y == 0,
    )


def head_rows(first, second):
    return jnp.where(rows_of(first.shape) < HALO, first, pltpu.roll(second, HALO, 0))


def tail_rows(first, second):
    return jnp.where(rows_of(first.shape) < HALO, pltpu.roll(first, HALO, 0), second)


def sides_x(xa, xb, place):
    odd, _, no_next, no_prev, _, _ = place
    after = jnp.where(no_next, 0.0, jnp.where(odd, xb, xa))
    before = jnp.where(no_prev, 0.0, jnp.where(odd, xa, xb))
    low = rows_of(after.shape) < HALO
    return jnp.where(low, after, pltpu.roll(before, HALO, 0)), jnp.where(low, pltpu.roll(after, HALO, 0), before)


def turns(kept):
    row = rows_of((SUB, LANES))
    out = []
    for turn in range(1, SUB):
        coef = coef_rest[min(turn, SUB - turn) - 1]
        inside = row >= turn if turn < HALO else row < turn if turn > HALO else row >= 0
        out.append(jnp.where(inside if kept else jnp.logical_not(inside) | (turn == HALO), coef, 0.0))
    return out


def along_x(cells, coefs):
    total = coefs[0] * pltpu.roll(cells, 1, 0)
    for turn in range(2, SUB):
        total = total + coefs[turn - 1] * pltpu.roll(cells, turn, 0)
    return total


def local_step(now_ref, old_ref, courant_ref, out_ref):
    deep = now_ref.shape[1]
    high, low = band(coef_high), band(coef_low)
    for field in range(2):
        cells = now_ref[field].reshape(deep * SUB, LANES)
        out_ref[field] = local_y(cells, high, low).reshape(deep, SUB, LANES)
    coefs = turns(True)

    def body(depth, static_depth):
        for field in range(2):
            cells = now_ref[field, depth]
            total = 3.0 * coef_zero * cells + out_ref[field, depth] + along_x(cells, coefs)
            for step in range(1, HALO + 1):
                near = None
                if static_depth is None or static_depth + step < deep:
                    near = now_ref[field, depth + step]
                if static_depth is None or static_depth >= step:
                    before = now_ref[field, depth - step]
                    near = before if near is None else near + before
                total = total + coef_rest[step - 1] * near
            out_ref[field, depth] = 2.0 * cells - old_ref[field, depth] + courant_ref[depth] * total

    over_depth(deep, body)


def halo_step(depth, base_ref, courant_ref, xa_ref, xb_ref, part_y_ref, place, coefs):
    sides = sides_x(xa_ref[depth], xb_ref[depth], place)
    return [
        base_ref[field, depth] + courant_ref[depth] * (part_y_ref[field, depth] + along_x(sides[field], coefs))
        for field in range(2)
    ]


def over_depth(deep, body):
    def inner(depth, carry):
        body(depth, None)
        return carry

    for depth in range(HALO):
        body(depth, depth)
    lax.fori_loop(HALO, deep - HALO, inner, 0, unroll=4)
    for depth in range(deep - HALO, deep):
        body(depth, depth)


def residual(counts, cells_x, cells_y, radius_sq, signs_ref, sx_ref, sy_ref, records_ref, cell_ref, out_ref, first):
    shots, rows, _ = records_ref.shape
    chunk = min(rows, 64)
    per = 2 * REC_DEV // LANES
    twice = (rows_of((chunk, chunk // 2)) >> 1 == lanes_of((chunk, chunk // 2))).astype(F32).astype(BF16)

    def chunk_step(c, carry):
        cell = cell_ref[pl.ds(pl.multiple_of(c * (chunk // 2), chunk // 2), chunk // 2), :]
        row, column = lax.shift_right_logical(cell, cells_y.bit_length() - 1), cell & (cells_y - 1)
        row, column = [dot(twice, v.astype(F32).astype(BF16)) for v in (row, column)]
        tile = c * (chunk // per) + rows_of((chunk, LANES)) // per
        tile_x, tile_y = tile // counts[1], tile % counts[1]
        pos_x = (tile_x * cells_x).astype(F32) + row
        pos_y = (tile_y * cells_y).astype(F32) + column
        start = pl.multiple_of(c * chunk, chunk)

        def shot_step(shot, sums):
            dx = pos_x - sx_ref[shot].astype(F32)
            dy = pos_y - sy_ref[shot].astype(F32)
            dist = dx * dx + dy * dy
            whole = dist + radius_sq
            inverse = pl.reciprocal(whole, approx=True)
            inverse = inverse * (2.0 - whole * inverse)
            taped = records_ref[shot, pl.ds(start, chunk), :].astype(F32) * (dist * inverse)
            return tuple(s + signs_ref[code, shot].astype(F32) * taped for code, s in enumerate(sums))

        sums = lax.fori_loop(0, shots, shot_step, (jnp.zeros((chunk, LANES), F32),) * 2, unroll=2)
        for t in range(chunk // per):
            both = [s[t * per : (t + 1) * per] for s in sums]
            out_ref[first + c * (chunk // per) + t] = jnp.concatenate(both, axis=0)
        return carry

    lax.fori_loop(0, rows // chunk, chunk_step, 0)


def prepare_kernel(
    radius_sq, counts, signs_hbm, sx_hbm, sy_hbm, records_hbm, cell_hbm, now_hbm,
    now_ref, cell_ref, xb_ref, xa_ref, ya_ref, yb_ref, records_ref, signs_ref, sx_ref, sy_ref, sems,
):
    odd, odd_y = where_am_i(counts)[:2]
    deep, cells_x, cells_y = now_ref.shape[1:]
    shots = records_ref.shape[0]
    pieces = 4
    copies = []

    def bring(source, target):
        copy = pltpu.make_async_copy(source, target, sems.at[len(copies)])
        copy.start()
        copies.append(copy)

    for piece in range(pieces):
        depths = pl.ds(piece * (deep // pieces), deep // pieces)
        bring(now_hbm.at[:, depths], now_ref.at[:, depths])
    for source, target in ((cell_hbm, cell_ref), (signs_hbm, signs_ref), (sx_hbm, sx_ref), (sy_hbm, sy_ref)):
        bring(source, target)
    for piece in range(pieces):
        some = pl.ds(piece * (shots // pieces), shots // pieces)
        bring(records_hbm.at[some], records_ref.at[some])

    def body(depth, carry):
        first, second = now_ref[0, depth], now_ref[1, depth]
        head, tail = head_rows(first, second), tail_rows(first, second)
        xb_ref[depth] = jnp.where(odd, tail, head)
        xa_ref[depth] = jnp.where(odd, head, tail)
        return carry

    for piece in range(pieces):
        copies[piece].wait()
        lax.fori_loop(piece * (deep // pieces), (piece + 1) * (deep // pieces), body, 0, unroll=4)
    pack_columns(now_ref, odd_y, ya_ref, yb_ref)
    for copy in copies[pieces:]:
        copy.wait()
    residual(counts, cells_x, cells_y, radius_sq, signs_ref, sx_ref, sy_ref, records_ref, cell_ref, xa_ref, deep)


def needed_tiles(counts, x, y):
    return (
        (x, y),
        (jnp.minimum(x + 1, counts[0] - 1), y), (jnp.maximum(x - 1, 0), y),
        (x, jnp.minimum(y + 1, counts[1] - 1)), (x, jnp.maximum(y - 1, 0)),
    )


def inject(pieces, samples, cells_y):
    values, hots = [], []
    for res, cells, row_kept, column_kept in pieces:
        for half in range(REC_DEV // LANES):
            row = lax.shift_right_logical(cells[half], cells_y.bit_length() - 1)
            column = cells[half] & (cells_y - 1)
            in_row = (rows_of((SUB, LANES)) == row) & row_kept(rows_of((SUB, LANES)))
            values.append(jnp.concatenate(
                [
                    jnp.where(in_row, res[code * 4 + half * 2 + sample][None, :], 0.0)
                    for code in range(2)
                    for sample in range(samples)
                ],
                axis=0,
            ))
            at = rows_of((cells_y, LANES))
            hots.append(((at == column) & column_kept(at)).astype(F32).astype(BF16))
    values = jnp.concatenate(split(jnp.concatenate(values, axis=1)), axis=0)
    got = lax.dot_general(
        values, jnp.concatenate(hots, axis=1), (((1,), (1,)), ((), ())), preferred_element_type=F32
    )
    count = 2 * samples * SUB
    return got[:count] + got[count : 2 * count] + got[2 * count :]


def local_kernel(counts, now_ref, old_ref, courant_ref, out_ref):
    local_step(now_ref, old_ref, courant_ref, out_ref)


def packed_sizes(counts):
    return counts[0] * counts[1] // 2, counts[0] * counts[1] // 8


def pack_samples(first, second):
    even = rows_of((SUB, LANES)) % 2 == 0
    return (
        jnp.where(even, first, pltpu.roll(second, 1, 0)),
        jnp.where(even, pltpu.roll(first, SUB - 1, 0), second),
    )


def join_kernel(counts, face_ref, own_ref, other_ref, out_ref, keep_ref):
    faces, at = face_ref.shape[0], own_ref.shape[0] - counts[0] * counts[1]
    out_ref[:faces] = face_ref[...]
    total = lambda x, y: own_ref[at + x * counts[1] + y] + other_ref[at + x * counts[1] + y]
    here = faces
    for high in range(0, counts[0], 4):
        for x in range(high, high + 2):
            for y in range(counts[1]):
                out_ref[here] = pack_samples(total(x, y), total(x + 2, y))[0]
                here += 1
    odd_x, odd_y = [lax.rem(lax.axis_index(axis), 2) for axis in AXES[1:]]
    i = 0
    for high in range(0, counts[0], 4):
        for y in range(0, counts[1], 2):
            x = high + odd_x
            out_ref[here + i] = pack_samples(total(x, y + 1 - odd_y), total(x + 2, y + 1 - odd_y))[1]
            keep_ref[i] = pack_samples(total(x, y + odd_y), total(x + 2, y + odd_y))[1]
            i += 1


def sum_kernel(counts, own_ref, keep_ref, other_ref, before_ref, more_ref, out_ref):
    del before_ref, more_ref
    firsts, seconds = packed_sizes(counts)
    at, at_other = [ref.shape[0] - firsts - seconds for ref in (own_ref, other_ref)]
    out_ref[:firsts] = own_ref[pl.ds(at, firsts)] + other_ref[pl.ds(at_other, firsts)]
    at_keep = keep_ref.shape[0] - seconds
    out_ref[firsts:] = keep_ref[pl.ds(at_keep, seconds)] + other_ref[pl.ds(at_other + firsts, seconds)]


def needed_kernel(counts, own_ref, other_ref, face_ref, out_ref, keep_ref, face_out):
    del face_ref, face_out
    firsts, _ = packed_sizes(counts)
    at_x, at_y = lax.axis_index("gx"), lax.axis_index("gy")
    half = counts[1] // 2
    even = rows_of((SUB, LANES)) % 2 == 0
    total = lambda i: own_ref[i] + other_ref[i]

    def collect(target_ref, y_here):
        for i, (x, y) in enumerate(needed_tiles(counts, at_x, y_here)):
            second_of_pair = lax.rem(lax.div(x, 2), 2) == 1
            got = total((lax.div(x, 4) * 2 + lax.rem(x, 2)) * counts[1] + y)
            got = jnp.where(second_of_pair, pltpu.roll(got, SUB - 1, 0), got)
            if i == 0:
                more = total(firsts + lax.div(x, 4) * half + lax.div(y, 2))
                got = jnp.where(even, got, jnp.where(second_of_pair, more, pltpu.roll(more, 1, 0)))
            target_ref[i] = got

    collect(out_ref, lax.rem(at_y + half, counts[1]))
    collect(keep_ref, at_y)


def middle_kernel(
    counts, base_ref, courant_ref, xa_ref, xb_ref, ya_ref, yb_ref,
    mid_ref, xa_out, xb_out, ya_out, yb_out, part_y_ref,
):
    place = where_am_i(counts)
    deep = base_ref.shape[1]
    halo_y(ya_ref, yb_ref, place, part_y_ref)
    coefs = turns(False)

    def body(depth, carry):
        fields = halo_step(depth, base_ref, courant_ref, xa_ref, xb_ref, part_y_ref, place, coefs)
        for field in range(2):
            mid_ref[field, depth] = fields[field]
        head, tail = head_rows(*fields), tail_rows(*fields)
        xa_out[depth] = jnp.where(place[0], head, tail)
        xb_out[depth] = jnp.where(place[0], tail, head)
        return carry

    lax.fori_loop(0, deep, body, 0, unroll=4)
    pack_columns(mid_ref, place[1], ya_out, yb_out)


def inject_kernel(counts, keep_ref, res_ref, cell_ref, courant_ref, layer_ref):
    _, _, no_next_x, no_prev_x, no_next_y, no_prev_y = where_am_i(counts)
    _, cells_x, cells_y = courant_ref.shape
    tiles = needed_tiles(counts, lax.axis_index("gx"), lax.axis_index("gy"))
    halves = REC_DEV // LANES
    res = [keep_ref[i] + res_ref[i] for i in range(len(tiles))]
    for i, absent in enumerate((no_next_x, no_prev_x, no_next_y, no_prev_y)):
        res[i + 1] = jnp.where(absent, 0.0, res[i + 1])
    cells = [
        [cell_ref[pl.ds((x * counts[1] + y) * halves + half, 1), :] for half in range(halves)] for x, y in tiles
    ]
    every = lambda at: at >= 0
    own = inject([(res[0], cells[0], every, every)], 2, cells_y)
    beside_x = inject(
        [(res[1], cells[1], lambda at: at < HALO, every), (res[2], cells[2], lambda at: at >= SUB - HALO, every)],
        1, cells_y,
    )
    beside_y = inject(
        [(res[3], cells[3], every, lambda at: at < HALO), (res[4], cells[4], every, lambda at: at >= cells_y - HALO)],
        1, cells_y,
    )
    kept, beside = turns(True), turns(False)
    lane = lanes_of((cells_x, cells_y))
    for field in range(2):
        layer = own[2 * field * cells_x : (2 * field + 1) * cells_x]
        side_x, side_y = [v[field * cells_x : (field + 1) * cells_x] for v in (beside_x, beside_y)]
        total = 3.0 * coef_zero * layer + along_x(layer, kept) + along_x(side_x, beside)
        for step in range(1, HALO + 1):
            up = pltpu.roll(jnp.where(lane < step, side_y, layer), cells_y - step, 1)
            down = pltpu.roll(jnp.where(lane >= cells_y - step, side_y, layer), step, 1)
            total = total + coef_rest[step - 1] * (up + down)
        layer_ref[field] = layer
        second = own[(2 * field + 1) * cells_x : (2 * field + 2) * cells_x]
        layer_ref[2 + field] = 2.0 * layer + courant_ref[RDEPTH] * total + second


def after_kernel(
    counts, base_ref, mid_ref, courant_ref, xa_ref, xb_ref, ya_ref, yb_ref, layer_ref,
    out_ref, mid_out, part_y_ref, held_ref, plane_ref, sems,
):
    place = where_am_i(counts)
    deep = base_ref.shape[1]
    beside = turns(False)
    copies = []

    def send_out(source, target):
        copy = pltpu.make_async_copy(source, target, sems.at[len(copies)])
        copy.start()
        copies.append(copy)

    send_out(mid_ref.at[:, pl.ds(0, RDEPTH)], mid_out.at[:, pl.ds(0, RDEPTH)])
    rest = pl.ds(RDEPTH + 1, deep - RDEPTH - 1)
    send_out(mid_ref.at[:, rest], mid_out.at[:, rest])
    for field in range(2):
        plane_ref[field, 0] = mid_ref[field, RDEPTH] + layer_ref[field]
    plane = pl.ds(RDEPTH, 1)
    send_out(plane_ref, mid_out.at[:, plane])

    halo_y(ya_ref, yb_ref, place, part_y_ref)
    size = deep // 4
    for part in range(4):
        def body(depth, carry):
            fields = halo_step(depth, base_ref, courant_ref, xa_ref, xb_ref, part_y_ref, place, beside)
            for field in range(2):
                held_ref[field, depth] = fields[field]
            return carry

        lax.fori_loop(part * size, (part + 1) * size, body, 0, unroll=4)
        if part == 0:
            for field in range(2):
                held_ref[field, RDEPTH] = held_ref[field, RDEPTH] + layer_ref[2 + field]
                for step in range(1, HALO + 1):
                    change = coef_rest[step - 1] * layer_ref[field]
                    for depth in (RDEPTH - step, RDEPTH + step):
                        if depth >= 0:
                            held_ref[field, depth] = held_ref[field, depth] + courant_ref[depth] * change
        depths = pl.ds(part * size, size)
        send_out(held_ref.at[:, depths], out_ref.at[:, depths])
    for copy in copies:
        copy.wait()


def paired(groups, count_x, count_y, partner):
    index = lambda g, x, y: (g * count_x + x) * count_y + y
    return [
        (index(g, x, y), index(*partner(g, x, y)))
        for g in range(groups)
        for x in range(count_x)
        for y in range(count_y)
    ]


def on_device(wave_now, wave_before, courant, records, signs, source_x, source_y, receiver_cell):
    _, deep, cells_x, cells_y = wave_now.shape
    groups, tiles_x, tiles_y = [lax.axis_size(axis) for axis in AXES]
    counts = (tiles_x, tiles_y)
    total_recv = receiver_cell.shape[0]
    tiles = total_recv // REC_DEV
    shots = records.shape[0]
    span = (cells_x * tiles_x + cells_y * tiles_y) // 4

    perms = functools.partial(paired, groups, tiles_x, tiles_y)
    swap_xa = perms(lambda g, x, y: (g, x ^ 1, y))
    swap_ya = perms(lambda g, x, y: (g, x, y ^ 1))
    swap_xb = perms(
        lambda g, x, y: ((g + groups // 2) % groups, x, y) if x in (0, tiles_x - 1) else (g, ((x + 1) ^ 1) - 1, y)
    )
    swap_yb = perms(lambda g, x, y: (g, x ^ 1, y) if y in (0, tiles_y - 1) else (g, x, ((y + 1) ^ 1) - 1))
    swap_along = {
        "gx": lambda step: perms(lambda g, x, y: (g, x ^ step, y)),
        "gy": lambda step: perms(lambda g, x, y: (g, x, y ^ step)),
    }
    steps = [("gx", 1 << i) for i in range(1, (tiles_x - 1).bit_length())]
    steps += [("gy", 1 << i) for i in range(1, (tiles_y - 1).bit_length() - 1)]
    send = lambda value, pairs: lax.ppermute(value, AXES, pairs)

    face_x = pltpu.VMEM((deep, cells_x, cells_y), F32)
    faces = deep // GROUP
    face_y = pltpu.VMEM((faces, cells_x, cells_y), F32)
    tiles_of = lambda count: pltpu.VMEM((count, SUB, LANES), F32)
    wave = wave_now.shape

    def kernel(body, outs, n_scalar, n_array, scratch=(), out_specs=None, aliases={}):
        name = body.__name__.removesuffix("_kernel")

        def call(*args):
            args = args[:n_scalar] + tuple(near_memory(a) for a in args[n_scalar:])
            return pl.pallas_call(
                functools.partial(body, counts),
                out_shape=outs,
                in_specs=[SM] * n_scalar + [VM] * n_array,
                out_specs=out_specs if out_specs is not None else jax.tree.map(lambda _: VM, outs),
                scratch_shapes=scratch,
                input_output_aliases=aliases,
                compiler_params=PARAMS,
                name=name,
            )(*args)

        return call

    wave_v = pltpu.VMEM(wave, F32)
    cell_rows = receiver_cell.reshape(total_recv // LANES, LANES)
    record_rows = records.reshape(shots, 2, total_recv // LANES, LANES).transpose(0, 2, 1, 3)
    record_rows = record_rows.reshape(shots, 2 * total_recv // LANES, LANES)
    far = lambda value: pltpu.with_memory_space_constraint(value, pltpu.HBM)
    now, cells, xb, xa, ya, yb = pl.pallas_call(
        functools.partial(prepare_kernel, float(span * span), counts),
        out_shape=(wave_v, pltpu.VMEM(cell_rows.shape, jnp.int32), face_x, tiles_of(deep + tiles), face_y, face_y),
        in_specs=[pl.BlockSpec(memory_space=pltpu.HBM)] * 6,
        out_specs=(VM,) * 6,
        scratch_shapes=[
            pltpu.VMEM(record_rows.shape, BF16),
            pltpu.SMEM(signs.shape, jnp.int32), pltpu.SMEM((shots,), jnp.int32), pltpu.SMEM((shots,), jnp.int32),
            pltpu.SemaphoreType.DMA((12,)),
        ],
        compiler_params=PARAMS,
        name="prepare",
    )(*(far(a) for a in (signs, source_x, source_y, record_rows, cell_rows, wave_now)))
    xb_in, xa_in = send(xb, swap_xb), send(xa, swap_xa)
    left = sum(packed_sizes(counts))
    partial_res, keep = kernel(join_kernel, (tiles_of(faces + left), tiles_of(packed_sizes(counts)[1])), 0, 3)(
        ya, xa, xa_in
    )
    ya_in, yb_in = send(partial_res, swap_ya), send(yb, swap_yb)
    other = ya_in
    base = kernel(local_kernel, wave_v, 0, 3)(now, wave_before, courant)
    for axis, step in steps:
        partial_res = kernel(sum_kernel, tiles_of(left), 0, 5)(partial_res, keep, other, base, yb_in)
        keep = partial_res
        other = send(partial_res, swap_along[axis](step))
    wave_middle, xa, xb, ya, yb = kernel(middle_kernel, (wave_v, face_x, face_x, face_y, face_y), 0, 6, [wave_v])(
        base, courant, xa_in, xb_in, ya_in, yb_in
    )
    wanted, keep, xb = kernel(needed_kernel, (tiles_of(5), tiles_of(5), face_x), 0, 3, aliases={2: 2})(
        partial_res, other, xb
    )
    xb_in, xa_in = send(xb, swap_xb), send(xa, swap_xa)
    res_in = send(wanted, swap_along["gy"](tiles_y // 2))
    ya_in, yb_in = send(ya, swap_ya), send(yb, swap_yb)
    base = kernel(local_kernel, wave_v, 0, 3)(wave_middle, now, courant)
    plane = (2, 1, cells_x, cells_y)
    layers = kernel(inject_kernel, tiles_of(4), 0, 4)(keep, res_in, cells, courant)
    wave_after, wave_middle = kernel(
        after_kernel, (jax.ShapeDtypeStruct(wave, F32),) * 2, 0, 8,
        [wave_v, wave_v, pltpu.VMEM(plane, F32), pltpu.SemaphoreType.DMA((7,))],
        out_specs=(pl.BlockSpec(memory_space=pl.ANY),) * 2,
    )(base, wave_middle, courant, xa_in, xb_in, ya_in, yb_in, layers)
    return (wave_after, wave_middle)


def solution(mesh):
    return jax.shard_map(
        on_device,
        mesh=mesh,
        in_specs=(
            P("group", None, "gx", "gy"),
            P("group", None, "gx", "gy"),
            P("group", "gx", "gy"),
            P(("group", "gx", "gy"), None, None),
            P("group", ("gx", "gy")),
            P(("group", "gx", "gy")),
            P(("group", "gx", "gy")),
            P("group"),
        ),
        out_specs=(P("group", None, "gx", "gy"), P("group", None, "gx", "gy")),
        check_vma=False,
    )
```

time: 32.3 us -> 25.3 us (0.78)
  waiting for transfers between devices: 6.68 us -> 4.09 us
  starting transfers between devices: 14.5 us -> 12.2 us
  local copies, waits for them, and re-layouts: 1.87 us -> 0.01 us
    all_to_all x1 -> x0, starting transfers between devices: 5.35 us -> none  [on_device(): res_in = lax.all_to_all(partial_res, ('gx', 'gy'), 0, 0, tiled=True)]
    ppermute x8 -> x10, starting transfers between devices: 9.12 us -> 12.2 us  [on_device(): send = lambda value, pairs: lax.ppermute(value, AXES, pairs)]
    unnamed x19 -> x4, local copies, waits for them, and re-layouts: 1.87 us -> 0.01 us
    all_to_all x1 -> x0, waiting for transfers between devices: 1.33 us -> none  [on_device(): res_in = lax.all_to_all(partial_res, ('gx', 'gy'), 0, 0, tiled=True)]
    ppermute x8 -> x10, waiting for transfers between devices: 5.36 us -> 4.09 us  [on_device(): send = lambda value, pairs: lax.ppermute(value, AXES, pairs)]
    pallas_call x4 -> x8, Pallas kernels: 6.71 us -> 6.01 us  [call(): pl.pallas_call(functools.partial(body, counts), out_shape=outs, in_specs=...]
    pallas_call x1, Pallas kernels: 1.57 us -> 2.22 us  [on_device(): pl.pallas_call(functools.partial(prepare_kernel, float(span * span), coun...]
  transfers between devices with their start and end apart: 9 -> 10, of which waited for: 4 -> 4; matrix products, arithmetic and copies ran while one was open for 2% -> 0% of each run, Pallas kernels for 8% -> 17%
where the time goes in v3:
time: 25.3 us; the launch traced here: 25.2 us
  starting transfers between devices  12.2 us (48%)
  Pallas kernels  8.23 us (33%)
  waiting for transfers between devices  4.09 us (16%)
  between operations  0.71 us (3%)
    ppermute x10, starting transfers between devices, on_device(): send = lambda value, pairs: lax.ppermute(value, AXES, pairs)  12.2 us
    pallas_call x8, Pallas kernels, call(): pl.pallas_call(functools.partial(body, counts), out_shape=outs, in_specs=...  6.01 us
    ppermute x10, waiting for transfers between devices, on_device(): send = lambda value, pairs: lax.ppermute(value, AXES, pairs)  4.09 us
    pallas_call x1, Pallas kernels, on_device(): pl.pallas_call(functools.partial(prepare_kernel, float(span * span), coun...  2.22 us
  transfers between devices with their start and end apart: 10, of which 4 were waited for; matrix products, arithmetic and copies ran while one was open for 0% of the time, Pallas kernels for 17%

profile of v3, /device:TPU:0, one launch (start us, length us, event | category | flops | bytes accessed | tf_op | source)
XLA Modules:
  0.0 25.2 jit_solution(4306634645966993370)
XLA Ops:
  0.6 0.0 copy-start.1
  0.6 2.2 %prepare.1 = (f32[2,64,8,128]{3,2,1,0:T(8,128)S(1)}, s32[32,128]{1,0:T(8,128)S(1)}, f32[64,8,128]{2,1,0:T(8,128)S(1)}, f32[80,8,128]{2,1,0:T(8,128)S(1)}, f32[4,...) custom-call(s32[2,16]{1,0:T(2,128)} %signs_hbm.1, s32[16]{0:T(128)} %sx_hbm.1, s32[16]{0:T(128)} %sy_hbm.1, ...), custom_call_target="tpu_custom_call" | custom-call | tf_op jit(solution)/shard_map/prepare/pallas_call | solution.py:560
  2.9 0.5 %collective-permute-start = (f32[80,8,128]{2,1,0:T(8,128)S(1)}, f32[80,8,128]{2,1,0:T(8,128)S(1)}, u32[]{:S(2)}, u32[]{:S(2)}) collective-permute-start(f32[80,8,128]{2,1,0:T(8,128)S(1)} %get-tuple-element.19.own_ref), channel_id=1, source_target_pairs={{0,4},{1,5},{2,6},{3,7},{4,0},{5,1},{6,2},{7,3},{8,12},{9,13},{10,... | collective-permute-start | bytes 983048 | tf_op jit(solution)/shard_map/ppermute | solution.py:529
  3.4 2.6 %collective-permute-start.1 = (f32[64,8,128]{2,1,0:T(8,128)S(1)}, f32[64,8,128]{2,1,0:T(8,128)S(1)}, u32[]{:S(2)}, u32[]{:S(2)}) collective-permute-start(f32[64,8,128]{2,1,0:T(8,128)S(1)} %get-tuple-element.20), channel_id=1, source_target_pairs={{0,16},{1,17},{2,18},{3,19},{4,8},{5,9},{6,10},{7,11},{8,4},{9,5},... | collective-permute-start | bytes 786440 | tf_op jit(solution)/shard_map/ppermute | solution.py:529
  6.0 0.0 collective-permute-done.other_ref.xa_ref
  6.0 0.0 copy-start
  6.0 1.7 %collective-permute-start.2 = (f32[14,8,128]{2,1,0:T(8,128)S(1)}, f32[14,8,128]{2,1,0:T(8,128)S(1)}, u32[]{:S(2)}, u32[]{:S(2)}) collective-permute-start(f32[14,8,128]{2,1,0:T(8,128)S(1)} %get-tuple-element.22.own_ref), channel_id=1, source_target_pairs={{0,1},{1,0},{2,3},{3,2},{4,5},{5,4},{6,7},{7,6},{8,9},{9,8},{10,11... | collective-permute-start | bytes 172040 | tf_op jit(solution)/shard_map/ppermute | solution.py:529
  7.7 0.0 collective-permute-start.3
  7.7 0.0 copy-done.1
  7.7 0.0 copy-done
  7.7 1.2 %local.2.base_ref.before_ref = f32[2,64,8,128]{3,2,1,0:T(8,128)S(1)} custom-call(f32[2,64,8,128]{3,2,1,0:T(8,128)S(1)} %get-tuple-element.18.now_ref.old_ref, f32[2,64,8,128]{3,2,1,0:T(8,128)S(1)} %copy-done.1, f32[64,8,128]{2,1,0:T(8,128)S(1)} %copy-done), custom_call_target="tpu_custom_call" | custom-call | tf_op jit(solution)/shard_map/local/pallas_call | solution.py:542
  8.9 0.0 collective-permute-done.3.yb_ref.more_ref
  8.9 1.3 %collective-permute-done.2.ya_ref.other_ref = f32[14,8,128]{2,1,0:T(8,128)S(1)} collective-permute-done((f32[14,8,128]{2,1,0:T(8,128)S(1)}, f32[14,8,128]{2,1,0:T(8,128)S(1)}, u32[]{:S(2)}, u32[]{:S(2)}) %collective-permute-start.2) | collective-permute-done | bytes 57376 | tf_op jit(solution)/shard_map/ppermute | solution.py:529
  10.2 1.6 %collective-permute-start.5 = (f32[10,8,128]{2,1,0:T(8,128)S(1)}, f32[10,8,128]{2,1,0:T(8,128)S(1)}, u32[]{:S(2)}, u32[]{:S(2)}) collective-permute-start(f32[10,8,128]{2,1,0:T(8,128)S(1)} %sum.1.own_ref), channel_id=1, source_target_pairs={{0,8},{1,9},{2,10},{3,11},{4,12},{5,13},{6,14},{7,15},{8,0},{9,1},... | collective-permute-start | bytes 122888 | tf_op jit(solution)/shard_map/ppermute | solution.py:529
  11.8 0.0 collective-permute-done.1.xb_ref
  11.8 1.5 %middle.1 = (f32[2,64,8,128]{3,2,1,0:T(8,128)S(1)}, f32[64,8,128]{2,1,0:T(8,128)S(1)}, f32[64,8,128]{2,1,0:T(8,128)S(1)}, f32[4,8,128]{2,1,0:T(8,128)S(1)}, f32[4,8,128]{2,1,0:T(8,128)S(1)}) custom-call(f32[2,64,8,128]{3,2,1,0:T(8,128)S(1)} %local.2.base_ref.before_ref, f32[64,8,128]{2,1,0:T(8,128)S(1)} %copy-done, ...), custom_call_target="tpu_custom_call" | custom-call | tf_op jit(solution)/shard_map/middle/pallas_call | solution.py:542
  13.3 0.0 collective-permute-start.4
  13.4 0.9 %collective-permute-done.5.other_ref = f32[10,8,128]{2,1,0:T(8,128)S(1)} collective-permute-done((f32[10,8,128]{2,1,0:T(8,128)S(1)}, f32[10,8,128]{2,1,0:T(8,128)S(1)}, u32[]{:S(2)}, u32[]{:S(2)}) %collective-permute-start.5) | collective-permute-done | bytes 40992 | tf_op jit(solution)/shard_map/ppermute | solution.py:529
  14.3 1.6 %collective-permute-start.6 = (f32[64,8,128]{2,1,0:T(8,128)S(1)}, f32[64,8,128]{2,1,0:T(8,128)S(1)}, u32[]{:S(2)}, u32[]{:S(2)}) collective-permute-start(f32[64,8,128]{2,1,0:T(8,128)S(1)} %get-tuple-element.28), channel_id=1, source_target_pairs={{0,16},{1,17},{2,18},{3,19},{4,8},{5,9},{6,10},{7,11},{8,4},{9,5},... | collective-permute-start | bytes 786440 | tf_op jit(solution)/shard_map/ppermute | solution.py:529
  15.9 3.8 %collective-permute-start.9 = (f32[5,8,128]{2,1,0:T(8,128)S(1)}, f32[5,8,128]{2,1,0:T(8,128)S(1)}, u32[]{:S(2)}, u32[]{:S(2)}) collective-permute-start(f32[5,8,128]{2,1,0:T(8,128)S(1)} %get-tuple-element.32), channel_id=1, source_target_pairs={{0,2},{1,3},{2,0},{3,1},{4,6},{5,7},{6,4},{7,5},{8,10},{9,11},{10,... | collective-permute-start | bytes 61448 | tf_op jit(solution)/shard_map/ppermute | solution.py:529
  19.7 0.4 %collective-permute-start.7 = (f32[4,8,128]{2,1,0:T(8,128)S(1)}, f32[4,8,128]{2,1,0:T(8,128)S(1)}, u32[]{:S(2)}, u32[]{:S(2)}) collective-permute-start(f32[4,8,128]{2,1,0:T(8,128)S(1)} %get-tuple-element.29), channel_id=1, source_target_pairs={{0,1},{1,0},{2,3},{3,2},{4,5},{5,4},{6,7},{7,6},{8,9},{9,8},{10,11... | collective-permute-start | bytes 49160 | tf_op jit(solution)/shard_map/ppermute | solution.py:529
  20.1 0.0 collective-permute-start.8
  20.1 1.2 %local.3.base_ref = f32[2,64,8,128]{3,2,1,0:T(8,128)S(1)} custom-call(f32[2,64,8,128]{3,2,1,0:T(8,128)S(1)} %get-tuple-element.24.now_ref.mid_ref, f32[2,64,8,128]{3,2,1,0:T(8,128)S(1)} %get-tuple-element.18.now_ref.old_ref, f32[64,8,128]{2,1,0:T(8,128)S(1)} %copy-done), custom_call_target="tpu_custom_call" | custom-call | tf_op jit(solution)/shard_map/local/pallas_call | solution.py:542
  21.2 0.4 %collective-permute-done.9.res_ref = f32[5,8,128]{2,1,0:T(8,128)S(1)} collective-permute-done((f32[5,8,128]{2,1,0:T(8,128)S(1)}, f32[5,8,128]{2,1,0:T(8,128)S(1)}, u32[]{:S(2)}, u32[]{:S(2)}) %collective-permute-start.9) | collective-permute-done | bytes 20512 | tf_op jit(solution)/shard_map/ppermute | solution.py:529
  21.7 0.3 %inject.1.layer_ref = f32[4,8,128]{2,1,0:T(8,128)S(1)} custom-call(f32[5,8,128]{2,1,0:T(8,128)S(1)} %get-tuple-element.31.keep_ref, f32[5,8,128]{2,1,0:T(8,128)S(1)} %collective-permute-done.9.res_ref, s32[32,128]{1,0:T(8,128)S(1)} %get-tuple-element.33.cell_ref, f32[64,8,128]{2,1,0:T(8,128)S(1)} %copy-done), custom_call_target="tpu_custom_call" | custom-call | tf_op jit(solution)/shard_map/inject/pallas_call | solution.py:542
  22.0 1.4 %collective-permute-done.7.ya_ref = f32[4,8,128]{2,1,0:T(8,128)S(1)} collective-permute-done((f32[4,8,128]{2,1,0:T(8,128)S(1)}, f32[4,8,128]{2,1,0:T(8,128)S(1)}, u32[]{:S(2)}, u32[]{:S(2)}) %collective-permute-start.7) | collective-permute-done | bytes 16416 | tf_op jit(solution)/shard_map/ppermute | solution.py:529
  23.4 0.0 collective-permute-done.8.yb_ref
  23.4 0.0 collective-permute-done.4.xa_ref
  23.4 0.0 collective-permute-done.6.xb_ref
  23.4 1.8 %after.1 = (f32[2,64,8,128]{3,2,1,0:T(8,128)}, f32[2,64,8,128]{3,2,1,0:T(8,128)}) custom-call(f32[2,64,8,128]{3,2,1,0:T(8,128)S(1)} %local.3.base_ref, f32[2,64,8,128]{3,2,1,0:T(8,128)S(1)} %get-tuple-element.24.now_ref.mid_ref, f32[64,8,128]{2,1,0:T(8,128)S(1)} %copy-done, f32[64,8,128]{2,1,0:T(8,128)S(1)} %collective-permute-done.4.xa_ref, ...), custom_call_target="tpu_custom_call" | custom-call | tf_op jit(solution)/shard_map/after/pallas_call | solution.py:542
  (3 shorter events, 0.1 us)
Async XLA Ops:
  0.6 7.1 %copy-start.1 = (f32[2,64,8,128]{3,2,1,0:T(8,128)S(1)}, f32[2,64,8,128]{3,2,1,0:T(8,128)}, u32[]{:S(2)}) copy-start(f32[2,64,8,128]{3,2,1,0:T(8,128)} %old_ref.1) | copy-start | bytes 1572868
  2.9 3.1 %collective-permute-start = (f32[80,8,128]{2,1,0:T(8,128)S(1)}, f32[80,8,128]{2,1,0:T(8,128)S(1)}, u32[]{:S(2)}, u32[]{:S(2)}) collective-permute-start(f32[80,8,128]{2,1,0:T(8,128)S(1)} %get-tuple-element.19.own_ref), channel_id=1, source_target_pairs={{0,4},{1,5},{2,6},{3,7},{4,0},{5,1},{6,2},{7,3},{8,12},{9,13},{10,... | collective-permute-start | bytes 983048 | tf_op jit(solution)/shard_map/ppermute | solution.py:529
  3.4 8.4 %collective-permute-start.1 = (f32[64,8,128]{2,1,0:T(8,128)S(1)}, f32[64,8,128]{2,1,0:T(8,128)S(1)}, u32[]{:S(2)}, u32[]{:S(2)}) collective-permute-start(f32[64,8,128]{2,1,0:T(8,128)S(1)} %get-tuple-element.20), channel_id=1, source_target_pairs={{0,16},{1,17},{2,18},{3,19},{4,8},{5,9},{6,10},{7,11},{8,4},{9,5},... | collective-permute-start | bytes 786440 | tf_op jit(solution)/shard_map/ppermute | solution.py:529
  6.0 1.7 %copy-start = (f32[64,8,128]{2,1,0:T(8,128)S(1)}, f32[64,8,128]{2,1,0:T(8,128)}, u32[]{:S(2)}) copy-start(f32[64,8,128]{2,1,0:T(8,128)} %courant_ref.9) | copy-start | bytes 786436
  6.0 4.2 %collective-permute-start.2 = (f32[14,8,128]{2,1,0:T(8,128)S(1)}, f32[14,8,128]{2,1,0:T(8,128)S(1)}, u32[]{:S(2)}, u32[]{:S(2)}) collective-permute-start(f32[14,8,128]{2,1,0:T(8,128)S(1)} %get-tuple-element.22.own_ref), channel_id=1, source_target_pairs={{0,1},{1,0},{2,3},{3,2},{4,5},{5,4},{6,7},{7,6},{8,9},{9,8},{10,11... | collective-permute-start | bytes 172040 | tf_op jit(solution)/shard_map/ppermute | solution.py:529
  7.7 1.2 %collective-permute-start.3 = (f32[4,8,128]{2,1,0:T(8,128)S(1)}, f32[4,8,128]{2,1,0:T(8,128)S(1)}, u32[]{:S(2)}, u32[]{:S(2)}) collective-permute-start(f32[4,8,128]{2,1,0:T(8,128)S(1)} %get-tuple-element.23), channel_id=1, source_target_pairs={{0,4},{1,2},{2,1},{3,7},{4,0},{5,6},{6,5},{7,3},{8,12},{9,10},{10,... | collective-permute-start | bytes 49160 | tf_op jit(solution)/shard_map/ppermute | solution.py:529
  10.2 4.0 %collective-permute-start.5 = (f32[10,8,128]{2,1,0:T(8,128)S(1)}, f32[10,8,128]{2,1,0:T(8,128)S(1)}, u32[]{:S(2)}, u32[]{:S(2)}) collective-permute-start(f32[10,8,128]{2,1,0:T(8,128)S(1)} %sum.1.own_ref), channel_id=1, source_target_pairs={{0,8},{1,9},{2,10},{3,11},{4,12},{5,13},{6,14},{7,15},{8,0},{9,1},... | collective-permute-start | bytes 122888 | tf_op jit(solution)/shard_map/ppermute | solution.py:529
  13.3 10.1 %collective-permute-start.4 = (f32[64,8,128]{2,1,0:T(8,128)S(1)}, f32[64,8,128]{2,1,0:T(8,128)S(1)}, u32[]{:S(2)}, u32[]{:S(2)}) collective-permute-start(f32[64,8,128]{2,1,0:T(8,128)S(1)} %get-tuple-element.25), channel_id=1, source_target_pairs={{0,4},{1,5},{2,6},{3,7},{4,0},{5,1},{6,2},{7,3},{8,12},{9,13},{10,... | collective-permute-start | bytes 786440 | tf_op jit(solution)/shard_map/ppermute | solution.py:529
  14.3 9.2 %collective-permute-start.6 = (f32[64,8,128]{2,1,0:T(8,128)S(1)}, f32[64,8,128]{2,1,0:T(8,128)S(1)}, u32[]{:S(2)}, u32[]{:S(2)}) collective-permute-start(f32[64,8,128]{2,1,0:T(8,128)S(1)} %get-tuple-element.28), channel_id=1, source_target_pairs={{0,16},{1,17},{2,18},{3,19},{4,8},{5,9},{6,10},{7,11},{8,4},{9,5},... | collective-permute-start | bytes 786440 | tf_op jit(solution)/shard_map/ppermute | solution.py:529
  15.9 5.8 %collective-permute-start.9 = (f32[5,8,128]{2,1,0:T(8,128)S(1)}, f32[5,8,128]{2,1,0:T(8,128)S(1)}, u32[]{:S(2)}, u32[]{:S(2)}) collective-permute-start(f32[5,8,128]{2,1,0:T(8,128)S(1)} %get-tuple-element.32), channel_id=1, source_target_pairs={{0,2},{1,3},{2,0},{3,1},{4,6},{5,7},{6,4},{7,5},{8,10},{9,11},{10,... | collective-permute-start | bytes 61448 | tf_op jit(solution)/shard_map/ppermute | solution.py:529
  19.7 3.7 %collective-permute-start.7 = (f32[4,8,128]{2,1,0:T(8,128)S(1)}, f32[4,8,128]{2,1,0:T(8,128)S(1)}, u32[]{:S(2)}, u32[]{:S(2)}) collective-permute-start(f32[4,8,128]{2,1,0:T(8,128)S(1)} %get-tuple-element.29), channel_id=1, source_target_pairs={{0,1},{1,0},{2,3},{3,2},{4,5},{5,4},{6,7},{7,6},{8,9},{9,8},{10,11... | collective-permute-start | bytes 49160 | tf_op jit(solution)/shard_map/ppermute | solution.py:529
  20.1 3.4 %collective-permute-start.8 = (f32[4,8,128]{2,1,0:T(8,128)S(1)}, f32[4,8,128]{2,1,0:T(8,128)S(1)}, u32[]{:S(2)}, u32[]{:S(2)}) collective-permute-start(f32[4,8,128]{2,1,0:T(8,128)S(1)} %get-tuple-element.30), channel_id=1, source_target_pairs={{0,4},{1,2},{2,1},{3,7},{4,0},{5,6},{6,5},{7,3},{8,12},{9,10},{10,... | collective-permute-start | bytes 49160 | tf_op jit(solution)/shard_map/ppermute | solution.py:529

commit v4 on v3

--- a/solution.py
+++ b/solution.py
@@ -215,7 +215,7 @@
         body(depth, depth)
 
 
-def residual(counts, cells_x, cells_y, radius_sq, signs_ref, sx_ref, sy_ref, records_ref, cell_ref, out_ref, first):
+def residual(counts, cells_x, cells_y, radius_sq, signs_ref, sx_ref, sy_ref, records_ref, cell_ref, out_ref):
     shots, rows, _ = records_ref.shape
     chunk = min(rows, 64)
     per = 2 * REC_DEV // LANES
@@ -244,20 +244,16 @@
         sums = lax.fori_loop(0, shots, shot_step, (jnp.zeros((chunk, LANES), F32),) * 2, unroll=2)
         for t in range(chunk // per):
             both = [s[t * per : (t + 1) * per] for s in sums]
-            out_ref[first + c * (chunk // per) + t] = jnp.concatenate(both, axis=0)
+            out_ref[c * (chunk // per) + t] = jnp.concatenate(both, axis=0)
         return carry
 
     lax.fori_loop(0, rows // chunk, chunk_step, 0)
 
 
-def prepare_kernel(
-    radius_sq, counts, signs_hbm, sx_hbm, sy_hbm, records_hbm, cell_hbm, now_hbm,
-    now_ref, cell_ref, xb_ref, xa_ref, ya_ref, yb_ref, records_ref, signs_ref, sx_ref, sy_ref, sems,
+def bring_kernel(
+    radius_sq, counts, signs_hbm, sx_hbm, sy_hbm, records_hbm, cell_hbm, now_hbm, old_hbm, courant_hbm,
+    now_ref, old_ref, courant_ref, cell_ref, res_ref, xa_ref, xb_ref, records_ref, signs_ref, sx_ref, sy_ref, sems,
 ):
-    odd, odd_y = where_am_i(counts)[:2]
-    deep, cells_x, cells_y = now_ref.shape[1:]
-    shots = records_ref.shape[0]
-    pieces = 4
     copies = []
 
     def bring(source, target):
@@ -265,14 +261,17 @@
         copy.start()
         copies.append(copy)
 
-    for piece in range(pieces):
-        depths = pl.ds(piece * (deep // pieces), deep // pieces)
-        bring(now_hbm.at[:, depths], now_ref.at[:, depths])
-    for source, target in ((cell_hbm, cell_ref), (signs_hbm, signs_ref), (sx_hbm, sx_ref), (sy_hbm, sy_ref)):
+    for source, target in (
+        (cell_hbm, cell_ref), (signs_hbm, signs_ref), (sx_hbm, sx_ref), (sy_hbm, sy_ref), (records_hbm, records_ref),
+        (now_hbm, now_ref), (old_hbm, old_ref), (courant_hbm, courant_ref),
+    ):
         bring(source, target)
-    for piece in range(pieces):
-        some = pl.ds(piece * (shots // pieces), shots // pieces)
-        bring(records_hbm.at[some], records_ref.at[some])
+    for copy in copies[:5]:
+        copy.wait()
+    _, deep, cells_x, cells_y = now_ref.shape
+    residual(counts, cells_x, cells_y, radius_sq, signs_ref, sx_ref, sy_ref, records_ref, cell_ref, res_ref)
+    copies[5].wait()
+    odd = where_am_i(counts)[0]
 
     def body(depth, carry):
         first, second = now_ref[0, depth], now_ref[1, depth]
@@ -281,13 +280,13 @@
         xa_ref[depth] = jnp.where(odd, head, tail)
         return carry
 
-    for piece in range(pieces):
-        copies[piece].wait()
-        lax.fori_loop(piece * (deep // pieces), (piece + 1) * (deep // pieces), body, 0, unroll=4)
-    pack_columns(now_ref, odd_y, ya_ref, yb_ref)
-    for copy in copies[pieces:]:
+    lax.fori_loop(0, deep, body, 0, unroll=4)
+    for copy in copies[6:]:
         copy.wait()
-    residual(counts, cells_x, cells_y, radius_sq, signs_ref, sx_ref, sy_ref, records_ref, cell_ref, xa_ref, deep)
+
+
+def pack_kernel(counts, now_ref, ya_ref, yb_ref):
+    pack_columns(now_ref, where_am_i(counts)[1], ya_ref, yb_ref)
 
 
 def needed_tiles(counts, x, y):
@@ -323,6 +322,11 @@
     return got[:count] + got[count : 2 * count] + got[2 * count :]
 
 
+def second_local_kernel(counts, now_ref, old_ref, courant_ref, before_ref, out_ref):
+    del before_ref
+    local_step(now_ref, old_ref, courant_ref, out_ref)
+
+
 def local_kernel(counts, now_ref, old_ref, courant_ref, out_ref):
     local_step(now_ref, old_ref, courant_ref, out_ref)
 
@@ -339,7 +343,8 @@
     )
 
 
-def join_kernel(counts, face_ref, own_ref, other_ref, out_ref, keep_ref):
+def join_kernel(counts, face_ref, own_ref, other_ref, xa_ref, out_ref, keep_ref, xa_out):
+    del xa_ref, xa_out
     faces, at = face_ref.shape[0], own_ref.shape[0] - counts[0] * counts[1]
     out_ref[:faces] = face_ref[...]
     total = lambda x, y: own_ref[at + x * counts[1] + y] + other_ref[at + x * counts[1] + y]
@@ -368,8 +373,8 @@
     out_ref[firsts:] = keep_ref[pl.ds(at_keep, seconds)] + other_ref[pl.ds(at_other + firsts, seconds)]
 
 
-def needed_kernel(counts, own_ref, other_ref, face_ref, out_ref, keep_ref, face_out):
-    del face_ref, face_out
+def needed_kernel(counts, own_ref, other_ref, before_ref, ya_ref, yb_ref, out_ref, keep_ref, *handed_on):
+    del before_ref, ya_ref, yb_ref, handed_on
     firsts, _ = packed_sizes(counts)
     at_x, at_y = lax.axis_index("gx"), lax.axis_index("gy")
     half = counts[1] // 2
@@ -534,7 +539,7 @@
     tiles_of = lambda count: pltpu.VMEM((count, SUB, LANES), F32)
     wave = wave_now.shape
 
-    def kernel(body, outs, n_scalar, n_array, scratch=(), out_specs=None, aliases={}):
+    def kernel(body, outs, n_scalar, n_array, scratch=(), out_specs=None, aliases={}, cost=None):
         name = body.__name__.removesuffix("_kernel")
 
         def call(*args):
@@ -546,6 +551,7 @@
                 out_specs=out_specs if out_specs is not None else jax.tree.map(lambda _: VM, outs),
                 scratch_shapes=scratch,
                 input_output_aliases=aliases,
+                cost_estimate=cost,
                 compiler_params=PARAMS,
                 name=name,
             )(*args)
@@ -557,48 +563,54 @@
     record_rows = records.reshape(shots, 2, total_recv // LANES, LANES).transpose(0, 2, 1, 3)
     record_rows = record_rows.reshape(shots, 2 * total_recv // LANES, LANES)
     far = lambda value: pltpu.with_memory_space_constraint(value, pltpu.HBM)
-    now, cells, xb, xa, ya, yb = pl.pallas_call(
-        functools.partial(prepare_kernel, float(span * span), counts),
-        out_shape=(wave_v, pltpu.VMEM(cell_rows.shape, jnp.int32), face_x, tiles_of(deep + tiles), face_y, face_y),
-        in_specs=[pl.BlockSpec(memory_space=pltpu.HBM)] * 6,
-        out_specs=(VM,) * 6,
+    left = sum(packed_sizes(counts))
+    pad = left + 2
+    now, old, speed, cells, partial_res, xa, xb = pl.pallas_call(
+        functools.partial(bring_kernel, float(span * span), counts),
+        out_shape=(
+            wave_v, wave_v, pltpu.VMEM(courant.shape, F32), pltpu.VMEM(cell_rows.shape, jnp.int32), tiles_of(tiles),
+            face_x, face_x,
+        ),
+        in_specs=[pl.BlockSpec(memory_space=pltpu.HBM)] * 8,
+        out_specs=(VM,) * 7,
         scratch_shapes=[
             pltpu.VMEM(record_rows.shape, BF16),
             pltpu.SMEM(signs.shape, jnp.int32), pltpu.SMEM((shots,), jnp.int32), pltpu.SMEM((shots,), jnp.int32),
-            pltpu.SemaphoreType.DMA((12,)),
+            pltpu.SemaphoreType.DMA((8,)),
         ],
         compiler_params=PARAMS,
-        name="prepare",
-    )(*(far(a) for a in (signs, source_x, source_y, record_rows, cell_rows, wave_now)))
-    xb_in, xa_in = send(xb, swap_xb), send(xa, swap_xa)
-    left = sum(packed_sizes(counts))
-    partial_res, keep = kernel(join_kernel, (tiles_of(faces + left), tiles_of(packed_sizes(counts)[1])), 0, 3)(
-        ya, xa, xa_in
-    )
-    ya_in, yb_in = send(partial_res, swap_ya), send(yb, swap_yb)
+        name="bring",
+    )(*(far(a) for a in (signs, source_x, source_y, record_rows, cell_rows, wave_now, wave_before, courant)))
+    xb_in, other = send(xb, swap_xb), send(partial_res, swap_xa)
+    ya, yb = kernel(pack_kernel, (face_y, tiles_of(faces + pad)), 0, 1)(now)
+    yb_in = send(yb, swap_yb)
+    partial_res, keep, xa = kernel(
+        join_kernel, (tiles_of(faces + left), tiles_of(packed_sizes(counts)[1]), face_x), 0, 4, aliases={3: 2},
+    )(ya, partial_res, other, xa)
+    ya_in, xa_in = send(partial_res, swap_ya), send(xa, swap_xa)
     other = ya_in
-    base = kernel(local_kernel, wave_v, 0, 3)(now, wave_before, courant)
+    base = kernel(local_kernel, wave_v, 0, 3)(now, old, speed)
     for axis, step in steps:
         partial_res = kernel(sum_kernel, tiles_of(left), 0, 5)(partial_res, keep, other, base, yb_in)
         keep = partial_res
         other = send(partial_res, swap_along[axis](step))
     wave_middle, xa, xb, ya, yb = kernel(middle_kernel, (wave_v, face_x, face_x, face_y, face_y), 0, 6, [wave_v])(
-        base, courant, xa_in, xb_in, ya_in, yb_in
-    )
-    wanted, keep, xb = kernel(needed_kernel, (tiles_of(5), tiles_of(5), face_x), 0, 3, aliases={2: 2})(
-        partial_res, other, xb
-    )
+        base, speed, xa_in, xb_in, ya_in, yb_in
+    )
+    wanted, keep, ya, yb = kernel(
+        needed_kernel, (tiles_of(5), tiles_of(5), face_y, face_y), 0, 5, aliases={3: 2, 4: 3}, cost=pl.CostEstimate(flops=30*10**8, bytes_accessed=0, transcendentals=0)
+    )(partial_res, other, wave_middle, ya, yb)
     xb_in, xa_in = send(xb, swap_xb), send(xa, swap_xa)
     res_in = send(wanted, swap_along["gy"](tiles_y // 2))
     ya_in, yb_in = send(ya, swap_ya), send(yb, swap_yb)
-    base = kernel(local_kernel, wave_v, 0, 3)(wave_middle, now, courant)
+    base = kernel(second_local_kernel, wave_v, 0, 4, cost=pl.CostEstimate(flops=0*10**8, bytes_accessed=0, transcendentals=0))(wave_middle, now, speed, keep)
     plane = (2, 1, cells_x, cells_y)
-    layers = kernel(inject_kernel, tiles_of(4), 0, 4)(keep, res_in, cells, courant)
+    layers = kernel(inject_kernel, tiles_of(4), 0, 4)(keep, res_in, cells, speed)
     wave_after, wave_middle = kernel(
         after_kernel, (jax.ShapeDtypeStruct(wave, F32),) * 2, 0, 8,
         [wave_v, wave_v, pltpu.VMEM(plane, F32), pltpu.SemaphoreType.DMA((7,))],
         out_specs=(pl.BlockSpec(memory_space=pl.ANY),) * 2,
-    )(base, wave_middle, courant, xa_in, xb_in, ya_in, yb_in, layers)
+    )(base, wave_middle, speed, xa_in, xb_in, ya_in, yb_in, layers)
     return (wave_after, wave_middle)
 
 

time: 25.3 us -> 23.1 us (0.913)
  waiting for transfers between devices: 4.09 us -> 1.86 us
    ppermute x10 -> x11, waiting for transfers between devices: 4.09 us -> 1.86 us  [on_device(): send = lambda value, pairs: lax.ppermute(value, AXES, pairs)]
    pallas_call x1, Pallas kernels: 2.22 us -> 1.67 us  [on_device(): pl.pallas_call(functools.partial(bring_kernel, float(span * span), counts...]
    pallas_call x8 -> x9, Pallas kernels: 6.01 us -> 6.39 us  [call(): pl.pallas_call(functools.partial(body, counts), out_shape=outs, in_specs=...]
    ppermute x10 -> x11, starting transfers between devices: 12.2 us -> 12.3 us  [on_device(): send = lambda value, pairs: lax.ppermute(value, AXES, pairs)]
  transfers between devices with their start and end apart: 10 -> 11, of which waited for: 4 -> 4; matrix products, arithmetic and copies ran while one was open for 0% -> 0% of each run, Pallas kernels for 17% -> 20%
where the time goes in v4:
time: 23.1 us; the launch traced here: 22.9 us
  starting transfers between devices  12.3 us (53%)
  Pallas kernels  8.06 us (35%)
  waiting for transfers between devices  1.86 us (8%)
  between operations  0.7 us (3%)
    ppermute x11, starting transfers between devices, on_device(): send = lambda value, pairs: lax.ppermute(value, AXES, pairs)  12.3 us
    pallas_call x9, Pallas kernels, call(): pl.pallas_call(functools.partial(body, counts), out_shape=outs, in_specs=...  6.39 us
    ppermute x11, waiting for transfers between devices, on_device(): send = lambda value, pairs: lax.ppermute(value, AXES, pairs)  1.86 us
    pallas_call x1, Pallas kernels, on_device(): pl.pallas_call(functools.partial(bring_kernel, float(span * span), counts...  1.67 us
  transfers between devices with their start and end apart: 11, of which 4 were waited for; matrix products, arithmetic and copies ran while one was open for 0% of the time, Pallas kernels for 20%

profile of v4, /device:TPU:0, one launch (start us, length us, event | category | flops | bytes accessed | tf_op | source)
XLA Modules:
  0.0 22.9 jit_solution(5115027472575788346)
XLA Ops:
  0.6 1.7 %bring.1 = (f32[2,64,8,128]{3,2,1,0:T(8,128)S(1)}, f32[2,64,8,128]{3,2,1,0:T(8,128)S(1)}, f32[64,8,128]{2,1,0:T(8,128)S(1)}, s32[32,128]{1,0:T(8,128)S(1)}, f32[...) custom-call(s32[2,16]{1,0:T(2,128)} %signs_hbm.1, s32[16]{0:T(128)} %sx_hbm.1, ...), custom_call_target="tpu_custom_call" | custom-call | tf_op jit(solution)/shard_map/bring/pallas_call | solution.py:568
  2.3 0.5 %collective-permute-start = (f32[16,8,128]{2,1,0:T(8,128)S(1)}, f32[16,8,128]{2,1,0:T(8,128)S(1)}, u32[]{:S(2)}, u32[]{:S(2)}) collective-permute-start(f32[16,8,128]{2,1,0:T(8,128)S(1)} %get-tuple-element.27.own_ref), channel_id=1, source_target_pairs={{0,4},{1,5},{2,6},{3,7},{4,0},{5,1},{6,2},{7,3},{8,12},{9,13},{10,... | collective-permute-start | bytes 196616 | tf_op jit(solution)/shard_map/ppermute | solution.py:534
  2.8 2.6 %collective-permute-start.2 = (f32[64,8,128]{2,1,0:T(8,128)S(1)}, f32[64,8,128]{2,1,0:T(8,128)S(1)}, u32[]{:S(2)}, u32[]{:S(2)}) collective-permute-start(f32[64,8,128]{2,1,0:T(8,128)S(1)} %get-tuple-element.30), channel_id=1, source_target_pairs={{0,16},{1,17},{2,18},{3,19},{4,8},{5,9},{6,10},{7,11},{8,4},{9,5},... | collective-permute-start | bytes 786440 | tf_op jit(solution)/shard_map/ppermute | solution.py:534
  5.4 0.4 %pack.1 = (f32[4,8,128]{2,1,0:T(8,128)S(1)}, f32[16,8,128]{2,1,0:T(8,128)S(1)}) custom-call(f32[2,64,8,128]{3,2,1,0:T(8,128)S(1)} %get-tuple-element.23.now_ref.old_ref), custom_call_target="tpu_custom_call" | custom-call | tf_op jit(solution)/shard_map/pack/pallas_call | solution.py:547
  5.8 0.0 collective-permute-done.other_ref
  5.8 0.2 collective-permute-start.1
  6.0 0.4 %collective-permute-start.4 = (f32[16,8,128]{2,1,0:T(8,128)S(1)}, f32[16,8,128]{2,1,0:T(8,128)S(1)}, u32[]{:S(2)}, u32[]{:S(2)}) collective-permute-start(f32[16,8,128]{2,1,0:T(8,128)S(1)} %get-tuple-element.32), channel_id=1, source_target_pairs={{0,4},{1,2},{2,1},{3,7},{4,0},{5,6},{6,5},{7,3},{8,12},{9,10},{10,... | collective-permute-start | bytes 196616 | tf_op jit(solution)/shard_map/ppermute | solution.py:534
  6.4 2.8 %collective-permute-start.3 = (f32[14,8,128]{2,1,0:T(8,128)S(1)}, f32[14,8,128]{2,1,0:T(8,128)S(1)}, u32[]{:S(2)}, u32[]{:S(2)}) collective-permute-start(f32[14,8,128]{2,1,0:T(8,128)S(1)} %get-tuple-element.31.own_ref), channel_id=1, source_target_pairs={{0,1},{1,0},{2,3},{3,2},{4,5},{5,4},{6,7},{7,6},{8,9},{9,8},{10,11... | collective-permute-start | bytes 172040 | tf_op jit(solution)/shard_map/ppermute | solution.py:534
  9.2 1.2 %local.1.base_ref.before_ref = f32[2,64,8,128]{3,2,1,0:T(8,128)S(1)} custom-call(f32[2,64,8,128]{3,2,1,0:T(8,128)S(1)} %get-tuple-element.23.now_ref.old_ref, f32[2,64,8,128]{3,2,1,0:T(8,128)S(1)} %get-tuple-element.24.old_ref, f32[64,8,128]{2,1,0:T(8,128)S(1)} %get-tuple-element.25.courant_ref), custom_call_target="tpu_custom_call" | custom-call | tf_op jit(solution)/shard_map/local/pallas_call | solution.py:547
  10.4 0.0 collective-permute-done.4.yb_ref.more_ref
  10.4 1.0 %collective-permute-done.3.ya_ref.other_ref = f32[14,8,128]{2,1,0:T(8,128)S(1)} collective-permute-done((f32[14,8,128]{2,1,0:T(8,128)S(1)}, f32[14,8,128]{2,1,0:T(8,128)S(1)}, u32[]{:S(2)}, u32[]{:S(2)}) %collective-permute-start.3) | collective-permute-done | bytes 57376 | tf_op jit(solution)/shard_map/ppermute | solution.py:534
  11.4 1.5 %collective-permute-start.5 = (f32[10,8,128]{2,1,0:T(8,128)S(1)}, f32[10,8,128]{2,1,0:T(8,128)S(1)}, u32[]{:S(2)}, u32[]{:S(2)}) collective-permute-start(f32[10,8,128]{2,1,0:T(8,128)S(1)} %sum.1.own_ref), channel_id=1, source_target_pairs={{0,8},{1,9},{2,10},{3,11},{4,12},{5,13},{6,14},{7,15},{8,0},{9,1},... | collective-permute-start | bytes 122888 | tf_op jit(solution)/shard_map/ppermute | solution.py:534
  12.9 0.0 collective-permute-done.2.xb_ref
  12.9 0.0 collective-permute-done.1.xa_ref
  12.9 1.5 %middle.1 = (f32[2,64,8,128]{3,2,1,0:T(8,128)S(1)}, f32[64,8,128]{2,1,0:T(8,128)S(1)}, f32[64,8,128]{2,1,0:T(8,128)S(1)}, f32[4,8,128]{2,1,0:T(8,128)S(1)}, f32[4,8,128]{2,1,0:T(8,128)S(1)}) custom-call(f32[2,64,8,128]{3,2,1,0:T(8,128)S(1)} %local.1.base_ref.before_ref, f32[64,8,128]{2,1,0:T(8,128)S(1)} %get-tuple-element.25.courant_ref, ...), custom_call_target="tpu_custom_call" | custom-call | tf_op jit(solution)/shard_map/middle/pallas_call | solution.py:547
  14.4 0.0 collective-permute-start.6
  14.4 0.8 %collective-permute-start.7 = (f32[64,8,128]{2,1,0:T(8,128)S(1)}, f32[64,8,128]{2,1,0:T(8,128)S(1)}, u32[]{:S(2)}, u32[]{:S(2)}) collective-permute-start(f32[64,8,128]{2,1,0:T(8,128)S(1)} %get-tuple-element.39), channel_id=1, source_target_pairs={{0,16},{1,17},{2,18},{3,19},{4,8},{5,9},{6,10},{7,11},{8,4},{9,5},... | collective-permute-start | bytes 786440 | tf_op jit(solution)/shard_map/ppermute | solution.py:534
  15.3 0.1 collective-permute-done.5.other_ref
  15.4 2.0 %collective-permute-start.10 = (f32[5,8,128]{2,1,0:T(8,128)S(1)}, f32[5,8,128]{2,1,0:T(8,128)S(1)}, u32[]{:S(2)}, u32[]{:S(2)}) collective-permute-start(f32[5,8,128]{2,1,0:T(8,128)S(1)} %get-tuple-element.42), channel_id=1, source_target_pairs={{0,2},{1,3},{2,0},{3,1},{4,6},{5,7},{6,4},{7,5},{8,10},{9,11},{10,... | collective-permute-start | bytes 61448 | tf_op jit(solution)/shard_map/ppermute | solution.py:534
  17.4 1.5 %collective-permute-start.8 = (f32[4,8,128]{2,1,0:T(8,128)S(1)}, f32[4,8,128]{2,1,0:T(8,128)S(1)}, u32[]{:S(2)}, u32[]{:S(2)}) collective-permute-start(f32[4,8,128]{2,1,0:T(8,128)S(1)} %get-tuple-element.40), channel_id=1, source_target_pairs={{0,1},{1,0},{2,3},{3,2},{4,5},{5,4},{6,7},{7,6},{8,9},{9,8},{10,11... | collective-permute-start | bytes 49160 | tf_op jit(solution)/shard_map/ppermute | solution.py:534
  18.9 0.0 collective-permute-start.9
  18.9 1.2 %second_local.1.base_ref = f32[2,64,8,128]{3,2,1,0:T(8,128)S(1)} custom-call(f32[2,64,8,128]{3,2,1,0:T(8,128)S(1)} %get-tuple-element.33.before_ref.now_ref.mid_ref, f32[2,64,8,128]{3,2,1,0:T(8,128)S(1)} %get-tuple-element.23.now_ref.old_ref, f32[64,8,128]{2,1,0:T(8,128)S(1)} %get-tuple-element.25.courant_ref, ...), custom_call_target="tpu_custom_call" | custom-call | tf_op jit(solution)/shard_map/second_local/pallas_call | solution.py:547
  20.0 0.1 collective-permute-done.10.res_ref
  20.2 0.3 %inject.1.layer_ref = f32[4,8,128]{2,1,0:T(8,128)S(1)} custom-call(f32[5,8,128]{2,1,0:T(8,128)S(1)} %get-tuple-element.37.before_ref.keep_ref, f32[5,8,128]{2,1,0:T(8,128)S(1)} %collective-permute-done.10.res_ref, s32[32,128]{1,0:T(8,128)S(1)} %get-tuple-element.43.cell_ref, f32[64,8,128]{2,1,0:T(8,128)S(1)} %get-tuple-element.25.courant_ref), custom_call_target="tpu_custom_call" | custom-call | tf_op jit(solution)/shard_map/inject/pallas_call | solution.py:547
  20.5 0.6 %collective-permute-done.8.ya_ref = f32[4,8,128]{2,1,0:T(8,128)S(1)} collective-permute-done((f32[4,8,128]{2,1,0:T(8,128)S(1)}, f32[4,8,128]{2,1,0:T(8,128)S(1)}, u32[]{:S(2)}, u32[]{:S(2)}) %collective-permute-start.8) | collective-permute-done | bytes 16416 | tf_op jit(solution)/shard_map/ppermute | solution.py:534
  21.1 0.0 collective-permute-done.9.yb_ref
  21.1 0.0 collective-permute-done.6.xa_ref
  21.1 0.0 collective-permute-done.7.xb_ref
  21.1 1.8 %after.1 = (f32[2,64,8,128]{3,2,1,0:T(8,128)}, f32[2,64,8,128]{3,2,1,0:T(8,128)}) custom-call(f32[2,64,8,128]{3,2,1,0:T(8,128)S(1)} %second_local.1.base_ref, f32[2,64,8,128]{3,2,1,0:T(8,128)S(1)} %get-tuple-element.33.before_ref.now_ref.mid_ref, f32[64,8,128]{2,1,0:T(8,128)S(1)} %get-tuple-element.25.courant_ref, ...), custom_call_target="tpu_custom_call" | custom-call | tf_op jit(solution)/shard_map/after/pallas_call | solution.py:547
  (3 shorter events, 0.1 us)
Async XLA Ops:
  2.3 3.5 %collective-permute-start = (f32[16,8,128]{2,1,0:T(8,128)S(1)}, f32[16,8,128]{2,1,0:T(8,128)S(1)}, u32[]{:S(2)}, u32[]{:S(2)}) collective-permute-start(f32[16,8,128]{2,1,0:T(8,128)S(1)} %get-tuple-element.27.own_ref), channel_id=1, source_target_pairs={{0,4},{1,5},{2,6},{3,7},{4,0},{5,1},{6,2},{7,3},{8,12},{9,13},{10,... | collective-permute-start | bytes 196616 | tf_op jit(solution)/shard_map/ppermute | solution.py:534
  2.8 10.1 %collective-permute-start.2 = (f32[64,8,128]{2,1,0:T(8,128)S(1)}, f32[64,8,128]{2,1,0:T(8,128)S(1)}, u32[]{:S(2)}, u32[]{:S(2)}) collective-permute-start(f32[64,8,128]{2,1,0:T(8,128)S(1)} %get-tuple-element.30), channel_id=1, source_target_pairs={{0,16},{1,17},{2,18},{3,19},{4,8},{5,9},{6,10},{7,11},{8,4},{9,5},... | collective-permute-start | bytes 786440 | tf_op jit(solution)/shard_map/ppermute | solution.py:534
  5.8 7.1 %collective-permute-start.1 = (f32[64,8,128]{2,1,0:T(8,128)S(1)}, f32[64,8,128]{2,1,0:T(8,128)S(1)}, u32[]{:S(2)}, u32[]{:S(2)}) collective-permute-start(f32[64,8,128]{2,1,0:T(8,128)S(1)} %get-tuple-element.29), channel_id=1, source_target_pairs={{0,4},{1,5},{2,6},{3,7},{4,0},{5,1},{6,2},{7,3},{8,12},{9,13},{10,... | collective-permute-start | bytes 786440 | tf_op jit(solution)/shard_map/ppermute | solution.py:534
  6.0 4.3 %collective-permute-start.4 = (f32[16,8,128]{2,1,0:T(8,128)S(1)}, f32[16,8,128]{2,1,0:T(8,128)S(1)}, u32[]{:S(2)}, u32[]{:S(2)}) collective-permute-start(f32[16,8,128]{2,1,0:T(8,128)S(1)} %get-tuple-element.32), channel_id=1, source_target_pairs={{0,4},{1,2},{2,1},{3,7},{4,0},{5,6},{6,5},{7,3},{8,12},{9,10},{10,... | collective-permute-start | bytes 196616 | tf_op jit(solution)/shard_map/ppermute | solution.py:534
  6.4 5.0 %collective-permute-start.3 = (f32[14,8,128]{2,1,0:T(8,128)S(1)}, f32[14,8,128]{2,1,0:T(8,128)S(1)}, u32[]{:S(2)}, u32[]{:S(2)}) collective-permute-start(f32[14,8,128]{2,1,0:T(8,128)S(1)} %get-tuple-element.31.own_ref), channel_id=1, source_target_pairs={{0,1},{1,0},{2,3},{3,2},{4,5},{5,4},{6,7},{7,6},{8,9},{9,8},{10,11... | collective-permute-start | bytes 172040 | tf_op jit(solution)/shard_map/ppermute | solution.py:534
  11.4 4.0 %collective-permute-start.5 = (f32[10,8,128]{2,1,0:T(8,128)S(1)}, f32[10,8,128]{2,1,0:T(8,128)S(1)}, u32[]{:S(2)}, u32[]{:S(2)}) collective-permute-start(f32[10,8,128]{2,1,0:T(8,128)S(1)} %sum.1.own_ref), channel_id=1, source_target_pairs={{0,8},{1,9},{2,10},{3,11},{4,12},{5,13},{6,14},{7,15},{8,0},{9,1},... | collective-permute-start | bytes 122888 | tf_op jit(solution)/shard_map/ppermute | solution.py:534
  14.4 6.7 %collective-permute-start.6 = (f32[64,8,128]{2,1,0:T(8,128)S(1)}, f32[64,8,128]{2,1,0:T(8,128)S(1)}, u32[]{:S(2)}, u32[]{:S(2)}) collective-permute-start(f32[64,8,128]{2,1,0:T(8,128)S(1)} %get-tuple-element.38), channel_id=1, source_target_pairs={{0,4},{1,5},{2,6},{3,7},{4,0},{5,1},{6,2},{7,3},{8,12},{9,13},{10,... | collective-permute-start | bytes 786440 | tf_op jit(solution)/shard_map/ppermute | solution.py:534
  14.4 6.7 %collective-permute-start.7 = (f32[64,8,128]{2,1,0:T(8,128)S(1)}, f32[64,8,128]{2,1,0:T(8,128)S(1)}, u32[]{:S(2)}, u32[]{:S(2)}) collective-permute-start(f32[64,8,128]{2,1,0:T(8,128)S(1)} %get-tuple-element.39), channel_id=1, source_target_pairs={{0,16},{1,17},{2,18},{3,19},{4,8},{5,9},{6,10},{7,11},{8,4},{9,5},... | collective-permute-start | bytes 786440 | tf_op jit(solution)/shard_map/ppermute | solution.py:534
  15.4 4.7 %collective-permute-start.10 = (f32[5,8,128]{2,1,0:T(8,128)S(1)}, f32[5,8,128]{2,1,0:T(8,128)S(1)}, u32[]{:S(2)}, u32[]{:S(2)}) collective-permute-start(f32[5,8,128]{2,1,0:T(8,128)S(1)} %get-tuple-element.42), channel_id=1, source_target_pairs={{0,2},{1,3},{2,0},{3,1},{4,6},{5,7},{6,4},{7,5},{8,10},{9,11},{10,... | collective-permute-start | bytes 61448 | tf_op jit(solution)/shard_map/ppermute | solution.py:534
  17.4 3.7 %collective-permute-start.8 = (f32[4,8,128]{2,1,0:T(8,128)S(1)}, f32[4,8,128]{2,1,0:T(8,128)S(1)}, u32[]{:S(2)}, u32[]{:S(2)}) collective-permute-start(f32[4,8,128]{2,1,0:T(8,128)S(1)} %get-tuple-element.40), channel_id=1, source_target_pairs={{0,1},{1,0},{2,3},{3,2},{4,5},{5,4},{6,7},{7,6},{8,9},{9,8},{10,11... | collective-permute-start | bytes 49160 | tf_op jit(solution)/shard_map/ppermute | solution.py:534
  18.9 2.3 %collective-permute-start.9 = (f32[4,8,128]{2,1,0:T(8,128)S(1)}, f32[4,8,128]{2,1,0:T(8,128)S(1)}, u32[]{:S(2)}, u32[]{:S(2)}) collective-permute-start(f32[4,8,128]{2,1,0:T(8,128)S(1)} %get-tuple-element.41), channel_id=1, source_target_pairs={{0,4},{1,2},{2,1},{3,7},{4,0},{5,6},{6,5},{7,3},{8,12},{9,10},{10,... | collective-permute-start | bytes 49160 | tf_op jit(solution)/shard_map/ppermute | solution.py:534

commit v5 on v4

--- a/solution.py
+++ b/solution.py
@@ -63,11 +63,12 @@
     return pick(jnp.abs(rows_of(shape) - lanes_of(shape)), coefs)
 
 
-def side(coefs):
+def side():
     shape = (LANES, LANES)
     c = rows_of(shape) & 7
     j = lanes_of(shape)
-    return pick(jnp.where(c < HALO, j + HALO - c, LANES + c - HALO - j), coefs)
+    step = jnp.where(c < HALO, j + HALO - c, LANES + c - HALO - j)
+    return jnp.where(rows_of(shape) < LANES // 2, pick(step, coef_high).astype(F32), pick(step, coef_low).astype(F32)).astype(BF16)
 
 
 def pack_columns(ref, odd, ya_ref, yb_ref):
@@ -110,22 +111,28 @@
 
 
 def halo_y(ya_ref, yb_ref, place, out_ref):
-    high, low = side(coef_high), side(coef_low)
-    weights = jnp.concatenate([high, high, low], axis=0)
+    weights = side()
     _, odd, _, _, no_next, no_prev = place
     groups = out_ref.shape[1] // GROUP
     lane_group = lanes_of((SUB, LANES)) >> 3
+    half, quarter = GROUP // 2, GROUP // 4
     for field in range(2):
-        firsts, seconds = [], []
+        rows = []
         for pair in range(groups // 2):
             at = field * (groups // 2) + pair
             for beside in sides_y(ya_ref[at], yb_ref[at], odd, no_next, no_prev):
                 first = beside.astype(BF16).astype(F32)
-                second = beside - first
-                firsts += [jnp.where(lane_group == q, first, 0.0) for q in range(GROUP)]
-                seconds += [jnp.where(lane_group == q, second, 0.0) for q in range(GROUP)]
-        first, second = [jnp.concatenate(v, axis=0).astype(BF16) for v in (firsts, seconds)]
-        total = dot(jnp.concatenate([first, second, first], axis=1), weights)
+                second = (beside - first).astype(BF16).astype(F32)
+                turned = pltpu.roll(first, LANES // 2, 1)
+                seconds = [pltpu.roll(second, turn, 1) for turn in (LANES // 4, LANES - LANES // 4)]
+                for q in range(GROUP):
+                    other = (q + half) % GROUP
+                    at_second = (q % half + quarter) % half
+                    tile = jnp.where(lane_group == q, first, 0.0)
+                    tile = jnp.where(lane_group == other, turned, tile)
+                    turn = 0 if (at_second - q) % GROUP == quarter else 1
+                    rows.append(jnp.where(lane_group == at_second, seconds[turn], tile))
+        total = dot(jnp.concatenate(rows, axis=0).astype(BF16), weights)
         out_ref[field] = total.reshape(groups * GROUP, SUB, LANES)
 
 
@@ -145,12 +152,25 @@
     return jnp.where(rows_of(first.shape) < HALO, pltpu.roll(first, HALO, 0), second)
 
 
-def sides_x(xa, xb, place):
-    odd, _, no_next, no_prev, _, _ = place
-    after = jnp.where(no_next, 0.0, jnp.where(odd, xb, xa))
-    before = jnp.where(no_prev, 0.0, jnp.where(odd, xa, xb))
+def face_turns(place):
+    _, _, no_next, no_prev, _, _ = place
+    row = rows_of((SUB, LANES)) % HALO
+    after = [jnp.where((row >= d) & jnp.logical_not(no_next), coef_rest[HALO - 1 - d], 0.0) for d in range(HALO)]
+    before = [jnp.where((row + d < HALO) & jnp.logical_not(no_prev), coef_rest[HALO - 1 - d], 0.0) for d in range(HALO)]
+    return after, before
+
+
+def from_faces(xa, xb, odd, coefs):
+    after, before = jnp.where(odd, xb, xa), jnp.where(odd, xa, xb)
+    after_sum, before_sum = coefs[0][0] * after, coefs[1][0] * before
+    for d in range(1, HALO):
+        after_sum = after_sum + coefs[0][d] * pltpu.roll(after, d, 0)
+        before_sum = before_sum + coefs[1][d] * pltpu.roll(before, SUB - d, 0)
     low = rows_of(after.shape) < HALO
-    return jnp.where(low, after, pltpu.roll(before, HALO, 0)), jnp.where(low, pltpu.roll(after, HALO, 0), before)
+    return (
+        jnp.where(low, before_sum, pltpu.roll(after_sum, HALO, 0)),
+        jnp.where(low, pltpu.roll(before_sum, HALO, 0), after_sum),
+    )
 
 
 def turns(kept):
@@ -195,11 +215,10 @@
     over_depth(deep, body)
 
 
-def halo_step(depth, base_ref, courant_ref, xa_ref, xb_ref, part_y_ref, place, coefs):
-    sides = sides_x(xa_ref[depth], xb_ref[depth], place)
+def halo_step(depth, base_ref, courant_ref, xa_ref, xb_ref, part_y_ref, odd, coefs):
+    sides = from_faces(xa_ref[depth], xb_ref[depth], odd, coefs)
     return [
-        base_ref[field, depth] + courant_ref[depth] * (part_y_ref[field, depth] + along_x(sides[field], coefs))
-        for field in range(2)
+        base_ref[field, depth] + courant_ref[depth] * (part_y_ref[field, depth] + sides[field]) for field in range(2)
     ]
 
 
@@ -210,7 +229,7 @@
 
     for depth in range(HALO):
         body(depth, depth)
-    lax.fori_loop(HALO, deep - HALO, inner, 0, unroll=4)
+    lax.fori_loop(HALO, deep - HALO, inner, 0, unroll=8)
     for depth in range(deep - HALO, deep):
         body(depth, depth)
 
@@ -280,7 +299,7 @@
         xa_ref[depth] = jnp.where(odd, head, tail)
         return carry
 
-    lax.fori_loop(0, deep, body, 0, unroll=4)
+    lax.fori_loop(0, deep, body, 0, unroll=8)
     for copy in copies[6:]:
         copy.wait()
 
@@ -402,10 +421,10 @@
     place = where_am_i(counts)
     deep = base_ref.shape[1]
     halo_y(ya_ref, yb_ref, place, part_y_ref)
-    coefs = turns(False)
+    coefs = face_turns(place)
 
     def body(depth, carry):
-        fields = halo_step(depth, base_ref, courant_ref, xa_ref, xb_ref, part_y_ref, place, coefs)
+        fields = halo_step(depth, base_ref, courant_ref, xa_ref, xb_ref, part_y_ref, place[0], coefs)
         for field in range(2):
             mid_ref[field, depth] = fields[field]
         head, tail = head_rows(*fields), tail_rows(*fields)
@@ -413,7 +432,7 @@
         xb_out[depth] = jnp.where(place[0], tail, head)
         return carry
 
-    lax.fori_loop(0, deep, body, 0, unroll=4)
+    lax.fori_loop(0, deep, body, 0, unroll=8)
     pack_columns(mid_ref, place[1], ya_out, yb_out)
 
 
@@ -459,7 +478,7 @@
 ):
     place = where_am_i(counts)
     deep = base_ref.shape[1]
-    beside = turns(False)
+    coefs = face_turns(place)
     copies = []
 
     def send_out(source, target):
@@ -476,15 +495,15 @@
     send_out(plane_ref, mid_out.at[:, plane])
 
     halo_y(ya_ref, yb_ref, place, part_y_ref)
-    size = deep // 4
-    for part in range(4):
+    size = deep // 8
+    for part in range(8):
         def body(depth, carry):
-            fields = halo_step(depth, base_ref, courant_ref, xa_ref, xb_ref, part_y_ref, place, beside)
+            fields = halo_step(depth, base_ref, courant_ref, xa_ref, xb_ref, part_y_ref, place[0], coefs)
             for field in range(2):
                 held_ref[field, depth] = fields[field]
             return carry
 
-        lax.fori_loop(part * size, (part + 1) * size, body, 0, unroll=4)
+        lax.fori_loop(part * size, (part + 1) * size, body, 0, unroll=8)
         if part == 0:
             for field in range(2):
                 held_ref[field, RDEPTH] = held_ref[field, RDEPTH] + layer_ref[2 + field]
@@ -591,7 +610,7 @@
     other = ya_in
     base = kernel(local_kernel, wave_v, 0, 3)(now, old, speed)
     for axis, step in steps:
-        partial_res = kernel(sum_kernel, tiles_of(left), 0, 5)(partial_res, keep, other, base, yb_in)
+        partial_res = kernel(sum_kernel, tiles_of(left), 0, 5)(partial_res, keep, other, base, cells)
         keep = partial_res
         other = send(partial_res, swap_along[axis](step))
     wave_middle, xa, xb, ya, yb = kernel(middle_kernel, (wave_v, face_x, face_x, face_y, face_y), 0, 6, [wave_v])(
@@ -608,7 +627,7 @@
     layers = kernel(inject_kernel, tiles_of(4), 0, 4)(keep, res_in, cells, speed)
     wave_after, wave_middle = kernel(
         after_kernel, (jax.ShapeDtypeStruct(wave, F32),) * 2, 0, 8,
-        [wave_v, wave_v, pltpu.VMEM(plane, F32), pltpu.SemaphoreType.DMA((7,))],
+        [wave_v, wave_v, pltpu.VMEM(plane, F32), pltpu.SemaphoreType.DMA((11,))],
         out_specs=(pl.BlockSpec(memory_space=pl.ANY),) * 2,
     )(base, wave_middle, speed, xa_in, xb_in, ya_in, yb_in, layers)
     return (wave_after, wave_middle)

time: 23.1 us -> 22.6 us (0.978)
  waiting for transfers between devices: 1.86 us -> 3.02 us
  Pallas kernels: 8.06 us -> 7.05 us
  starting transfers between devices: 12.3 us -> 11.5 us
    ppermute x11, waiting for transfers between devices: 1.86 us -> 3.02 us  [on_device(): send = lambda value, pairs: lax.ppermute(value, AXES, pairs)]
    pallas_call x9, Pallas kernels: 6.39 us -> 5.42 us  [call(): pl.pallas_call(functools.partial(body, counts), out_shape=outs, in_specs=...]
    ppermute x11, starting transfers between devices: 12.3 us -> 11.5 us  [on_device(): send = lambda value, pairs: lax.ppermute(value, AXES, pairs)]
  transfers between devices with their start and end apart: 11 -> 11, of which waited for: 4 -> 3; matrix products, arithmetic and copies ran while one was open for 0% -> 0% of each run, Pallas kernels for 20% -> 19%
where the time goes in v5:
time: 22.6 us; the launch traced here: 22.3 us
  starting transfers between devices  11.5 us (51%)
  Pallas kernels  7.05 us (31%)
  waiting for transfers between devices  3.02 us (13%)
  between operations  0.7 us (3%)
    ppermute x11, starting transfers between devices, on_device(): send = lambda value, pairs: lax.ppermute(value, AXES, pairs)  11.5 us
    pallas_call x9, Pallas kernels, call(): pl.pallas_call(functools.partial(body, counts), out_shape=outs, in_specs=...  5.42 us
    ppermute x11, waiting for transfers between devices, on_device(): send = lambda value, pairs: lax.ppermute(value, AXES, pairs)  3.02 us
    pallas_call x1, Pallas kernels, on_device(): pl.pallas_call(functools.partial(bring_kernel, float(span * span), counts...  1.63 us
  transfers between devices with their start and end apart: 11, of which 3 were waited for; matrix products, arithmetic and copies ran while one was open for 0% of the time, Pallas kernels for 19%

profile of v5, /device:TPU:0, one launch (start us, length us, event | category | flops | bytes accessed | tf_op | source)
XLA Modules:
  0.0 22.3 jit_solution(52028292807588000)
XLA Ops:
  0.6 1.6 %bring.1 = (f32[2,64,8,128]{3,2,1,0:T(8,128)S(1)}, f32[2,64,8,128]{3,2,1,0:T(8,128)S(1)}, f32[64,8,128]{2,1,0:T(8,128)S(1)}, s32[32,128]{1,0:T(8,128)S(1)}, f32[...) custom-call(s32[2,16]{1,0:T(2,128)} %signs_hbm.1, s32[16]{0:T(128)} %sx_hbm.1, ...), custom_call_target="tpu_custom_call" | custom-call | tf_op jit(solution)/shard_map/bring/pallas_call | solution.py:587
  2.3 0.5 %collective-permute-start = (f32[16,8,128]{2,1,0:T(8,128)S(1)}, f32[16,8,128]{2,1,0:T(8,128)S(1)}, u32[]{:S(2)}, u32[]{:S(2)}) collective-permute-start(f32[16,8,128]{2,1,0:T(8,128)S(1)} %get-tuple-element.27.own_ref), channel_id=1, source_target_pairs={{0,4},{1,5},{2,6},{3,7},{4,0},{5,1},{6,2},{7,3},{8,12},{9,13},{10,... | collective-permute-start | bytes 196616 | tf_op jit(solution)/shard_map/ppermute | solution.py:553
  2.8 2.6 %collective-permute-start.2 = (f32[64,8,128]{2,1,0:T(8,128)S(1)}, f32[64,8,128]{2,1,0:T(8,128)S(1)}, u32[]{:S(2)}, u32[]{:S(2)}) collective-permute-start(f32[64,8,128]{2,1,0:T(8,128)S(1)} %get-tuple-element.30), channel_id=1, source_target_pairs={{0,16},{1,17},{2,18},{3,19},{4,8},{5,9},{6,10},{7,11},{8,4},{9,5},... | collective-permute-start | bytes 786440 | tf_op jit(solution)/shard_map/ppermute | solution.py:553
  5.4 0.4 %pack.1 = (f32[4,8,128]{2,1,0:T(8,128)S(1)}, f32[16,8,128]{2,1,0:T(8,128)S(1)}) custom-call(f32[2,64,8,128]{3,2,1,0:T(8,128)S(1)} %get-tuple-element.23.now_ref.old_ref), custom_call_target="tpu_custom_call" | custom-call | tf_op jit(solution)/shard_map/pack/pallas_call | solution.py:566
  5.8 0.0 collective-permute-done.other_ref
  5.8 0.2 collective-permute-start.1
  6.0 1.6 %collective-permute-start.3 = (f32[14,8,128]{2,1,0:T(8,128)S(1)}, f32[14,8,128]{2,1,0:T(8,128)S(1)}, u32[]{:S(2)}, u32[]{:S(2)}) collective-permute-start(f32[14,8,128]{2,1,0:T(8,128)S(1)} %get-tuple-element.31.own_ref), channel_id=1, source_target_pairs={{0,1},{1,0},{2,3},{3,2},{4,5},{5,4},{6,7},{7,6},{8,9},{9,8},{10,11... | collective-permute-start | bytes 172040 | tf_op jit(solution)/shard_map/ppermute | solution.py:553
  7.6 0.1 collective-permute-start.4
  7.7 1.1 %local.1.base_ref.before_ref = f32[2,64,8,128]{3,2,1,0:T(8,128)S(1)} custom-call(f32[2,64,8,128]{3,2,1,0:T(8,128)S(1)} %get-tuple-element.23.now_ref.old_ref, f32[2,64,8,128]{3,2,1,0:T(8,128)S(1)} %get-tuple-element.24.old_ref, f32[64,8,128]{2,1,0:T(8,128)S(1)} %get-tuple-element.25.courant_ref), custom_call_target="tpu_custom_call" | custom-call | tf_op jit(solution)/shard_map/local/pallas_call | solution.py:566
  8.8 1.4 %collective-permute-done.3.ya_ref.other_ref = f32[14,8,128]{2,1,0:T(8,128)S(1)} collective-permute-done((f32[14,8,128]{2,1,0:T(8,128)S(1)}, f32[14,8,128]{2,1,0:T(8,128)S(1)}, u32[]{:S(2)}, u32[]{:S(2)}) %collective-permute-start.3) | collective-permute-done | bytes 57376 | tf_op jit(solution)/shard_map/ppermute | solution.py:553
  10.2 1.5 %collective-permute-start.5 = (f32[10,8,128]{2,1,0:T(8,128)S(1)}, f32[10,8,128]{2,1,0:T(8,128)S(1)}, u32[]{:S(2)}, u32[]{:S(2)}) collective-permute-start(f32[10,8,128]{2,1,0:T(8,128)S(1)} %sum.1.own_ref), channel_id=1, source_target_pairs={{0,8},{1,9},{2,10},{3,11},{4,12},{5,13},{6,14},{7,15},{8,0},{9,1},... | collective-permute-start | bytes 122888 | tf_op jit(solution)/shard_map/ppermute | solution.py:553
  11.7 0.0 collective-permute-done.4.yb_ref
  11.7 0.0 collective-permute-done.2.xb_ref
  11.7 0.0 collective-permute-done.1.xa_ref
  11.7 1.2 %middle.1 = (f32[2,64,8,128]{3,2,1,0:T(8,128)S(1)}, f32[64,8,128]{2,1,0:T(8,128)S(1)}, f32[64,8,128]{2,1,0:T(8,128)S(1)}, f32[4,8,128]{2,1,0:T(8,128)S(1)}, f32[4,8,128]{2,1,0:T(8,128)S(1)}) custom-call(f32[2,64,8,128]{3,2,1,0:T(8,128)S(1)} %local.1.base_ref.before_ref, f32[64,8,128]{2,1,0:T(8,128)S(1)} %get-tuple-element.25.courant_ref, ...), custom_call_target="tpu_custom_call" | custom-call | tf_op jit(solution)/shard_map/middle/pallas_call | solution.py:566
  12.9 0.0 collective-permute-start.6
  12.9 0.8 %collective-permute-start.7 = (f32[64,8,128]{2,1,0:T(8,128)S(1)}, f32[64,8,128]{2,1,0:T(8,128)S(1)}, u32[]{:S(2)}, u32[]{:S(2)}) collective-permute-start(f32[64,8,128]{2,1,0:T(8,128)S(1)} %get-tuple-element.40), channel_id=1, source_target_pairs={{0,16},{1,17},{2,18},{3,19},{4,8},{5,9},{6,10},{7,11},{8,4},{9,5},... | collective-permute-start | bytes 786440 | tf_op jit(solution)/shard_map/ppermute | solution.py:553
  13.8 0.4 %collective-permute-done.5.other_ref = f32[10,8,128]{2,1,0:T(8,128)S(1)} collective-permute-done((f32[10,8,128]{2,1,0:T(8,128)S(1)}, f32[10,8,128]{2,1,0:T(8,128)S(1)}, u32[]{:S(2)}, u32[]{:S(2)}) %collective-permute-start.5) | collective-permute-done | bytes 40992 | tf_op jit(solution)/shard_map/ppermute | solution.py:553
  14.2 3.1 %collective-permute-start.10 = (f32[5,8,128]{2,1,0:T(8,128)S(1)}, f32[5,8,128]{2,1,0:T(8,128)S(1)}, u32[]{:S(2)}, u32[]{:S(2)}) collective-permute-start(f32[5,8,128]{2,1,0:T(8,128)S(1)} %get-tuple-element.43), channel_id=1, source_target_pairs={{0,2},{1,3},{2,0},{3,1},{4,6},{5,7},{6,4},{7,5},{8,10},{9,11},{10,... | collective-permute-start | bytes 61448 | tf_op jit(solution)/shard_map/ppermute | solution.py:553
  17.3 1.2 %collective-permute-start.8 = (f32[4,8,128]{2,1,0:T(8,128)S(1)}, f32[4,8,128]{2,1,0:T(8,128)S(1)}, u32[]{:S(2)}, u32[]{:S(2)}) collective-permute-start(f32[4,8,128]{2,1,0:T(8,128)S(1)} %get-tuple-element.41), channel_id=1, source_target_pairs={{0,1},{1,0},{2,3},{3,2},{4,5},{5,4},{6,7},{7,6},{8,9},{9,8},{10,11... | collective-permute-start | bytes 49160 | tf_op jit(solution)/shard_map/ppermute | solution.py:553
  18.5 0.0 collective-permute-start.9
  18.5 1.1 %second_local.1.base_ref = f32[2,64,8,128]{3,2,1,0:T(8,128)S(1)} custom-call(f32[2,64,8,128]{3,2,1,0:T(8,128)S(1)} %get-tuple-element.33.before_ref.now_ref.mid_ref, f32[2,64,8,128]{3,2,1,0:T(8,128)S(1)} %get-tuple-element.23.now_ref.old_ref, f32[64,8,128]{2,1,0:T(8,128)S(1)} %get-tuple-element.25.courant_ref, ...), custom_call_target="tpu_custom_call" | custom-call | tf_op jit(solution)/shard_map/second_local/pallas_call | solution.py:566
  19.6 0.0 collective-permute-done.10.res_ref
  19.6 0.3 %inject.1.layer_ref = f32[4,8,128]{2,1,0:T(8,128)S(1)} custom-call(f32[5,8,128]{2,1,0:T(8,128)S(1)} %get-tuple-element.38.before_ref.keep_ref, f32[5,8,128]{2,1,0:T(8,128)S(1)} %collective-permute-done.10.res_ref, s32[32,128]{1,0:T(8,128)S(1)} %get-tuple-element.35.more_ref.cell_ref, f32[64,8,128]{2,1,0:T(8,128)S(1)} %get-tuple-element.25.courant_ref), custom_call_target="tpu_custom_call" | custom-call | tf_op jit(solution)/shard_map/inject/pallas_call | solution.py:566
  19.9 1.1 %collective-permute-done.8.ya_ref = f32[4,8,128]{2,1,0:T(8,128)S(1)} collective-permute-done((f32[4,8,128]{2,1,0:T(8,128)S(1)}, f32[4,8,128]{2,1,0:T(8,128)S(1)}, u32[]{:S(2)}, u32[]{:S(2)}) %collective-permute-start.8) | collective-permute-done | bytes 16416 | tf_op jit(solution)/shard_map/ppermute | solution.py:553
  21.0 0.0 collective-permute-done.9.yb_ref
  21.0 0.0 collective-permute-done.6.xa_ref
  21.0 0.0 collective-permute-done.7.xb_ref
  21.1 1.3 %after.1 = (f32[2,64,8,128]{3,2,1,0:T(8,128)}, f32[2,64,8,128]{3,2,1,0:T(8,128)}) custom-call(f32[2,64,8,128]{3,2,1,0:T(8,128)S(1)} %second_local.1.base_ref, f32[2,64,8,128]{3,2,1,0:T(8,128)S(1)} %get-tuple-element.33.before_ref.now_ref.mid_ref, f32[64,8,128]{2,1,0:T(8,128)S(1)} %get-tuple-element.25.courant_ref, ...), custom_call_target="tpu_custom_call" | custom-call | tf_op jit(solution)/shard_map/after/pallas_call | solution.py:566
  (3 shorter events, 0.1 us)
Async XLA Ops:
  2.3 3.5 %collective-permute-start = (f32[16,8,128]{2,1,0:T(8,128)S(1)}, f32[16,8,128]{2,1,0:T(8,128)S(1)}, u32[]{:S(2)}, u32[]{:S(2)}) collective-permute-start(f32[16,8,128]{2,1,0:T(8,128)S(1)} %get-tuple-element.27.own_ref), channel_id=1, source_target_pairs={{0,4},{1,5},{2,6},{3,7},{4,0},{5,1},{6,2},{7,3},{8,12},{9,13},{10,... | collective-permute-start | bytes 196616 | tf_op jit(solution)/shard_map/ppermute | solution.py:553
  2.8 8.9 %collective-permute-start.2 = (f32[64,8,128]{2,1,0:T(8,128)S(1)}, f32[64,8,128]{2,1,0:T(8,128)S(1)}, u32[]{:S(2)}, u32[]{:S(2)}) collective-permute-start(f32[64,8,128]{2,1,0:T(8,128)S(1)} %get-tuple-element.30), channel_id=1, source_target_pairs={{0,16},{1,17},{2,18},{3,19},{4,8},{5,9},{6,10},{7,11},{8,4},{9,5},... | collective-permute-start | bytes 786440 | tf_op jit(solution)/shard_map/ppermute | solution.py:553
  5.8 5.9 %collective-permute-start.1 = (f32[64,8,128]{2,1,0:T(8,128)S(1)}, f32[64,8,128]{2,1,0:T(8,128)S(1)}, u32[]{:S(2)}, u32[]{:S(2)}) collective-permute-start(f32[64,8,128]{2,1,0:T(8,128)S(1)} %get-tuple-element.29), channel_id=1, source_target_pairs={{0,4},{1,5},{2,6},{3,7},{4,0},{5,1},{6,2},{7,3},{8,12},{9,13},{10,... | collective-permute-start | bytes 786440 | tf_op jit(solution)/shard_map/ppermute | solution.py:553
  6.0 4.2 %collective-permute-start.3 = (f32[14,8,128]{2,1,0:T(8,128)S(1)}, f32[14,8,128]{2,1,0:T(8,128)S(1)}, u32[]{:S(2)}, u32[]{:S(2)}) collective-permute-start(f32[14,8,128]{2,1,0:T(8,128)S(1)} %get-tuple-element.31.own_ref), channel_id=1, source_target_pairs={{0,1},{1,0},{2,3},{3,2},{4,5},{5,4},{6,7},{7,6},{8,9},{9,8},{10,11... | collective-permute-start | bytes 172040 | tf_op jit(solution)/shard_map/ppermute | solution.py:553
  7.6 4.1 %collective-permute-start.4 = (f32[16,8,128]{2,1,0:T(8,128)S(1)}, f32[16,8,128]{2,1,0:T(8,128)S(1)}, u32[]{:S(2)}, u32[]{:S(2)}) collective-permute-start(f32[16,8,128]{2,1,0:T(8,128)S(1)} %get-tuple-element.32), channel_id=1, source_target_pairs={{0,4},{1,2},{2,1},{3,7},{4,0},{5,6},{6,5},{7,3},{8,12},{9,10},{10,... | collective-permute-start | bytes 196616 | tf_op jit(solution)/shard_map/ppermute | solution.py:553
  10.2 4.0 %collective-permute-start.5 = (f32[10,8,128]{2,1,0:T(8,128)S(1)}, f32[10,8,128]{2,1,0:T(8,128)S(1)}, u32[]{:S(2)}, u32[]{:S(2)}) collective-permute-start(f32[10,8,128]{2,1,0:T(8,128)S(1)} %sum.1.own_ref), channel_id=1, source_target_pairs={{0,8},{1,9},{2,10},{3,11},{4,12},{5,13},{6,14},{7,15},{8,0},{9,1},... | collective-permute-start | bytes 122888 | tf_op jit(solution)/shard_map/ppermute | solution.py:553
  12.9 8.1 %collective-permute-start.6 = (f32[64,8,128]{2,1,0:T(8,128)S(1)}, f32[64,8,128]{2,1,0:T(8,128)S(1)}, u32[]{:S(2)}, u32[]{:S(2)}) collective-permute-start(f32[64,8,128]{2,1,0:T(8,128)S(1)} %get-tuple-element.39), channel_id=1, source_target_pairs={{0,4},{1,5},{2,6},{3,7},{4,0},{5,1},{6,2},{7,3},{8,12},{9,13},{10,... | collective-permute-start | bytes 786440 | tf_op jit(solution)/shard_map/ppermute | solution.py:553
  12.9 8.1 %collective-permute-start.7 = (f32[64,8,128]{2,1,0:T(8,128)S(1)}, f32[64,8,128]{2,1,0:T(8,128)S(1)}, u32[]{:S(2)}, u32[]{:S(2)}) collective-permute-start(f32[64,8,128]{2,1,0:T(8,128)S(1)} %get-tuple-element.40), channel_id=1, source_target_pairs={{0,16},{1,17},{2,18},{3,19},{4,8},{5,9},{6,10},{7,11},{8,4},{9,5},... | collective-permute-start | bytes 786440 | tf_op jit(solution)/shard_map/ppermute | solution.py:553
  14.2 5.3 %collective-permute-start.10 = (f32[5,8,128]{2,1,0:T(8,128)S(1)}, f32[5,8,128]{2,1,0:T(8,128)S(1)}, u32[]{:S(2)}, u32[]{:S(2)}) collective-permute-start(f32[5,8,128]{2,1,0:T(8,128)S(1)} %get-tuple-element.43), channel_id=1, source_target_pairs={{0,2},{1,3},{2,0},{3,1},{4,6},{5,7},{6,4},{7,5},{8,10},{9,11},{10,... | collective-permute-start | bytes 61448 | tf_op jit(solution)/shard_map/ppermute | solution.py:553
  17.3 3.7 %collective-permute-start.8 = (f32[4,8,128]{2,1,0:T(8,128)S(1)}, f32[4,8,128]{2,1,0:T(8,128)S(1)}, u32[]{:S(2)}, u32[]{:S(2)}) collective-permute-start(f32[4,8,128]{2,1,0:T(8,128)S(1)} %get-tuple-element.41), channel_id=1, source_target_pairs={{0,1},{1,0},{2,3},{3,2},{4,5},{5,4},{6,7},{7,6},{8,9},{9,8},{10,11... | collective-permute-start | bytes 49160 | tf_op jit(solution)/shard_map/ppermute | solution.py:553
  18.5 2.6 %collective-permute-start.9 = (f32[4,8,128]{2,1,0:T(8,128)S(1)}, f32[4,8,128]{2,1,0:T(8,128)S(1)}, u32[]{:S(2)}, u32[]{:S(2)}) collective-permute-start(f32[4,8,128]{2,1,0:T(8,128)S(1)} %get-tuple-element.42), channel_id=1, source_target_pairs={{0,4},{1,2},{2,1},{3,7},{4,0},{5,6},{6,5},{7,3},{8,12},{9,10},{10,... | collective-permute-start | bytes 49160 | tf_op jit(solution)/shard_map/ppermute | solution.py:553

commit v6 on v5

--- a/solution.py
+++ b/solution.py
@@ -234,7 +234,7 @@
         body(depth, depth)
 
 
-def residual(counts, cells_x, cells_y, radius_sq, signs_ref, sx_ref, sy_ref, records_ref, cell_ref, out_ref):
+def residual(counts, cells_x, cells_y, radius_sq, signs_ref, sx_ref, sy_ref, records_ref, cell_ref, out_ref, first):
     shots, rows, _ = records_ref.shape
     chunk = min(rows, 64)
     per = 2 * REC_DEV // LANES
@@ -263,7 +263,7 @@
         sums = lax.fori_loop(0, shots, shot_step, (jnp.zeros((chunk, LANES), F32),) * 2, unroll=2)
         for t in range(chunk // per):
             both = [s[t * per : (t + 1) * per] for s in sums]
-            out_ref[c * (chunk // per) + t] = jnp.concatenate(both, axis=0)
+            out_ref[first + c * (chunk // per) + t] = jnp.concatenate(both, axis=0)
         return carry
 
     lax.fori_loop(0, rows // chunk, chunk_step, 0)
@@ -271,7 +271,7 @@
 
 def bring_kernel(
     radius_sq, counts, signs_hbm, sx_hbm, sy_hbm, records_hbm, cell_hbm, now_hbm, old_hbm, courant_hbm,
-    now_ref, old_ref, courant_ref, cell_ref, res_ref, xa_ref, xb_ref, records_ref, signs_ref, sx_ref, sy_ref, sems,
+    now_ref, old_ref, courant_ref, cell_ref, xa_ref, xb_ref, records_ref, signs_ref, sx_ref, sy_ref, sems,
 ):
     copies = []
 
@@ -288,7 +288,7 @@
     for copy in copies[:5]:
         copy.wait()
     _, deep, cells_x, cells_y = now_ref.shape
-    residual(counts, cells_x, cells_y, radius_sq, signs_ref, sx_ref, sy_ref, records_ref, cell_ref, res_ref)
+    residual(counts, cells_x, cells_y, radius_sq, signs_ref, sx_ref, sy_ref, records_ref, cell_ref, xa_ref, deep)
     copies[5].wait()
     odd = where_am_i(counts)[0]
 
@@ -362,11 +362,11 @@
     )
 
 
-def join_kernel(counts, face_ref, own_ref, other_ref, xa_ref, out_ref, keep_ref, xa_out):
-    del xa_ref, xa_out
+def join_kernel(counts, face_ref, own_ref, other_ref, out_ref, keep_ref):
     faces, at = face_ref.shape[0], own_ref.shape[0] - counts[0] * counts[1]
+    at_other = other_ref.shape[0] - counts[0] * counts[1]
     out_ref[:faces] = face_ref[...]
-    total = lambda x, y: own_ref[at + x * counts[1] + y] + other_ref[at + x * counts[1] + y]
+    total = lambda x, y: own_ref[at + x * counts[1] + y] + other_ref[at_other + x * counts[1] + y]
     here = faces
     for high in range(0, counts[0], 4):
         for x in range(high, high + 2):
@@ -583,15 +583,14 @@
     record_rows = record_rows.reshape(shots, 2 * total_recv // LANES, LANES)
     far = lambda value: pltpu.with_memory_space_constraint(value, pltpu.HBM)
     left = sum(packed_sizes(counts))
-    pad = left + 2
-    now, old, speed, cells, partial_res, xa, xb = pl.pallas_call(
+    now, old, speed, cells, xa, xb = pl.pallas_call(
         functools.partial(bring_kernel, float(span * span), counts),
         out_shape=(
-            wave_v, wave_v, pltpu.VMEM(courant.shape, F32), pltpu.VMEM(cell_rows.shape, jnp.int32), tiles_of(tiles),
-            face_x, face_x,
+            wave_v, wave_v, pltpu.VMEM(courant.shape, F32), pltpu.VMEM(cell_rows.shape, jnp.int32),
+            tiles_of(deep + tiles), face_x,
         ),
         in_specs=[pl.BlockSpec(memory_space=pltpu.HBM)] * 8,
-        out_specs=(VM,) * 7,
+        out_specs=(VM,) * 6,
         scratch_shapes=[
             pltpu.VMEM(record_rows.shape, BF16),
             pltpu.SMEM(signs.shape, jnp.int32), pltpu.SMEM((shots,), jnp.int32), pltpu.SMEM((shots,), jnp.int32),
@@ -600,20 +599,20 @@
         compiler_params=PARAMS,
         name="bring",
     )(*(far(a) for a in (signs, source_x, source_y, record_rows, cell_rows, wave_now, wave_before, courant)))
-    xb_in, other = send(xb, swap_xb), send(partial_res, swap_xa)
-    ya, yb = kernel(pack_kernel, (face_y, tiles_of(faces + pad)), 0, 1)(now)
+    xb_in, xa_in = send(xb, swap_xb), send(xa, swap_xa)
+    ya, yb = kernel(pack_kernel, (face_y, face_y), 0, 1)(now)
     yb_in = send(yb, swap_yb)
-    partial_res, keep, xa = kernel(
-        join_kernel, (tiles_of(faces + left), tiles_of(packed_sizes(counts)[1]), face_x), 0, 4, aliases={3: 2},
-    )(ya, partial_res, other, xa)
-    ya_in, xa_in = send(partial_res, swap_ya), send(xa, swap_xa)
+    partial_res, keep = kernel(join_kernel, (tiles_of(faces + left), tiles_of(packed_sizes(counts)[1])), 0, 3)(
+        ya, xa, xa_in
+    )
+    ya_in = send(partial_res, swap_ya)
     other = ya_in
     base = kernel(local_kernel, wave_v, 0, 3)(now, old, speed)
     for axis, step in steps:
         partial_res = kernel(sum_kernel, tiles_of(left), 0, 5)(partial_res, keep, other, base, cells)
         keep = partial_res
         other = send(partial_res, swap_along[axis](step))
-    wave_middle, xa, xb, ya, yb = kernel(middle_kernel, (wave_v, face_x, face_x, face_y, face_y), 0, 6, [wave_v])(
+    wave_middle, xa, xb, ya, yb = kernel(middle_kernel, (wave_v, face_x, face_x, face_y, face_y), 0, 6, [wave_v], cost=pl.CostEstimate(flops=10*10**8, bytes_accessed=0, transcendentals=0))(
         base, speed, xa_in, xb_in, ya_in, yb_in
     )
     wanted, keep, ya, yb = kernel(

time: 22.6 us -> 22 us (0.973)
  waiting for transfers between devices: 3.02 us -> 2.32 us
    ppermute x11 -> x10, waiting for transfers between devices: 3.02 us -> 2.32 us  [on_device(): send = lambda value, pairs: lax.ppermute(value, AXES, pairs)]
    ppermute x11 -> x10, starting transfers between devices: 11.5 us -> 11.7 us  [on_device(): send = lambda value, pairs: lax.ppermute(value, AXES, pairs)]
  transfers between devices with their start and end apart: 11 -> 10, of which waited for: 3 -> 3; matrix products, arithmetic and copies ran while one was open for 0% -> 0% of each run, Pallas kernels for 19% -> 19%
where the time goes in v6:
time: 22 us; the launch traced here: 21.8 us
  starting transfers between devices  11.7 us (53%)
  Pallas kernels  7.05 us (32%)
  waiting for transfers between devices  2.32 us (11%)
  between operations  0.7 us (3%)
    ppermute x10, starting transfers between devices, on_device(): send = lambda value, pairs: lax.ppermute(value, AXES, pairs)  11.7 us
    pallas_call x9, Pallas kernels, call(): pl.pallas_call(functools.partial(body, counts), out_shape=outs, in_specs=...  5.42 us
    ppermute x10, waiting for transfers between devices, on_device(): send = lambda value, pairs: lax.ppermute(value, AXES, pairs)  2.32 us
    pallas_call x1, Pallas kernels, on_device(): pl.pallas_call(functools.partial(bring_kernel, float(span * span), counts...  1.63 us
  transfers between devices with their start and end apart: 10, of which 3 were waited for; matrix products, arithmetic and copies ran while one was open for 0% of the time, Pallas kernels for 19%

profile of v6, /device:TPU:0, one launch (start us, length us, event | category | flops | bytes accessed | tf_op | source)
XLA Modules:
  0.0 21.8 jit_solution(9678495876025202600)
XLA Ops:
  0.6 1.6 %bring.1 = (f32[2,64,8,128]{3,2,1,0:T(8,128)S(1)}, f32[2,64,8,128]{3,2,1,0:T(8,128)S(1)}, f32[64,8,128]{2,1,0:T(8,128)S(1)}, s32[32,128]{1,0:T(8,128)S(1)}, f32[...) custom-call(s32[2,16]{1,0:T(2,128)} %signs_hbm.1, s32[16]{0:T(128)} %sx_hbm.1, s32[16]{0:T(128)} %sy_hbm.1, ...), custom_call_target="tpu_custom_call" | custom-call | tf_op jit(solution)/shard_map/bring/pallas_call | solution.py:586
  2.3 0.5 %collective-permute-start = (f32[80,8,128]{2,1,0:T(8,128)S(1)}, f32[80,8,128]{2,1,0:T(8,128)S(1)}, u32[]{:S(2)}, u32[]{:S(2)}) collective-permute-start(f32[80,8,128]{2,1,0:T(8,128)S(1)} %get-tuple-element.24.own_ref), channel_id=1, source_target_pairs={{0,4},{1,5},{2,6},{3,7},{4,0},{5,1},{6,2},{7,3},{8,12},{9,13},{10,... | collective-permute-start | bytes 983048 | tf_op jit(solution)/shard_map/ppermute | solution.py:553
  2.8 2.6 %collective-permute-start.1 = (f32[64,8,128]{2,1,0:T(8,128)S(1)}, f32[64,8,128]{2,1,0:T(8,128)S(1)}, u32[]{:S(2)}, u32[]{:S(2)}) collective-permute-start(f32[64,8,128]{2,1,0:T(8,128)S(1)} %get-tuple-element.25), channel_id=1, source_target_pairs={{0,16},{1,17},{2,18},{3,19},{4,8},{5,9},{6,10},{7,11},{8,4},{9,5},... | collective-permute-start | bytes 786440 | tf_op jit(solution)/shard_map/ppermute | solution.py:553
  5.4 0.4 %pack.1 = (f32[4,8,128]{2,1,0:T(8,128)S(1)}, f32[4,8,128]{2,1,0:T(8,128)S(1)}) custom-call(f32[2,64,8,128]{3,2,1,0:T(8,128)S(1)} %get-tuple-element.21.now_ref.old_ref), custom_call_target="tpu_custom_call" | custom-call | tf_op jit(solution)/shard_map/pack/pallas_call | solution.py:566
  5.8 0.0 collective-permute-done.other_ref.xa_ref
  5.8 1.6 %collective-permute-start.2 = (f32[14,8,128]{2,1,0:T(8,128)S(1)}, f32[14,8,128]{2,1,0:T(8,128)S(1)}, u32[]{:S(2)}, u32[]{:S(2)}) collective-permute-start(f32[14,8,128]{2,1,0:T(8,128)S(1)} %get-tuple-element.27.own_ref), channel_id=1, source_target_pairs={{0,1},{1,0},{2,3},{3,2},{4,5},{5,4},{6,7},{7,6},{8,9},{9,8},{10,11... | collective-permute-start | bytes 172040 | tf_op jit(solution)/shard_map/ppermute | solution.py:553
  7.4 0.0 collective-permute-start.3
  7.4 1.1 %local.1.base_ref.before_ref = f32[2,64,8,128]{3,2,1,0:T(8,128)S(1)} custom-call(f32[2,64,8,128]{3,2,1,0:T(8,128)S(1)} %get-tuple-element.21.now_ref.old_ref, f32[2,64,8,128]{3,2,1,0:T(8,128)S(1)} %get-tuple-element.22.old_ref, f32[64,8,128]{2,1,0:T(8,128)S(1)} %get-tuple-element.23.courant_ref), custom_call_target="tpu_custom_call" | custom-call | tf_op jit(solution)/shard_map/local/pallas_call | solution.py:566
  8.5 1.5 %collective-permute-done.2.ya_ref.other_ref = f32[14,8,128]{2,1,0:T(8,128)S(1)} collective-permute-done((f32[14,8,128]{2,1,0:T(8,128)S(1)}, f32[14,8,128]{2,1,0:T(8,128)S(1)}, u32[]{:S(2)}, u32[]{:S(2)}) %collective-permute-start.2) | collective-permute-done | bytes 57376 | tf_op jit(solution)/shard_map/ppermute | solution.py:553
  10.0 1.3 %collective-permute-start.4 = (f32[10,8,128]{2,1,0:T(8,128)S(1)}, f32[10,8,128]{2,1,0:T(8,128)S(1)}, u32[]{:S(2)}, u32[]{:S(2)}) collective-permute-start(f32[10,8,128]{2,1,0:T(8,128)S(1)} %sum.1.own_ref), channel_id=1, source_target_pairs={{0,8},{1,9},{2,10},{3,11},{4,12},{5,13},{6,14},{7,15},{8,0},{9,1},... | collective-permute-start | bytes 122888 | tf_op jit(solution)/shard_map/ppermute | solution.py:553
  11.4 0.0 collective-permute-done.3.yb_ref
  11.4 0.0 collective-permute-done.1.xb_ref
  11.4 1.2 %middle.1 = (f32[2,64,8,128]{3,2,1,0:T(8,128)S(1)}, f32[64,8,128]{2,1,0:T(8,128)S(1)}, f32[64,8,128]{2,1,0:T(8,128)S(1)}, f32[4,8,128]{2,1,0:T(8,128)S(1)}, f32[4,8,128]{2,1,0:T(8,128)S(1)}) custom-call(f32[2,64,8,128]{3,2,1,0:T(8,128)S(1)} %local.1.base_ref.before_ref, f32[64,8,128]{2,1,0:T(8,128)S(1)} %get-tuple-element.23.courant_ref, ...), custom_call_target="tpu_custom_call" | custom-call | flops 1000000000 | tf_op jit(solution)/shard_map/middle/pallas_call | solution.py:566
  12.6 0.0 collective-permute-start.5
  12.6 1.4 %collective-permute-start.6 = (f32[64,8,128]{2,1,0:T(8,128)S(1)}, f32[64,8,128]{2,1,0:T(8,128)S(1)}, u32[]{:S(2)}, u32[]{:S(2)}) collective-permute-start(f32[64,8,128]{2,1,0:T(8,128)S(1)} %get-tuple-element.36), channel_id=1, source_target_pairs={{0,16},{1,17},{2,18},{3,19},{4,8},{5,9},{6,10},{7,11},{8,4},{9,5},... | collective-permute-start | bytes 786440 | tf_op jit(solution)/shard_map/ppermute | solution.py:553
  14.0 0.1 collective-permute-done.4.other_ref
  14.1 2.7 %collective-permute-start.9 = (f32[5,8,128]{2,1,0:T(8,128)S(1)}, f32[5,8,128]{2,1,0:T(8,128)S(1)}, u32[]{:S(2)}, u32[]{:S(2)}) collective-permute-start(f32[5,8,128]{2,1,0:T(8,128)S(1)} %get-tuple-element.39), channel_id=1, source_target_pairs={{0,2},{1,3},{2,0},{3,1},{4,6},{5,7},{6,4},{7,5},{8,10},{9,11},{10,... | collective-permute-start | bytes 61448 | tf_op jit(solution)/shard_map/ppermute | solution.py:553
  16.7 1.6 %collective-permute-start.7 = (f32[4,8,128]{2,1,0:T(8,128)S(1)}, f32[4,8,128]{2,1,0:T(8,128)S(1)}, u32[]{:S(2)}, u32[]{:S(2)}) collective-permute-start(f32[4,8,128]{2,1,0:T(8,128)S(1)} %get-tuple-element.37), channel_id=1, source_target_pairs={{0,1},{1,0},{2,3},{3,2},{4,5},{5,4},{6,7},{7,6},{8,9},{9,8},{10,11... | collective-permute-start | bytes 49160 | tf_op jit(solution)/shard_map/ppermute | solution.py:553
  18.3 0.0 collective-permute-start.8
  18.3 1.1 %second_local.1.base_ref = f32[2,64,8,128]{3,2,1,0:T(8,128)S(1)} custom-call(f32[2,64,8,128]{3,2,1,0:T(8,128)S(1)} %get-tuple-element.29.before_ref.now_ref.mid_ref, f32[2,64,8,128]{3,2,1,0:T(8,128)S(1)} %get-tuple-element.21.now_ref.old_ref, f32[64,8,128]{2,1,0:T(8,128)S(1)} %get-tuple-element.23.courant_ref, ...), custom_call_target="tpu_custom_call" | custom-call | tf_op jit(solution)/shard_map/second_local/pallas_call | solution.py:566
  19.4 0.0 collective-permute-done.9.res_ref
  19.4 0.3 %inject.1.layer_ref = f32[4,8,128]{2,1,0:T(8,128)S(1)} custom-call(f32[5,8,128]{2,1,0:T(8,128)S(1)} %get-tuple-element.34.before_ref.keep_ref, f32[5,8,128]{2,1,0:T(8,128)S(1)} %collective-permute-done.9.res_ref, s32[32,128]{1,0:T(8,128)S(1)} %get-tuple-element.31.more_ref.cell_ref, f32[64,8,128]{2,1,0:T(8,128)S(1)} %get-tuple-element.23.courant_ref), custom_call_target="tpu_custom_call" | custom-call | tf_op jit(solution)/shard_map/inject/pallas_call | solution.py:566
  19.8 0.7 %collective-permute-done.7.ya_ref = f32[4,8,128]{2,1,0:T(8,128)S(1)} collective-permute-done((f32[4,8,128]{2,1,0:T(8,128)S(1)}, f32[4,8,128]{2,1,0:T(8,128)S(1)}, u32[]{:S(2)}, u32[]{:S(2)}) %collective-permute-start.7) | collective-permute-done | bytes 16416 | tf_op jit(solution)/shard_map/ppermute | solution.py:553
  20.5 0.0 collective-permute-done.8.yb_ref
  20.5 0.0 collective-permute-done.5.xa_ref
  20.5 0.0 collective-permute-done.6.xb_ref
  20.5 1.3 %after.1 = (f32[2,64,8,128]{3,2,1,0:T(8,128)}, f32[2,64,8,128]{3,2,1,0:T(8,128)}) custom-call(f32[2,64,8,128]{3,2,1,0:T(8,128)S(1)} %second_local.1.base_ref, f32[2,64,8,128]{3,2,1,0:T(8,128)S(1)} %get-tuple-element.29.before_ref.now_ref.mid_ref, f32[64,8,128]{2,1,0:T(8,128)S(1)} %get-tuple-element.23.courant_ref, ...), custom_call_target="tpu_custom_call" | custom-call | tf_op jit(solution)/shard_map/after/pallas_call | solution.py:566
  (3 shorter events, 0.1 us)
Async XLA Ops:
  2.3 3.5 %collective-permute-start = (f32[80,8,128]{2,1,0:T(8,128)S(1)}, f32[80,8,128]{2,1,0:T(8,128)S(1)}, u32[]{:S(2)}, u32[]{:S(2)}) collective-permute-start(f32[80,8,128]{2,1,0:T(8,128)S(1)} %get-tuple-element.24.own_ref), channel_id=1, source_target_pairs={{0,4},{1,5},{2,6},{3,7},{4,0},{5,1},{6,2},{7,3},{8,12},{9,13},{10,... | collective-permute-start | bytes 983048 | tf_op jit(solution)/shard_map/ppermute | solution.py:553
  2.8 8.6 %collective-permute-start.1 = (f32[64,8,128]{2,1,0:T(8,128)S(1)}, f32[64,8,128]{2,1,0:T(8,128)S(1)}, u32[]{:S(2)}, u32[]{:S(2)}) collective-permute-start(f32[64,8,128]{2,1,0:T(8,128)S(1)} %get-tuple-element.25), channel_id=1, source_target_pairs={{0,16},{1,17},{2,18},{3,19},{4,8},{5,9},{6,10},{7,11},{8,4},{9,5},... | collective-permute-start | bytes 786440 | tf_op jit(solution)/shard_map/ppermute | solution.py:553
  5.8 4.2 %collective-permute-start.2 = (f32[14,8,128]{2,1,0:T(8,128)S(1)}, f32[14,8,128]{2,1,0:T(8,128)S(1)}, u32[]{:S(2)}, u32[]{:S(2)}) collective-permute-start(f32[14,8,128]{2,1,0:T(8,128)S(1)} %get-tuple-element.27.own_ref), channel_id=1, source_target_pairs={{0,1},{1,0},{2,3},{3,2},{4,5},{5,4},{6,7},{7,6},{8,9},{9,8},{10,11... | collective-permute-start | bytes 172040 | tf_op jit(solution)/shard_map/ppermute | solution.py:553
  7.4 3.9 %collective-permute-start.3 = (f32[4,8,128]{2,1,0:T(8,128)S(1)}, f32[4,8,128]{2,1,0:T(8,128)S(1)}, u32[]{:S(2)}, u32[]{:S(2)}) collective-permute-start(f32[4,8,128]{2,1,0:T(8,128)S(1)} %get-tuple-element.28), channel_id=1, source_target_pairs={{0,4},{1,2},{2,1},{3,7},{4,0},{5,6},{6,5},{7,3},{8,12},{9,10},{10,... | collective-permute-start | bytes 49160 | tf_op jit(solution)/shard_map/ppermute | solution.py:553
  10.0 4.0 %collective-permute-start.4 = (f32[10,8,128]{2,1,0:T(8,128)S(1)}, f32[10,8,128]{2,1,0:T(8,128)S(1)}, u32[]{:S(2)}, u32[]{:S(2)}) collective-permute-start(f32[10,8,128]{2,1,0:T(8,128)S(1)} %sum.1.own_ref), channel_id=1, source_target_pairs={{0,8},{1,9},{2,10},{3,11},{4,12},{5,13},{6,14},{7,15},{8,0},{9,1},... | collective-permute-start | bytes 122888 | tf_op jit(solution)/shard_map/ppermute | solution.py:553
  12.6 7.9 %collective-permute-start.5 = (f32[64,8,128]{2,1,0:T(8,128)S(1)}, f32[64,8,128]{2,1,0:T(8,128)S(1)}, u32[]{:S(2)}, u32[]{:S(2)}) collective-permute-start(f32[64,8,128]{2,1,0:T(8,128)S(1)} %get-tuple-element.35), channel_id=1, source_target_pairs={{0,4},{1,5},{2,6},{3,7},{4,0},{5,1},{6,2},{7,3},{8,12},{9,13},{10,... | collective-permute-start | bytes 786440 | tf_op jit(solution)/shard_map/ppermute | solution.py:553
  12.6 7.9 %collective-permute-start.6 = (f32[64,8,128]{2,1,0:T(8,128)S(1)}, f32[64,8,128]{2,1,0:T(8,128)S(1)}, u32[]{:S(2)}, u32[]{:S(2)}) collective-permute-start(f32[64,8,128]{2,1,0:T(8,128)S(1)} %get-tuple-element.36), channel_id=1, source_target_pairs={{0,16},{1,17},{2,18},{3,19},{4,8},{5,9},{6,10},{7,11},{8,4},{9,5},... | collective-permute-start | bytes 786440 | tf_op jit(solution)/shard_map/ppermute | solution.py:553
  14.1 5.3 %collective-permute-start.9 = (f32[5,8,128]{2,1,0:T(8,128)S(1)}, f32[5,8,128]{2,1,0:T(8,128)S(1)}, u32[]{:S(2)}, u32[]{:S(2)}) collective-permute-start(f32[5,8,128]{2,1,0:T(8,128)S(1)} %get-tuple-element.39), channel_id=1, source_target_pairs={{0,2},{1,3},{2,0},{3,1},{4,6},{5,7},{6,4},{7,5},{8,10},{9,11},{10,... | collective-permute-start | bytes 61448 | tf_op jit(solution)/shard_map/ppermute | solution.py:553
  16.7 3.7 %collective-permute-start.7 = (f32[4,8,128]{2,1,0:T(8,128)S(1)}, f32[4,8,128]{2,1,0:T(8,128)S(1)}, u32[]{:S(2)}, u32[]{:S(2)}) collective-permute-start(f32[4,8,128]{2,1,0:T(8,128)S(1)} %get-tuple-element.37), channel_id=1, source_target_pairs={{0,1},{1,0},{2,3},{3,2},{4,5},{5,4},{6,7},{7,6},{8,9},{9,8},{10,11... | collective-permute-start | bytes 49160 | tf_op jit(solution)/shard_map/ppermute | solution.py:553
  18.3 2.2 %collective-permute-start.8 = (f32[4,8,128]{2,1,0:T(8,128)S(1)}, f32[4,8,128]{2,1,0:T(8,128)S(1)}, u32[]{:S(2)}, u32[]{:S(2)}) collective-permute-start(f32[4,8,128]{2,1,0:T(8,128)S(1)} %get-tuple-element.38), channel_id=1, source_target_pairs={{0,4},{1,2},{2,1},{3,7},{4,0},{5,6},{6,5},{7,3},{8,12},{9,10},{10,... | collective-permute-start | bytes 49160 | tf_op jit(solution)/shard_map/ppermute | solution.py:553

commit v7 on v6

--- a/solution.py
+++ b/solution.py
@@ -260,7 +260,7 @@
             taped = records_ref[shot, pl.ds(start, chunk), :].astype(F32) * (dist * inverse)
             return tuple(s + signs_ref[code, shot].astype(F32) * taped for code, s in enumerate(sums))
 
-        sums = lax.fori_loop(0, shots, shot_step, (jnp.zeros((chunk, LANES), F32),) * 2, unroll=2)
+        sums = lax.fori_loop(0, shots, shot_step, (jnp.zeros((chunk, LANES), F32),) * 2, unroll=8)
         for t in range(chunk // per):
             both = [s[t * per : (t + 1) * per] for s in sums]
             out_ref[first + c * (chunk // per) + t] = jnp.concatenate(both, axis=0)
@@ -350,8 +350,9 @@
     local_step(now_ref, old_ref, courant_ref, out_ref)
 
 
-def packed_sizes(counts):
-    return counts[0] * counts[1] // 2, counts[0] * counts[1] // 8
+def block_parts(counts, block):
+    pairs, own = counts[0] // 2, counts[0] // 4
+    return pairs, own, block * pairs, block * pairs + 2 * own, block * pairs + 2 * own + block * own
 
 
 def pack_samples(first, second):
@@ -362,56 +363,92 @@
     )
 
 
-def join_kernel(counts, face_ref, own_ref, other_ref, out_ref, keep_ref):
-    faces, at = face_ref.shape[0], own_ref.shape[0] - counts[0] * counts[1]
-    at_other = other_ref.shape[0] - counts[0] * counts[1]
-    out_ref[:faces] = face_ref[...]
+def outside(counts, start, block):
+    return jnp.minimum(start + block, counts[1] - 1), jnp.maximum(start - 1, 0)
+
+
+def partner_block(at_y, half):
+    mine = lax.div(at_y, half) * half
+    return mine, lax.div(at_y, 2 * half) * (4 * half) + half - mine
+
+
+def join_kernel(counts, own_ref, other_ref, before_ref, out_ref, keep_ref):
+    del before_ref
+    at_x, at_y = lax.axis_index("gx"), lax.axis_index("gy")
+    at, at_other = [ref.shape[0] - counts[0] * counts[1] for ref in (own_ref, other_ref)]
+    half = counts[1] // 2
+    pairs, own, at_outside, at_second, _ = block_parts(counts, half)
     total = lambda x, y: own_ref[at + x * counts[1] + y] + other_ref[at_other + x * counts[1] + y]
-    here = faces
-    for high in range(0, counts[0], 4):
-        for x in range(high, high + 2):
-            for y in range(counts[1]):
-                out_ref[here] = pack_samples(total(x, y), total(x + 2, y))[0]
-                here += 1
-    odd_x, odd_y = [lax.rem(lax.axis_index(axis), 2) for axis in AXES[1:]]
-    i = 0
-    for high in range(0, counts[0], 4):
-        for y in range(0, counts[1], 2):
-            x = high + odd_x
-            out_ref[here + i] = pack_samples(total(x, y + 1 - odd_y), total(x + 2, y + 1 - odd_y))[1]
-            keep_ref[i] = pack_samples(total(x, y + odd_y), total(x + 2, y + odd_y))[1]
-            i += 1
-
-
-def sum_kernel(counts, own_ref, keep_ref, other_ref, before_ref, more_ref, out_ref):
-    del before_ref, more_ref
-    firsts, seconds = packed_sizes(counts)
-    at, at_other = [ref.shape[0] - firsts - seconds for ref in (own_ref, other_ref)]
-    out_ref[:firsts] = own_ref[pl.ds(at, firsts)] + other_ref[pl.ds(at_other, firsts)]
-    at_keep = keep_ref.shape[0] - seconds
-    out_ref[firsts:] = keep_ref[pl.ds(at_keep, seconds)] + other_ref[pl.ds(at_other + firsts, seconds)]
-
-
-def needed_kernel(counts, own_ref, other_ref, before_ref, ya_ref, yb_ref, out_ref, keep_ref, *handed_on):
-    del before_ref, ya_ref, yb_ref, handed_on
-    firsts, _ = packed_sizes(counts)
+    row = lambda m: 4 * m + lax.rem(at_x, 2)
+    mine, partner = partner_block(at_y, half)
+    for ref, start in ((keep_ref, mine), (out_ref, partner)):
+        for i in range(half):
+            for j in range(pairs):
+                x = j // 2 * 4 + j % 2
+                ref[i * pairs + j] = pack_samples(total(x, start + i), total(x + 2, start + i))[0]
+            for m in range(own):
+                ref[at_second + i * own + m] = pack_samples(total(row(m), start + i), total(row(m) + 2, start + i))[1]
+        for side, y in enumerate(outside(counts, start, half)):
+            for m in range(own):
+                ref[at_outside + side * own + m] = pack_samples(total(row(m), y), total(row(m) + 2, y))[0]
+
+
+def fold_kernel(block, counts, own_ref, other_ref, out_ref, keep_ref):
     at_x, at_y = lax.axis_index("gx"), lax.axis_index("gy")
-    half = counts[1] // 2
+    half = block // 2
+    pairs, own, at_outside, at_second, _ = block_parts(counts, block)
+    _, _, new_outside, new_second, _ = block_parts(counts, half)
+    total = lambda i: own_ref[i] + other_ref[i]
+    first = lax.div(at_y, block) * block
+    mine, partner = partner_block(at_y, half)
+    for ref, start in ((keep_ref, mine), (out_ref, partner)):
+        for i in range(half):
+            for j in range(pairs):
+                ref[i * pairs + j] = total((start - first + i) * pairs + j)
+            for m in range(own):
+                ref[new_second + i * own + m] = total(at_second + (start - first + i) * own + m)
+        for side, y in enumerate(outside(counts, start, half)):
+            for m in range(own):
+                inside = (y - first) * pairs + 2 * m + lax.rem(at_x, 2)
+                after, before = at_outside + m, at_outside + own + m
+                ref[new_outside + side * own + m] = total(
+                    jnp.where(y < first, before, jnp.where(y >= first + block, after, inside))
+                )
+
+
+def sum_kernel(counts, own_ref, other_ref, before_ref, out_ref):
+    del before_ref
+    out_ref[...] = own_ref[...] + other_ref[...]
+
+
+def needed_kernel(counts, own_ref, other_ref, before_ref, ya_ref, yb_ref, out_ref, keep_ref, yb_out):
+    del before_ref, yb_ref, yb_out
+    at_x, at_y = lax.axis_index("gx"), lax.axis_index("gy")
+    pairs, own, at_outside, at_second, _ = block_parts(counts, 2)
     even = rows_of((SUB, LANES)) % 2 == 0
     total = lambda i: own_ref[i] + other_ref[i]
-
-    def collect(target_ref, y_here):
-        for i, (x, y) in enumerate(needed_tiles(counts, at_x, y_here)):
-            second_of_pair = lax.rem(lax.div(x, 2), 2) == 1
-            got = total((lax.div(x, 4) * 2 + lax.rem(x, 2)) * counts[1] + y)
-            got = jnp.where(second_of_pair, pltpu.roll(got, SUB - 1, 0), got)
-            if i == 0:
-                more = total(firsts + lax.div(x, 4) * half + lax.div(y, 2))
-                got = jnp.where(even, got, jnp.where(second_of_pair, more, pltpu.roll(more, 1, 0)))
-            target_ref[i] = got
-
-    collect(out_ref, lax.rem(at_y + half, counts[1]))
-    collect(keep_ref, at_y)
+    is_second = lambda x: lax.rem(lax.div(x, 2), 2) == 1
+    pick_first = lambda got, x: jnp.where(is_second(x), pltpu.roll(got, SUB - 1, 0), got)
+    faces = ya_ref.shape[0]
+    out_ref[:faces] = ya_ref[...]
+
+    def inside(x, column):
+        return pick_first(total(column * pairs + lax.div(x, 4) * 2 + lax.rem(x, 2)), x)
+
+    def collect(target_ref, first, column):
+        more = total(at_second + column * own + lax.div(at_x, 4))
+        more = jnp.where(is_second(at_x), more, pltpu.roll(more, 1, 0))
+        target_ref[first] = jnp.where(even, inside(at_x, column), more)
+        beside = inside(jnp.minimum(at_x + 1, counts[0] - 1), column), inside(jnp.maximum(at_x - 1, 0), column)
+        target_ref[first + 1] = jnp.where(even, beside[0], pltpu.roll(beside[1], 1, 0))
+        after, before = [pick_first(total(at_outside + side * own + lax.div(at_x, 4)), at_x) for side in range(2)]
+        after = jnp.where(column == 0, inside(at_x, 1), after)
+        before = jnp.where(column == 0, before, inside(at_x, 0))
+        target_ref[first + 2] = jnp.where(even, after, pltpu.roll(before, 1, 0))
+
+    column = lax.rem(at_y, 2)
+    collect(out_ref, faces, 1 - column)
+    collect(keep_ref, 0, column)
 
 
 def middle_kernel(
@@ -441,7 +478,9 @@
     _, cells_x, cells_y = courant_ref.shape
     tiles = needed_tiles(counts, lax.axis_index("gx"), lax.axis_index("gy"))
     halves = REC_DEV // LANES
-    res = [keep_ref[i] + res_ref[i] for i in range(len(tiles))]
+    at = res_ref.shape[0] - 3
+    own, *pairs = [keep_ref[i] + res_ref[at + i] for i in range(3)]
+    res = [own] + [half for pair in pairs for half in (pair, pltpu.roll(pair, SUB - 1, 0))]
     for i, absent in enumerate((no_next_x, no_prev_x, no_next_y, no_prev_y)):
         res[i + 1] = jnp.where(absent, 0.0, res[i + 1])
     cells = [
@@ -548,8 +587,8 @@
         "gx": lambda step: perms(lambda g, x, y: (g, x ^ step, y)),
         "gy": lambda step: perms(lambda g, x, y: (g, x, y ^ step)),
     }
-    steps = [("gx", 1 << i) for i in range(1, (tiles_x - 1).bit_length())]
-    steps += [("gy", 1 << i) for i in range(1, (tiles_y - 1).bit_length() - 1)]
+    steps_x = [1 << i for i in range(1, (tiles_x - 1).bit_length())]
+    blocks = [tiles_y >> i for i in range(1, (tiles_y - 1).bit_length())]
     send = lambda value, pairs: lax.ppermute(value, AXES, pairs)
 
     face_x = pltpu.VMEM((deep, cells_x, cells_y), F32)
@@ -559,7 +598,7 @@
     wave = wave_now.shape
 
     def kernel(body, outs, n_scalar, n_array, scratch=(), out_specs=None, aliases={}, cost=None):
-        name = body.__name__.removesuffix("_kernel")
+        name = getattr(body, "func", body).__name__.removesuffix("_kernel")
 
         def call(*args):
             args = args[:n_scalar] + tuple(near_memory(a) for a in args[n_scalar:])
@@ -582,7 +621,6 @@
     record_rows = records.reshape(shots, 2, total_recv // LANES, LANES).transpose(0, 2, 1, 3)
     record_rows = record_rows.reshape(shots, 2 * total_recv // LANES, LANES)
     far = lambda value: pltpu.with_memory_space_constraint(value, pltpu.HBM)
-    left = sum(packed_sizes(counts))
     now, old, speed, cells, xa, xb = pl.pallas_call(
         functools.partial(bring_kernel, float(span * span), counts),
         out_shape=(
@@ -602,28 +640,30 @@
     xb_in, xa_in = send(xb, swap_xb), send(xa, swap_xa)
     ya, yb = kernel(pack_kernel, (face_y, face_y), 0, 1)(now)
     yb_in = send(yb, swap_yb)
-    partial_res, keep = kernel(join_kernel, (tiles_of(faces + left), tiles_of(packed_sizes(counts)[1])), 0, 3)(
-        ya, xa, xa_in
-    )
-    ya_in = send(partial_res, swap_ya)
-    other = ya_in
+    sums = tiles_of(block_parts(counts, blocks[0])[-1])
+    wanted, partial_res = kernel(join_kernel, (sums, sums), 0, 3)(xa, xa_in, ya)
+    other = send(wanted, swap_along["gy"](blocks[0]))
+    for block in blocks[:-1]:
+        sums = tiles_of(block_parts(counts, block // 2)[-1])
+        fold = functools.partial(fold_kernel, block)
+        wanted, partial_res = kernel(fold, (sums, sums), 0, 2)(partial_res, other)
+        other = send(wanted, swap_along["gy"](block // 2))
+    ya_in = send(ya, swap_ya)
     base = kernel(local_kernel, wave_v, 0, 3)(now, old, speed)
-    for axis, step in steps:
-        partial_res = kernel(sum_kernel, tiles_of(left), 0, 5)(partial_res, keep, other, base, cells)
-        keep = partial_res
-        other = send(partial_res, swap_along[axis](step))
+    for step in steps_x:
+        partial_res = kernel(sum_kernel, sums, 0, 3)(partial_res, other, base)
+        other = send(partial_res, swap_along["gx"](step))
     wave_middle, xa, xb, ya, yb = kernel(middle_kernel, (wave_v, face_x, face_x, face_y, face_y), 0, 6, [wave_v], cost=pl.CostEstimate(flops=10*10**8, bytes_accessed=0, transcendentals=0))(
         base, speed, xa_in, xb_in, ya_in, yb_in
     )
-    wanted, keep, ya, yb = kernel(
-        needed_kernel, (tiles_of(5), tiles_of(5), face_y, face_y), 0, 5, aliases={3: 2, 4: 3}, cost=pl.CostEstimate(flops=30*10**8, bytes_accessed=0, transcendentals=0)
+    y_more, keep, yb = kernel(
+        needed_kernel, (tiles_of(faces + 3), tiles_of(3), face_y), 0, 5, aliases={4: 2}, cost=pl.CostEstimate(flops=30*10**8, bytes_accessed=0, transcendentals=0)
     )(partial_res, other, wave_middle, ya, yb)
     xb_in, xa_in = send(xb, swap_xb), send(xa, swap_xa)
-    res_in = send(wanted, swap_along["gy"](tiles_y // 2))
-    ya_in, yb_in = send(ya, swap_ya), send(yb, swap_yb)
+    ya_in, yb_in = send(y_more, swap_ya), send(yb, swap_yb)
     base = kernel(second_local_kernel, wave_v, 0, 4, cost=pl.CostEstimate(flops=0*10**8, bytes_accessed=0, transcendentals=0))(wave_middle, now, speed, keep)
     plane = (2, 1, cells_x, cells_y)
-    layers = kernel(inject_kernel, tiles_of(4), 0, 4)(keep, res_in, cells, speed)
+    layers = kernel(inject_kernel, tiles_of(4), 0, 4)(keep, ya_in, cells, speed)
     wave_after, wave_middle = kernel(
         after_kernel, (jax.ShapeDtypeStruct(wave, F32),) * 2, 0, 8,
         [wave_v, wave_v, pltpu.VMEM(plane, F32), pltpu.SemaphoreType.DMA((11,))],

time: 22 us -> 21.5 us (0.977)
  starting transfers between devices: 11.7 us -> 11.2 us
    ppermute x10, starting transfers between devices: 11.7 us -> 11.2 us  [on_device(): send = lambda value, pairs: lax.ppermute(value, AXES, pairs)]
  transfers between devices with their start and end apart: 10 -> 10, of which waited for: 3 -> 2; matrix products, arithmetic and copies ran while one was open for 0% -> 0% of each run, Pallas kernels for 19% -> 19%
where the time goes in v7:
time: 21.5 us; the launch traced here: 21.2 us
  starting transfers between devices  11.2 us (52%)
  Pallas kernels  6.99 us (33%)
  waiting for transfers between devices  2.29 us (11%)
  between operations  0.72 us (3%)
    ppermute x10, starting transfers between devices, on_device(): send = lambda value, pairs: lax.ppermute(value, AXES, pairs)  11.2 us
    pallas_call x9, Pallas kernels, call(): pl.pallas_call(functools.partial(body, counts), out_shape=outs, in_specs=...  5.4 us
    ppermute x10, waiting for transfers between devices, on_device(): send = lambda value, pairs: lax.ppermute(value, AXES, pairs)  2.29 us
    pallas_call x1, Pallas kernels, on_device(): pl.pallas_call(functools.partial(bring_kernel, float(span * span), counts...  1.59 us
  transfers between devices with their start and end apart: 10, of which 2 were waited for; matrix products, arithmetic and copies ran while one was open for 0% of the time, Pallas kernels for 19%

profile of v7, /device:TPU:0, one launch (start us, length us, event | category | flops | bytes accessed | tf_op | source)
XLA Modules:
  0.0 21.2 jit_solution(3543560941383948104)
XLA Ops:
  0.6 1.6 %bring.1 = (f32[2,64,8,128]{3,2,1,0:T(8,128)S(1)}, f32[2,64,8,128]{3,2,1,0:T(8,128)S(1)}, f32[64,8,128]{2,1,0:T(8,128)S(1)}, s32[32,128]{1,0:T(8,128)S(1)}, f32[...) custom-call(s32[2,16]{1,0:T(2,128)} %signs_hbm.1, s32[16]{0:T(128)} %sx_hbm.1, s32[16]{0:T(128)} %sy_hbm.1, ...), custom_call_target="tpu_custom_call" | custom-call | tf_op jit(solution)/shard_map/bring/pallas_call | solution.py:624
  2.2 0.5 %collective-permute-start = (f32[80,8,128]{2,1,0:T(8,128)S(1)}, f32[80,8,128]{2,1,0:T(8,128)S(1)}, u32[]{:S(2)}, u32[]{:S(2)}) collective-permute-start(f32[80,8,128]{2,1,0:T(8,128)S(1)} %get-tuple-element.23.own_ref), channel_id=1, source_target_pairs={{0,4},{1,5},{2,6},{3,7},{4,0},{5,1},{6,2},{7,3},{8,12},{9,13},{10,... | collective-permute-start | bytes 983048 | tf_op jit(solution)/shard_map/ppermute | solution.py:592
  2.8 2.6 %collective-permute-start.1 = (f32[64,8,128]{2,1,0:T(8,128)S(1)}, f32[64,8,128]{2,1,0:T(8,128)S(1)}, u32[]{:S(2)}, u32[]{:S(2)}) collective-permute-start(f32[64,8,128]{2,1,0:T(8,128)S(1)} %get-tuple-element.24), channel_id=1, source_target_pairs={{0,16},{1,17},{2,18},{3,19},{4,8},{5,9},{6,10},{7,11},{8,4},{9,5},... | collective-permute-start | bytes 786440 | tf_op jit(solution)/shard_map/ppermute | solution.py:592
  5.3 0.4 %pack.1 = (f32[4,8,128]{2,1,0:T(8,128)S(1)}, f32[4,8,128]{2,1,0:T(8,128)S(1)}) custom-call(f32[2,64,8,128]{3,2,1,0:T(8,128)S(1)} %get-tuple-element.20.now_ref.old_ref), custom_call_target="tpu_custom_call" | custom-call | tf_op jit(solution)/shard_map/pack/pallas_call | solution.py:605
  5.7 0.0 collective-permute-done.xa_ref.other_ref
  5.8 2.7 %collective-permute-start.4 = (f32[8,8,128]{2,1,0:T(8,128)S(1)}, f32[8,8,128]{2,1,0:T(8,128)S(1)}, u32[]{:S(2)}, u32[]{:S(2)}) collective-permute-start(f32[8,8,128]{2,1,0:T(8,128)S(1)} %get-tuple-element.29), channel_id=1, source_target_pairs={{0,2},{1,3},{2,0},{3,1},{4,6},{5,7},{6,4},{7,5},{8,10},{9,11},{10,... | collective-permute-start | bytes 98312 | tf_op jit(solution)/shard_map/ppermute | solution.py:592
  8.4 0.0 collective-permute-start.3
  8.4 1.6 %collective-permute-start.2 = (f32[4,8,128]{2,1,0:T(8,128)S(1)}, f32[4,8,128]{2,1,0:T(8,128)S(1)}, u32[]{:S(2)}, u32[]{:S(2)}) collective-permute-start(f32[4,8,128]{2,1,0:T(8,128)S(1)} %get-tuple-element.25.before_ref), channel_id=1, source_target_pairs={{0,1},{1,0},{2,3},{3,2},{4,5},{5,4},{6,7},{7,6},{8,9},{9,8},{10,11... | collective-permute-start | bytes 49160 | tf_op jit(solution)/shard_map/ppermute | solution.py:592
  10.0 1.1 %local.1.base_ref.before_ref = f32[2,64,8,128]{3,2,1,0:T(8,128)S(1)} custom-call(f32[2,64,8,128]{3,2,1,0:T(8,128)S(1)} %get-tuple-element.20.now_ref.old_ref, f32[2,64,8,128]{3,2,1,0:T(8,128)S(1)} %get-tuple-element.21.old_ref, f32[64,8,128]{2,1,0:T(8,128)S(1)} %get-tuple-element.22.courant_ref), custom_call_target="tpu_custom_call" | custom-call | tf_op jit(solution)/shard_map/local/pallas_call | solution.py:605
  11.1 0.0 collective-permute-done.4.other_ref
  11.1 1.2 %collective-permute-start.5 = (f32[8,8,128]{2,1,0:T(8,128)S(1)}, f32[8,8,128]{2,1,0:T(8,128)S(1)}, u32[]{:S(2)}, u32[]{:S(2)}) collective-permute-start(f32[8,8,128]{2,1,0:T(8,128)S(1)} %sum.1.own_ref), channel_id=1, source_target_pairs={{0,8},{1,9},{2,10},{3,11},{4,12},{5,13},{6,14},{7,15},{8,0},{9,1},... | collective-permute-start | bytes 98312 | tf_op jit(solution)/shard_map/ppermute | solution.py:592
  12.3 0.0 collective-permute-done.3.yb_ref
  12.3 0.0 collective-permute-done.2.ya_ref
  12.3 0.0 collective-permute-done.1.xb_ref
  12.3 1.2 %middle.1 = (f32[2,64,8,128]{3,2,1,0:T(8,128)S(1)}, f32[64,8,128]{2,1,0:T(8,128)S(1)}, f32[64,8,128]{2,1,0:T(8,128)S(1)}, f32[4,8,128]{2,1,0:T(8,128)S(1)}, f32[4,8,128]{2,1,0:T(8,128)S(1)}) custom-call(f32[2,64,8,128]{3,2,1,0:T(8,128)S(1)} %local.1.base_ref.before_ref, f32[64,8,128]{2,1,0:T(8,128)S(1)} %get-tuple-element.22.courant_ref, ...), custom_call_target="tpu_custom_call" | custom-call | flops 1000000000 | tf_op jit(solution)/shard_map/middle/pallas_call | solution.py:605
  13.5 0.0 collective-permute-start.6
  13.5 1.6 %collective-permute-start.7 = (f32[64,8,128]{2,1,0:T(8,128)S(1)}, f32[64,8,128]{2,1,0:T(8,128)S(1)}, u32[]{:S(2)}, u32[]{:S(2)}) collective-permute-start(f32[64,8,128]{2,1,0:T(8,128)S(1)} %get-tuple-element.34), channel_id=1, source_target_pairs={{0,16},{1,17},{2,18},{3,19},{4,8},{5,9},{6,10},{7,11},{8,4},{9,5},... | collective-permute-start | bytes 786440 | tf_op jit(solution)/shard_map/ppermute | solution.py:592
  15.1 0.0 collective-permute-done.5.other_ref
  15.1 1.1 %collective-permute-start.8 = (f32[7,8,128]{2,1,0:T(8,128)S(1)}, f32[7,8,128]{2,1,0:T(8,128)S(1)}, u32[]{:S(2)}, u32[]{:S(2)}) collective-permute-start(f32[7,8,128]{2,1,0:T(8,128)S(1)} %get-tuple-element.35), channel_id=1, source_target_pairs={{0,1},{1,0},{2,3},{3,2},{4,5},{5,4},{6,7},{7,6},{8,9},{9,8},{10,11... | collective-permute-start | bytes 86024 | tf_op jit(solution)/shard_map/ppermute | solution.py:592
  16.3 0.0 collective-permute-start.9
  16.3 1.1 %second_local.1.base_ref = f32[2,64,8,128]{3,2,1,0:T(8,128)S(1)} custom-call(f32[2,64,8,128]{3,2,1,0:T(8,128)S(1)} %get-tuple-element.27.before_ref.now_ref.mid_ref, f32[2,64,8,128]{3,2,1,0:T(8,128)S(1)} %get-tuple-element.20.now_ref.old_ref, f32[64,8,128]{2,1,0:T(8,128)S(1)} %get-tuple-element.22.courant_ref, ...), custom_call_target="tpu_custom_call" | custom-call | tf_op jit(solution)/shard_map/second_local/pallas_call | solution.py:605
  17.3 1.7 %collective-permute-done.8.res_ref.ya_ref = f32[7,8,128]{2,1,0:T(8,128)S(1)} collective-permute-done((f32[7,8,128]{2,1,0:T(8,128)S(1)}, f32[7,8,128]{2,1,0:T(8,128)S(1)}, u32[]{:S(2)}, u32[]{:S(2)}) %collective-permute-start.8) | collective-permute-done | bytes 28704 | tf_op jit(solution)/shard_map/ppermute | solution.py:592
  19.1 0.3 %inject.1.layer_ref = f32[4,8,128]{2,1,0:T(8,128)S(1)} custom-call(f32[3,8,128]{2,1,0:T(8,128)S(1)} %get-tuple-element.32.before_ref.keep_ref, f32[7,8,128]{2,1,0:T(8,128)S(1)} %collective-permute-done.8.res_ref.ya_ref, s32[32,128]{1,0:T(8,128)S(1)} %get-tuple-element.37.cell_ref, f32[64,8,128]{2,1,0:T(8,128)S(1)} %get-tuple-element.22.courant_ref), custom_call_target="tpu_custom_call" | custom-call | tf_op jit(solution)/shard_map/inject/pallas_call | solution.py:605
  19.4 0.0 collective-permute-done.9.yb_ref
  19.4 0.0 collective-permute-done.6.xa_ref
  19.4 0.5 %collective-permute-done.7.xb_ref = f32[64,8,128]{2,1,0:T(8,128)S(1)} collective-permute-done((f32[64,8,128]{2,1,0:T(8,128)S(1)}, f32[64,8,128]{2,1,0:T(8,128)S(1)}, u32[]{:S(2)}, u32[]{:S(2)}) %collective-permute-start.7) | collective-permute-done | bytes 262176 | tf_op jit(solution)/shard_map/ppermute | solution.py:592
  20.0 1.3 %after.1 = (f32[2,64,8,128]{3,2,1,0:T(8,128)}, f32[2,64,8,128]{3,2,1,0:T(8,128)}) custom-call(f32[2,64,8,128]{3,2,1,0:T(8,128)S(1)} %second_local.1.base_ref, f32[2,64,8,128]{3,2,1,0:T(8,128)S(1)} %get-tuple-element.27.before_ref.now_ref.mid_ref, f32[64,8,128]{2,1,0:T(8,128)S(1)} %get-tuple-element.22.courant_ref, ...), custom_call_target="tpu_custom_call" | custom-call | tf_op jit(solution)/shard_map/after/pallas_call | solution.py:605
  (3 shorter events, 0.1 us)
Async XLA Ops:
  2.2 3.5 %collective-permute-start = (f32[80,8,128]{2,1,0:T(8,128)S(1)}, f32[80,8,128]{2,1,0:T(8,128)S(1)}, u32[]{:S(2)}, u32[]{:S(2)}) collective-permute-start(f32[80,8,128]{2,1,0:T(8,128)S(1)} %get-tuple-element.23.own_ref), channel_id=1, source_target_pairs={{0,4},{1,5},{2,6},{3,7},{4,0},{5,1},{6,2},{7,3},{8,12},{9,13},{10,... | collective-permute-start | bytes 983048 | tf_op jit(solution)/shard_map/ppermute | solution.py:592
  2.8 9.6 %collective-permute-start.1 = (f32[64,8,128]{2,1,0:T(8,128)S(1)}, f32[64,8,128]{2,1,0:T(8,128)S(1)}, u32[]{:S(2)}, u32[]{:S(2)}) collective-permute-start(f32[64,8,128]{2,1,0:T(8,128)S(1)} %get-tuple-element.24), channel_id=1, source_target_pairs={{0,16},{1,17},{2,18},{3,19},{4,8},{5,9},{6,10},{7,11},{8,4},{9,5},... | collective-permute-start | bytes 786440 | tf_op jit(solution)/shard_map/ppermute | solution.py:592
  5.8 5.3 %collective-permute-start.4 = (f32[8,8,128]{2,1,0:T(8,128)S(1)}, f32[8,8,128]{2,1,0:T(8,128)S(1)}, u32[]{:S(2)}, u32[]{:S(2)}) collective-permute-start(f32[8,8,128]{2,1,0:T(8,128)S(1)} %get-tuple-element.29), channel_id=1, source_target_pairs={{0,2},{1,3},{2,0},{3,1},{4,6},{5,7},{6,4},{7,5},{8,10},{9,11},{10,... | collective-permute-start | bytes 98312 | tf_op jit(solution)/shard_map/ppermute | solution.py:592
  8.4 3.9 %collective-permute-start.3 = (f32[4,8,128]{2,1,0:T(8,128)S(1)}, f32[4,8,128]{2,1,0:T(8,128)S(1)}, u32[]{:S(2)}, u32[]{:S(2)}) collective-permute-start(f32[4,8,128]{2,1,0:T(8,128)S(1)} %get-tuple-element.26), channel_id=1, source_target_pairs={{0,4},{1,2},{2,1},{3,7},{4,0},{5,6},{6,5},{7,3},{8,12},{9,10},{10,... | collective-permute-start | bytes 49160 | tf_op jit(solution)/shard_map/ppermute | solution.py:592
  8.4 3.9 %collective-permute-start.2 = (f32[4,8,128]{2,1,0:T(8,128)S(1)}, f32[4,8,128]{2,1,0:T(8,128)S(1)}, u32[]{:S(2)}, u32[]{:S(2)}) collective-permute-start(f32[4,8,128]{2,1,0:T(8,128)S(1)} %get-tuple-element.25.before_ref), channel_id=1, source_target_pairs={{0,1},{1,0},{2,3},{3,2},{4,5},{5,4},{6,7},{7,6},{8,9},{9,8},{10,11... | collective-permute-start | bytes 49160 | tf_op jit(solution)/shard_map/ppermute | solution.py:592
  11.1 4.0 %collective-permute-start.5 = (f32[8,8,128]{2,1,0:T(8,128)S(1)}, f32[8,8,128]{2,1,0:T(8,128)S(1)}, u32[]{:S(2)}, u32[]{:S(2)}) collective-permute-start(f32[8,8,128]{2,1,0:T(8,128)S(1)} %sum.1.own_ref), channel_id=1, source_target_pairs={{0,8},{1,9},{2,10},{3,11},{4,12},{5,13},{6,14},{7,15},{8,0},{9,1},... | collective-permute-start | bytes 98312 | tf_op jit(solution)/shard_map/ppermute | solution.py:592
  13.5 5.9 %collective-permute-start.6 = (f32[64,8,128]{2,1,0:T(8,128)S(1)}, f32[64,8,128]{2,1,0:T(8,128)S(1)}, u32[]{:S(2)}, u32[]{:S(2)}) collective-permute-start(f32[64,8,128]{2,1,0:T(8,128)S(1)} %get-tuple-element.33), channel_id=1, source_target_pairs={{0,4},{1,5},{2,6},{3,7},{4,0},{5,1},{6,2},{7,3},{8,12},{9,13},{10,... | collective-permute-start | bytes 786440 | tf_op jit(solution)/shard_map/ppermute | solution.py:592
  13.5 6.4 %collective-permute-start.7 = (f32[64,8,128]{2,1,0:T(8,128)S(1)}, f32[64,8,128]{2,1,0:T(8,128)S(1)}, u32[]{:S(2)}, u32[]{:S(2)}) collective-permute-start(f32[64,8,128]{2,1,0:T(8,128)S(1)} %get-tuple-element.34), channel_id=1, source_target_pairs={{0,16},{1,17},{2,18},{3,19},{4,8},{5,9},{6,10},{7,11},{8,4},{9,5},... | collective-permute-start | bytes 786440 | tf_op jit(solution)/shard_map/ppermute | solution.py:592
  15.1 3.9 %collective-permute-start.8 = (f32[7,8,128]{2,1,0:T(8,128)S(1)}, f32[7,8,128]{2,1,0:T(8,128)S(1)}, u32[]{:S(2)}, u32[]{:S(2)}) collective-permute-start(f32[7,8,128]{2,1,0:T(8,128)S(1)} %get-tuple-element.35), channel_id=1, source_target_pairs={{0,1},{1,0},{2,3},{3,2},{4,5},{5,4},{6,7},{7,6},{8,9},{9,8},{10,11... | collective-permute-start | bytes 86024 | tf_op jit(solution)/shard_map/ppermute | solution.py:592
  16.3 3.2 %collective-permute-start.9 = (f32[4,8,128]{2,1,0:T(8,128)S(1)}, f32[4,8,128]{2,1,0:T(8,128)S(1)}, u32[]{:S(2)}, u32[]{:S(2)}) collective-permute-start(f32[4,8,128]{2,1,0:T(8,128)S(1)} %get-tuple-element.36), channel_id=1, source_target_pairs={{0,4},{1,2},{2,1},{3,7},{4,0},{5,6},{6,5},{7,3},{8,12},{9,10},{10,... | collective-permute-start | bytes 49160 | tf_op jit(solution)/shard_map/ppermute | solution.py:592

commit v8 on v7

--- a/solution.py
+++ b/solution.py
@@ -421,8 +421,8 @@
     out_ref[...] = own_ref[...] + other_ref[...]
 
 
-def needed_kernel(counts, own_ref, other_ref, before_ref, ya_ref, yb_ref, out_ref, keep_ref, yb_out):
-    del before_ref, yb_ref, yb_out
+def needed_kernel(counts, own_ref, other_ref, before_ref, ya_ref, yb_ref, xa_ref, out_ref, keep_ref, yb_out, xa_out):
+    del before_ref, yb_ref, yb_out, xa_ref, xa_out
     at_x, at_y = lax.axis_index("gx"), lax.axis_index("gy")
     pairs, own, at_outside, at_second, _ = block_parts(counts, 2)
     even = rows_of((SUB, LANES)) % 2 == 0
@@ -651,14 +651,14 @@
     ya_in = send(ya, swap_ya)
     base = kernel(local_kernel, wave_v, 0, 3)(now, old, speed)
     for step in steps_x:
-        partial_res = kernel(sum_kernel, sums, 0, 3)(partial_res, other, base)
+        partial_res = kernel(sum_kernel, sums, 0, 3)(partial_res, other, cells)
         other = send(partial_res, swap_along["gx"](step))
     wave_middle, xa, xb, ya, yb = kernel(middle_kernel, (wave_v, face_x, face_x, face_y, face_y), 0, 6, [wave_v], cost=pl.CostEstimate(flops=10*10**8, bytes_accessed=0, transcendentals=0))(
         base, speed, xa_in, xb_in, ya_in, yb_in
     )
-    y_more, keep, yb = kernel(
-        needed_kernel, (tiles_of(faces + 3), tiles_of(3), face_y), 0, 5, aliases={4: 2}, cost=pl.CostEstimate(flops=30*10**8, bytes_accessed=0, transcendentals=0)
-    )(partial_res, other, wave_middle, ya, yb)
+    y_more, keep, yb, xa = kernel(
+        needed_kernel, (tiles_of(faces + 3), tiles_of(3), face_y, face_x), 0, 6, aliases={4: 2, 5: 3}, cost=pl.CostEstimate(flops=30*10**8, bytes_accessed=0, transcendentals=0)
+    )(partial_res, other, wave_middle, ya, yb, xa)
     xb_in, xa_in = send(xb, swap_xb), send(xa, swap_xa)
     ya_in, yb_in = send(y_more, swap_ya), send(yb, swap_yb)
     base = kernel(second_local_kernel, wave_v, 0, 4, cost=pl.CostEstimate(flops=0*10**8, bytes_accessed=0, transcendentals=0))(wave_middle, now, speed, keep)

time: 21.5 us -> 21.4 us (level)
  waiting for transfers between devices: 2.29 us -> 2.05 us
    ppermute x10, waiting for transfers between devices: 2.29 us -> 2.05 us  [on_device(): send = lambda value, pairs: lax.ppermute(value, AXES, pairs)]
  transfers between devices with their start and end apart: 10 -> 10, of which waited for: 2 -> 3; matrix products, arithmetic and copies ran while one was open for 0% -> 0% of each run, Pallas kernels for 19% -> 20%
where the time goes in v8:
time: 21.4 us; the launch traced here: 21.2 us
  starting transfers between devices  11.4 us (53%)
  Pallas kernels  7.01 us (33%)
  waiting for transfers between devices  2.05 us (10%)
  between operations  0.71 us (3%)
    ppermute x10, starting transfers between devices, on_device(): send = lambda value, pairs: lax.ppermute(value, AXES, pairs)  11.4 us
    pallas_call x9, Pallas kernels, call(): pl.pallas_call(functools.partial(body, counts), out_shape=outs, in_specs=...  5.42 us
    ppermute x10, waiting for transfers between devices, on_device(): send = lambda value, pairs: lax.ppermute(value, AXES, pairs)  2.05 us
    pallas_call x1, Pallas kernels, on_device(): pl.pallas_call(functools.partial(bring_kernel, float(span * span), counts...  1.59 us
  transfers between devices with their start and end apart: 10, of which 3 were waited for; matrix products, arithmetic and copies ran while one was open for 0% of the time, Pallas kernels for 20%

profile of v8, /device:TPU:0, one launch (start us, length us, event | category | flops | bytes accessed | tf_op | source)
XLA Modules:
  0.0 21.2 jit_solution(2272104612832393519)
XLA Ops:
  0.6 1.6 %bring.1 = (f32[2,64,8,128]{3,2,1,0:T(8,128)S(1)}, f32[2,64,8,128]{3,2,1,0:T(8,128)S(1)}, f32[64,8,128]{2,1,0:T(8,128)S(1)}, s32[32,128]{1,0:T(8,128)S(1)}, f32[...) custom-call(s32[2,16]{1,0:T(2,128)} %signs_hbm.1, s32[16]{0:T(128)} %sx_hbm.1, s32[16]{0:T(128)} %sy_hbm.1, ...), custom_call_target="tpu_custom_call" | custom-call | tf_op jit(solution)/shard_map/bring/pallas_call | solution.py:624
  2.2 0.5 %collective-permute-start = (f32[80,8,128]{2,1,0:T(8,128)S(1)}, f32[80,8,128]{2,1,0:T(8,128)S(1)}, u32[]{:S(2)}, u32[]{:S(2)}) collective-permute-start(f32[80,8,128]{2,1,0:T(8,128)S(1)} %get-tuple-element.24.own_ref), channel_id=1, source_target_pairs={{0,4},{1,5},{2,6},{3,7},{4,0},{5,1},{6,2},{7,3},{8,12},{9,13},{10,... | collective-permute-start | bytes 983048 | tf_op jit(solution)/shard_map/ppermute | solution.py:592
  2.8 2.6 %collective-permute-start.1 = (f32[64,8,128]{2,1,0:T(8,128)S(1)}, f32[64,8,128]{2,1,0:T(8,128)S(1)}, u32[]{:S(2)}, u32[]{:S(2)}) collective-permute-start(f32[64,8,128]{2,1,0:T(8,128)S(1)} %get-tuple-element.25), channel_id=1, source_target_pairs={{0,16},{1,17},{2,18},{3,19},{4,8},{5,9},{6,10},{7,11},{8,4},{9,5},... | collective-permute-start | bytes 786440 | tf_op jit(solution)/shard_map/ppermute | solution.py:592
  5.3 0.4 %pack.1 = (f32[4,8,128]{2,1,0:T(8,128)S(1)}, f32[4,8,128]{2,1,0:T(8,128)S(1)}) custom-call(f32[2,64,8,128]{3,2,1,0:T(8,128)S(1)} %get-tuple-element.21.now_ref.old_ref), custom_call_target="tpu_custom_call" | custom-call | tf_op jit(solution)/shard_map/pack/pallas_call | solution.py:605
  5.7 0.0 collective-permute-done.xa_ref.other_ref
  5.8 2.7 %collective-permute-start.4 = (f32[8,8,128]{2,1,0:T(8,128)S(1)}, f32[8,8,128]{2,1,0:T(8,128)S(1)}, u32[]{:S(2)}, u32[]{:S(2)}) collective-permute-start(f32[8,8,128]{2,1,0:T(8,128)S(1)} %get-tuple-element.30), channel_id=1, source_target_pairs={{0,2},{1,3},{2,0},{3,1},{4,6},{5,7},{6,4},{7,5},{8,10},{9,11},{10,... | collective-permute-start | bytes 98312 | tf_op jit(solution)/shard_map/ppermute | solution.py:592
  8.4 0.0 collective-permute-start.3
  8.4 1.6 %collective-permute-start.2 = (f32[4,8,128]{2,1,0:T(8,128)S(1)}, f32[4,8,128]{2,1,0:T(8,128)S(1)}, u32[]{:S(2)}, u32[]{:S(2)}) collective-permute-start(f32[4,8,128]{2,1,0:T(8,128)S(1)} %get-tuple-element.26.before_ref), channel_id=1, source_target_pairs={{0,1},{1,0},{2,3},{3,2},{4,5},{5,4},{6,7},{7,6},{8,9},{9,8},{10,11... | collective-permute-start | bytes 49160 | tf_op jit(solution)/shard_map/ppermute | solution.py:592
  10.0 1.1 %local.1.base_ref = f32[2,64,8,128]{3,2,1,0:T(8,128)S(1)} custom-call(f32[2,64,8,128]{3,2,1,0:T(8,128)S(1)} %get-tuple-element.21.now_ref.old_ref, f32[2,64,8,128]{3,2,1,0:T(8,128)S(1)} %get-tuple-element.22.old_ref, f32[64,8,128]{2,1,0:T(8,128)S(1)} %get-tuple-element.23.courant_ref), custom_call_target="tpu_custom_call" | custom-call | tf_op jit(solution)/shard_map/local/pallas_call | solution.py:605
  11.1 0.0 collective-permute-done.4.other_ref
  11.1 1.2 %collective-permute-start.5 = (f32[8,8,128]{2,1,0:T(8,128)S(1)}, f32[8,8,128]{2,1,0:T(8,128)S(1)}, u32[]{:S(2)}, u32[]{:S(2)}) collective-permute-start(f32[8,8,128]{2,1,0:T(8,128)S(1)} %sum.1.own_ref), channel_id=1, source_target_pairs={{0,8},{1,9},{2,10},{3,11},{4,12},{5,13},{6,14},{7,15},{8,0},{9,1},... | collective-permute-start | bytes 98312 | tf_op jit(solution)/shard_map/ppermute | solution.py:592
  12.3 0.0 collective-permute-done.3.yb_ref
  12.3 0.0 collective-permute-done.2.ya_ref
  12.3 0.0 collective-permute-done.1.xb_ref
  12.3 1.2 %middle.1 = (f32[2,64,8,128]{3,2,1,0:T(8,128)S(1)}, f32[64,8,128]{2,1,0:T(8,128)S(1)}, f32[64,8,128]{2,1,0:T(8,128)S(1)}, f32[4,8,128]{2,1,0:T(8,128)S(1)}, f32[4,8,128]{2,1,0:T(8,128)S(1)}) custom-call(f32[2,64,8,128]{3,2,1,0:T(8,128)S(1)} %local.1.base_ref, f32[64,8,128]{2,1,0:T(8,128)S(1)} %get-tuple-element.23.courant_ref, ...), custom_call_target="tpu_custom_call" | custom-call | flops 1000000000 | tf_op jit(solution)/shard_map/middle/pallas_call | solution.py:605
  13.5 1.5 %collective-permute-start.7 = (f32[64,8,128]{2,1,0:T(8,128)S(1)}, f32[64,8,128]{2,1,0:T(8,128)S(1)}, u32[]{:S(2)}, u32[]{:S(2)}) collective-permute-start(f32[64,8,128]{2,1,0:T(8,128)S(1)} %get-tuple-element.37), channel_id=1, source_target_pairs={{0,16},{1,17},{2,18},{3,19},{4,8},{5,9},{6,10},{7,11},{8,4},{9,5},... | collective-permute-start | bytes 786440 | tf_op jit(solution)/shard_map/ppermute | solution.py:592
  15.0 0.1 collective-permute-done.5.other_ref
  15.1 0.1 collective-permute-start.6
  15.2 1.1 %collective-permute-start.8 = (f32[7,8,128]{2,1,0:T(8,128)S(1)}, f32[7,8,128]{2,1,0:T(8,128)S(1)}, u32[]{:S(2)}, u32[]{:S(2)}) collective-permute-start(f32[7,8,128]{2,1,0:T(8,128)S(1)} %get-tuple-element.38), channel_id=1, source_target_pairs={{0,1},{1,0},{2,3},{3,2},{4,5},{5,4},{6,7},{7,6},{8,9},{9,8},{10,11... | collective-permute-start | bytes 86024 | tf_op jit(solution)/shard_map/ppermute | solution.py:592
  16.3 0.2 collective-permute-start.9
  16.5 1.1 %second_local.1.base_ref = f32[2,64,8,128]{3,2,1,0:T(8,128)S(1)} custom-call(f32[2,64,8,128]{3,2,1,0:T(8,128)S(1)} %get-tuple-element.28.before_ref.now_ref.mid_ref, f32[2,64,8,128]{3,2,1,0:T(8,128)S(1)} %get-tuple-element.21.now_ref.old_ref, f32[64,8,128]{2,1,0:T(8,128)S(1)} %get-tuple-element.23.courant_ref, ...), custom_call_target="tpu_custom_call" | custom-call | tf_op jit(solution)/shard_map/second_local/pallas_call | solution.py:605
  17.6 1.6 %collective-permute-done.8.res_ref.ya_ref = f32[7,8,128]{2,1,0:T(8,128)S(1)} collective-permute-done((f32[7,8,128]{2,1,0:T(8,128)S(1)}, f32[7,8,128]{2,1,0:T(8,128)S(1)}, u32[]{:S(2)}, u32[]{:S(2)}) %collective-permute-start.8) | collective-permute-done | bytes 28704 | tf_op jit(solution)/shard_map/ppermute | solution.py:592
  19.1 0.3 %inject.1.layer_ref = f32[4,8,128]{2,1,0:T(8,128)S(1)} custom-call(f32[3,8,128]{2,1,0:T(8,128)S(1)} %get-tuple-element.35.before_ref.keep_ref, f32[7,8,128]{2,1,0:T(8,128)S(1)} %collective-permute-done.8.res_ref.ya_ref, s32[32,128]{1,0:T(8,128)S(1)} %get-tuple-element.31.before_ref.cell_ref, f32[64,8,128]{2,1,0:T(8,128)S(1)} %get-tuple-element.23.courant_ref), custom_call_target="tpu_custom_call" | custom-call | tf_op jit(solution)/shard_map/inject/pallas_call | solution.py:605
  19.5 0.0 collective-permute-done.9.yb_ref
  19.5 0.4 %collective-permute-done.7.xb_ref = f32[64,8,128]{2,1,0:T(8,128)S(1)} collective-permute-done((f32[64,8,128]{2,1,0:T(8,128)S(1)}, f32[64,8,128]{2,1,0:T(8,128)S(1)}, u32[]{:S(2)}, u32[]{:S(2)}) %collective-permute-start.7) | collective-permute-done | bytes 262176 | tf_op jit(solution)/shard_map/ppermute | solution.py:592
  19.9 0.0 collective-permute-done.6.xa_ref
  19.9 1.3 %after.1 = (f32[2,64,8,128]{3,2,1,0:T(8,128)}, f32[2,64,8,128]{3,2,1,0:T(8,128)}) custom-call(f32[2,64,8,128]{3,2,1,0:T(8,128)S(1)} %second_local.1.base_ref, f32[2,64,8,128]{3,2,1,0:T(8,128)S(1)} %get-tuple-element.28.before_ref.now_ref.mid_ref, f32[64,8,128]{2,1,0:T(8,128)S(1)} %get-tuple-element.23.courant_ref, ...), custom_call_target="tpu_custom_call" | custom-call | tf_op jit(solution)/shard_map/after/pallas_call | solution.py:605
  (3 shorter events, 0.1 us)
Async XLA Ops:
  2.2 3.5 %collective-permute-start = (f32[80,8,128]{2,1,0:T(8,128)S(1)}, f32[80,8,128]{2,1,0:T(8,128)S(1)}, u32[]{:S(2)}, u32[]{:S(2)}) collective-permute-start(f32[80,8,128]{2,1,0:T(8,128)S(1)} %get-tuple-element.24.own_ref), channel_id=1, source_target_pairs={{0,4},{1,5},{2,6},{3,7},{4,0},{5,1},{6,2},{7,3},{8,12},{9,13},{10,... | collective-permute-start | bytes 983048 | tf_op jit(solution)/shard_map/ppermute | solution.py:592
  2.8 9.6 %collective-permute-start.1 = (f32[64,8,128]{2,1,0:T(8,128)S(1)}, f32[64,8,128]{2,1,0:T(8,128)S(1)}, u32[]{:S(2)}, u32[]{:S(2)}) collective-permute-start(f32[64,8,128]{2,1,0:T(8,128)S(1)} %get-tuple-element.25), channel_id=1, source_target_pairs={{0,16},{1,17},{2,18},{3,19},{4,8},{5,9},{6,10},{7,11},{8,4},{9,5},... | collective-permute-start | bytes 786440 | tf_op jit(solution)/shard_map/ppermute | solution.py:592
  5.8 5.3 %collective-permute-start.4 = (f32[8,8,128]{2,1,0:T(8,128)S(1)}, f32[8,8,128]{2,1,0:T(8,128)S(1)}, u32[]{:S(2)}, u32[]{:S(2)}) collective-permute-start(f32[8,8,128]{2,1,0:T(8,128)S(1)} %get-tuple-element.30), channel_id=1, source_target_pairs={{0,2},{1,3},{2,0},{3,1},{4,6},{5,7},{6,4},{7,5},{8,10},{9,11},{10,... | collective-permute-start | bytes 98312 | tf_op jit(solution)/shard_map/ppermute | solution.py:592
  8.4 3.9 %collective-permute-start.3 = (f32[4,8,128]{2,1,0:T(8,128)S(1)}, f32[4,8,128]{2,1,0:T(8,128)S(1)}, u32[]{:S(2)}, u32[]{:S(2)}) collective-permute-start(f32[4,8,128]{2,1,0:T(8,128)S(1)} %get-tuple-element.27), channel_id=1, source_target_pairs={{0,4},{1,2},{2,1},{3,7},{4,0},{5,6},{6,5},{7,3},{8,12},{9,10},{10,... | collective-permute-start | bytes 49160 | tf_op jit(solution)/shard_map/ppermute | solution.py:592
  8.4 3.9 %collective-permute-start.2 = (f32[4,8,128]{2,1,0:T(8,128)S(1)}, f32[4,8,128]{2,1,0:T(8,128)S(1)}, u32[]{:S(2)}, u32[]{:S(2)}) collective-permute-start(f32[4,8,128]{2,1,0:T(8,128)S(1)} %get-tuple-element.26.before_ref), channel_id=1, source_target_pairs={{0,1},{1,0},{2,3},{3,2},{4,5},{5,4},{6,7},{7,6},{8,9},{9,8},{10,11... | collective-permute-start | bytes 49160 | tf_op jit(solution)/shard_map/ppermute | solution.py:592
  11.1 4.0 %collective-permute-start.5 = (f32[8,8,128]{2,1,0:T(8,128)S(1)}, f32[8,8,128]{2,1,0:T(8,128)S(1)}, u32[]{:S(2)}, u32[]{:S(2)}) collective-permute-start(f32[8,8,128]{2,1,0:T(8,128)S(1)} %sum.1.own_ref), channel_id=1, source_target_pairs={{0,8},{1,9},{2,10},{3,11},{4,12},{5,13},{6,14},{7,15},{8,0},{9,1},... | collective-permute-start | bytes 98312 | tf_op jit(solution)/shard_map/ppermute | solution.py:592
  13.5 6.4 %collective-permute-start.7 = (f32[64,8,128]{2,1,0:T(8,128)S(1)}, f32[64,8,128]{2,1,0:T(8,128)S(1)}, u32[]{:S(2)}, u32[]{:S(2)}) collective-permute-start(f32[64,8,128]{2,1,0:T(8,128)S(1)} %get-tuple-element.37), channel_id=1, source_target_pairs={{0,16},{1,17},{2,18},{3,19},{4,8},{5,9},{6,10},{7,11},{8,4},{9,5},... | collective-permute-start | bytes 786440 | tf_op jit(solution)/shard_map/ppermute | solution.py:592
  15.1 4.8 %collective-permute-start.6 = (f32[64,8,128]{2,1,0:T(8,128)S(1)}, f32[64,8,128]{2,1,0:T(8,128)S(1)}, u32[]{:S(2)}, u32[]{:S(2)}) collective-permute-start(f32[64,8,128]{2,1,0:T(8,128)S(1)} %get-tuple-element.36), channel_id=1, source_target_pairs={{0,4},{1,5},{2,6},{3,7},{4,0},{5,1},{6,2},{7,3},{8,12},{9,13},{10,... | collective-permute-start | bytes 786440 | tf_op jit(solution)/shard_map/ppermute | solution.py:592
  15.2 3.9 %collective-permute-start.8 = (f32[7,8,128]{2,1,0:T(8,128)S(1)}, f32[7,8,128]{2,1,0:T(8,128)S(1)}, u32[]{:S(2)}, u32[]{:S(2)}) collective-permute-start(f32[7,8,128]{2,1,0:T(8,128)S(1)} %get-tuple-element.38), channel_id=1, source_target_pairs={{0,1},{1,0},{2,3},{3,2},{4,5},{5,4},{6,7},{7,6},{8,9},{9,8},{10,11... | collective-permute-start | bytes 86024 | tf_op jit(solution)/shard_map/ppermute | solution.py:592
  16.3 3.2 %collective-permute-start.9 = (f32[4,8,128]{2,1,0:T(8,128)S(1)}, f32[4,8,128]{2,1,0:T(8,128)S(1)}, u32[]{:S(2)}, u32[]{:S(2)}) collective-permute-start(f32[4,8,128]{2,1,0:T(8,128)S(1)} %get-tuple-element.39), channel_id=1, source_target_pairs={{0,4},{1,2},{2,1},{3,7},{4,0},{5,6},{6,5},{7,3},{8,12},{9,10},{10,... | collective-permute-start | bytes 49160 | tf_op jit(solution)/shard_map/ppermute | solution.py:592

commit v9 on v8

--- a/solution.py
+++ b/solution.py
@@ -638,7 +638,7 @@
         name="bring",
     )(*(far(a) for a in (signs, source_x, source_y, record_rows, cell_rows, wave_now, wave_before, courant)))
     xb_in, xa_in = send(xb, swap_xb), send(xa, swap_xa)
-    ya, yb = kernel(pack_kernel, (face_y, face_y), 0, 1)(now)
+    ya, yb = kernel(pack_kernel, (tiles_of(faces + 1), face_y), 0, 1)(now)
     yb_in = send(yb, swap_yb)
     sums = tiles_of(block_parts(counts, blocks[0])[-1])
     wanted, partial_res = kernel(join_kernel, (sums, sums), 0, 3)(xa, xa_in, ya)

time: 21.4 us -> 21.4 us (level)
  waiting for transfers between devices: 2.05 us -> 1.73 us
  starting transfers between devices: 11.4 us -> 11.7 us
    ppermute x10, starting transfers between devices: 11.4 us -> 11.7 us  [on_device(): send = lambda value, pairs: lax.ppermute(value, AXES, pairs)]
    ppermute x10, waiting for transfers between devices: 2.05 us -> 1.73 us  [on_device(): send = lambda value, pairs: lax.ppermute(value, AXES, pairs)]
where the time goes in v9:
time: 21.4 us; the launch traced here: 21.2 us
  starting transfers between devices  11.7 us (55%)
  Pallas kernels  7.01 us (33%)
  waiting for transfers between devices  1.73 us (8%)
  between operations  0.7 us (3%)
    ppermute x10, starting transfers between devices, on_device(): send = lambda value, pairs: lax.ppermute(value, AXES, pairs)  11.7 us
    pallas_call x9, Pallas kernels, call(): pl.pallas_call(functools.partial(body, counts), out_shape=outs, in_specs=...  5.41 us
    ppermute x10, waiting for transfers between devices, on_device(): send = lambda value, pairs: lax.ppermute(value, AXES, pairs)  1.73 us
    pallas_call x1, Pallas kernels, on_device(): pl.pallas_call(functools.partial(bring_kernel, float(span * span), counts...  1.59 us
  transfers between devices with their start and end apart: 10, of which 3 were waited for; matrix products, arithmetic and copies ran while one was open for 0% of the time, Pallas kernels for 20%

profile of v9, /device:TPU:0, one launch (start us, length us, event | category | flops | bytes accessed | tf_op | source)
XLA Modules:
  0.0 21.2 jit_solution(15685847482763532455)
XLA Ops:
  0.6 1.6 %bring.1 = (f32[2,64,8,128]{3,2,1,0:T(8,128)S(1)}, f32[2,64,8,128]{3,2,1,0:T(8,128)S(1)}, f32[64,8,128]{2,1,0:T(8,128)S(1)}, s32[32,128]{1,0:T(8,128)S(1)}, f32[...) custom-call(s32[2,16]{1,0:T(2,128)} %signs_hbm.1, s32[16]{0:T(128)} %sx_hbm.1, s32[16]{0:T(128)} %sy_hbm.1, ...), custom_call_target="tpu_custom_call" | custom-call | tf_op jit(solution)/shard_map/bring/pallas_call | solution.py:624
  2.2 0.5 %collective-permute-start = (f32[80,8,128]{2,1,0:T(8,128)S(1)}, f32[80,8,128]{2,1,0:T(8,128)S(1)}, u32[]{:S(2)}, u32[]{:S(2)}) collective-permute-start(f32[80,8,128]{2,1,0:T(8,128)S(1)} %get-tuple-element.24.own_ref), channel_id=1, source_target_pairs={{0,4},{1,5},{2,6},{3,7},{4,0},{5,1},{6,2},{7,3},{8,12},{9,13},{10,... | collective-permute-start | bytes 983048 | tf_op jit(solution)/shard_map/ppermute | solution.py:592
  2.8 2.6 %collective-permute-start.1 = (f32[64,8,128]{2,1,0:T(8,128)S(1)}, f32[64,8,128]{2,1,0:T(8,128)S(1)}, u32[]{:S(2)}, u32[]{:S(2)}) collective-permute-start(f32[64,8,128]{2,1,0:T(8,128)S(1)} %get-tuple-element.25), channel_id=1, source_target_pairs={{0,16},{1,17},{2,18},{3,19},{4,8},{5,9},{6,10},{7,11},{8,4},{9,5},... | collective-permute-start | bytes 786440 | tf_op jit(solution)/shard_map/ppermute | solution.py:592
  5.3 0.4 %pack.1 = (f32[5,8,128]{2,1,0:T(8,128)S(1)}, f32[4,8,128]{2,1,0:T(8,128)S(1)}) custom-call(f32[2,64,8,128]{3,2,1,0:T(8,128)S(1)} %get-tuple-element.21.now_ref.old_ref), custom_call_target="tpu_custom_call" | custom-call | tf_op jit(solution)/shard_map/pack/pallas_call | solution.py:605
  5.7 0.0 collective-permute-done.xa_ref.other_ref
  5.8 2.7 %collective-permute-start.4 = (f32[8,8,128]{2,1,0:T(8,128)S(1)}, f32[8,8,128]{2,1,0:T(8,128)S(1)}, u32[]{:S(2)}, u32[]{:S(2)}) collective-permute-start(f32[8,8,128]{2,1,0:T(8,128)S(1)} %get-tuple-element.30), channel_id=1, source_target_pairs={{0,2},{1,3},{2,0},{3,1},{4,6},{5,7},{6,4},{7,5},{8,10},{9,11},{10,... | collective-permute-start | bytes 98312 | tf_op jit(solution)/shard_map/ppermute | solution.py:592
  8.4 1.6 %collective-permute-start.2 = (f32[5,8,128]{2,1,0:T(8,128)S(1)}, f32[5,8,128]{2,1,0:T(8,128)S(1)}, u32[]{:S(2)}, u32[]{:S(2)}) collective-permute-start(f32[5,8,128]{2,1,0:T(8,128)S(1)} %get-tuple-element.26.before_ref), channel_id=1, source_target_pairs={{0,1},{1,0},{2,3},{3,2},{4,5},{5,4},{6,7},{7,6},{8,9},{9,8},{10,11... | collective-permute-start | bytes 61448 | tf_op jit(solution)/shard_map/ppermute | solution.py:592
  10.0 0.0 collective-permute-start.3
  10.0 1.1 %local.1.base_ref = f32[2,64,8,128]{3,2,1,0:T(8,128)S(1)} custom-call(f32[2,64,8,128]{3,2,1,0:T(8,128)S(1)} %get-tuple-element.21.now_ref.old_ref, f32[2,64,8,128]{3,2,1,0:T(8,128)S(1)} %get-tuple-element.22.old_ref, f32[64,8,128]{2,1,0:T(8,128)S(1)} %get-tuple-element.23.courant_ref), custom_call_target="tpu_custom_call" | custom-call | tf_op jit(solution)/shard_map/local/pallas_call | solution.py:605
  11.1 0.0 collective-permute-done.4.other_ref
  11.1 1.2 %collective-permute-start.5 = (f32[8,8,128]{2,1,0:T(8,128)S(1)}, f32[8,8,128]{2,1,0:T(8,128)S(1)}, u32[]{:S(2)}, u32[]{:S(2)}) collective-permute-start(f32[8,8,128]{2,1,0:T(8,128)S(1)} %sum.1.own_ref), channel_id=1, source_target_pairs={{0,8},{1,9},{2,10},{3,11},{4,12},{5,13},{6,14},{7,15},{8,0},{9,1},... | collective-permute-start | bytes 98312 | tf_op jit(solution)/shard_map/ppermute | solution.py:592
  12.3 0.0 collective-permute-done.3.yb_ref
  12.3 0.0 collective-permute-done.2.ya_ref
  12.3 0.0 collective-permute-done.1.xb_ref
  12.3 1.2 %middle.1 = (f32[2,64,8,128]{3,2,1,0:T(8,128)S(1)}, f32[64,8,128]{2,1,0:T(8,128)S(1)}, f32[64,8,128]{2,1,0:T(8,128)S(1)}, f32[4,8,128]{2,1,0:T(8,128)S(1)}, f32[4,8,128]{2,1,0:T(8,128)S(1)}) custom-call(f32[2,64,8,128]{3,2,1,0:T(8,128)S(1)} %local.1.base_ref, f32[64,8,128]{2,1,0:T(8,128)S(1)} %get-tuple-element.23.courant_ref, ...), custom_call_target="tpu_custom_call" | custom-call | flops 1000000000 | tf_op jit(solution)/shard_map/middle/pallas_call | solution.py:605
  13.5 1.5 %collective-permute-start.7 = (f32[64,8,128]{2,1,0:T(8,128)S(1)}, f32[64,8,128]{2,1,0:T(8,128)S(1)}, u32[]{:S(2)}, u32[]{:S(2)}) collective-permute-start(f32[64,8,128]{2,1,0:T(8,128)S(1)} %get-tuple-element.37), channel_id=1, source_target_pairs={{0,16},{1,17},{2,18},{3,19},{4,8},{5,9},{6,10},{7,11},{8,4},{9,5},... | collective-permute-start | bytes 786440 | tf_op jit(solution)/shard_map/ppermute | solution.py:592
  15.0 0.1 collective-permute-done.5.other_ref
  15.1 0.1 collective-permute-start.6
  15.2 1.6 %collective-permute-start.8 = (f32[7,8,128]{2,1,0:T(8,128)S(1)}, f32[7,8,128]{2,1,0:T(8,128)S(1)}, u32[]{:S(2)}, u32[]{:S(2)}) collective-permute-start(f32[7,8,128]{2,1,0:T(8,128)S(1)} %get-tuple-element.38), channel_id=1, source_target_pairs={{0,1},{1,0},{2,3},{3,2},{4,5},{5,4},{6,7},{7,6},{8,9},{9,8},{10,11... | collective-permute-start | bytes 86024 | tf_op jit(solution)/shard_map/ppermute | solution.py:592
  16.8 0.1 collective-permute-start.9
  16.8 1.1 %second_local.1.base_ref = f32[2,64,8,128]{3,2,1,0:T(8,128)S(1)} custom-call(f32[2,64,8,128]{3,2,1,0:T(8,128)S(1)} %get-tuple-element.28.before_ref.now_ref.mid_ref, f32[2,64,8,128]{3,2,1,0:T(8,128)S(1)} %get-tuple-element.21.now_ref.old_ref, f32[64,8,128]{2,1,0:T(8,128)S(1)} %get-tuple-element.23.courant_ref, ...), custom_call_target="tpu_custom_call" | custom-call | tf_op jit(solution)/shard_map/second_local/pallas_call | solution.py:605
  17.9 1.2 %collective-permute-done.8.res_ref.ya_ref = f32[7,8,128]{2,1,0:T(8,128)S(1)} collective-permute-done((f32[7,8,128]{2,1,0:T(8,128)S(1)}, f32[7,8,128]{2,1,0:T(8,128)S(1)}, u32[]{:S(2)}, u32[]{:S(2)}) %collective-permute-start.8) | collective-permute-done | bytes 28704 | tf_op jit(solution)/shard_map/ppermute | solution.py:592
  19.1 0.3 %inject.1.layer_ref = f32[4,8,128]{2,1,0:T(8,128)S(1)} custom-call(f32[3,8,128]{2,1,0:T(8,128)S(1)} %get-tuple-element.35.before_ref.keep_ref, f32[7,8,128]{2,1,0:T(8,128)S(1)} %collective-permute-done.8.res_ref.ya_ref, s32[32,128]{1,0:T(8,128)S(1)} %get-tuple-element.31.before_ref.cell_ref, f32[64,8,128]{2,1,0:T(8,128)S(1)} %get-tuple-element.23.courant_ref), custom_call_target="tpu_custom_call" | custom-call | tf_op jit(solution)/shard_map/inject/pallas_call | solution.py:605
  19.5 0.0 collective-permute-done.9.yb_ref
  19.5 0.4 %collective-permute-done.7.xb_ref = f32[64,8,128]{2,1,0:T(8,128)S(1)} collective-permute-done((f32[64,8,128]{2,1,0:T(8,128)S(1)}, f32[64,8,128]{2,1,0:T(8,128)S(1)}, u32[]{:S(2)}, u32[]{:S(2)}) %collective-permute-start.7) | collective-permute-done | bytes 262176 | tf_op jit(solution)/shard_map/ppermute | solution.py:592
  19.9 0.0 collective-permute-done.6.xa_ref
  19.9 1.3 %after.1 = (f32[2,64,8,128]{3,2,1,0:T(8,128)}, f32[2,64,8,128]{3,2,1,0:T(8,128)}) custom-call(f32[2,64,8,128]{3,2,1,0:T(8,128)S(1)} %second_local.1.base_ref, f32[2,64,8,128]{3,2,1,0:T(8,128)S(1)} %get-tuple-element.28.before_ref.now_ref.mid_ref, f32[64,8,128]{2,1,0:T(8,128)S(1)} %get-tuple-element.23.courant_ref, ...), custom_call_target="tpu_custom_call" | custom-call | tf_op jit(solution)/shard_map/after/pallas_call | solution.py:605
  (3 shorter events, 0.1 us)
Async XLA Ops:
  2.2 3.5 %collective-permute-start = (f32[80,8,128]{2,1,0:T(8,128)S(1)}, f32[80,8,128]{2,1,0:T(8,128)S(1)}, u32[]{:S(2)}, u32[]{:S(2)}) collective-permute-start(f32[80,8,128]{2,1,0:T(8,128)S(1)} %get-tuple-element.24.own_ref), channel_id=1, source_target_pairs={{0,4},{1,5},{2,6},{3,7},{4,0},{5,1},{6,2},{7,3},{8,12},{9,13},{10,... | collective-permute-start | bytes 983048 | tf_op jit(solution)/shard_map/ppermute | solution.py:592
  2.8 9.6 %collective-permute-start.1 = (f32[64,8,128]{2,1,0:T(8,128)S(1)}, f32[64,8,128]{2,1,0:T(8,128)S(1)}, u32[]{:S(2)}, u32[]{:S(2)}) collective-permute-start(f32[64,8,128]{2,1,0:T(8,128)S(1)} %get-tuple-element.25), channel_id=1, source_target_pairs={{0,16},{1,17},{2,18},{3,19},{4,8},{5,9},{6,10},{7,11},{8,4},{9,5},... | collective-permute-start | bytes 786440 | tf_op jit(solution)/shard_map/ppermute | solution.py:592
  5.8 5.3 %collective-permute-start.4 = (f32[8,8,128]{2,1,0:T(8,128)S(1)}, f32[8,8,128]{2,1,0:T(8,128)S(1)}, u32[]{:S(2)}, u32[]{:S(2)}) collective-permute-start(f32[8,8,128]{2,1,0:T(8,128)S(1)} %get-tuple-element.30), channel_id=1, source_target_pairs={{0,2},{1,3},{2,0},{3,1},{4,6},{5,7},{6,4},{7,5},{8,10},{9,11},{10,... | collective-permute-start | bytes 98312 | tf_op jit(solution)/shard_map/ppermute | solution.py:592
  8.4 3.9 %collective-permute-start.2 = (f32[5,8,128]{2,1,0:T(8,128)S(1)}, f32[5,8,128]{2,1,0:T(8,128)S(1)}, u32[]{:S(2)}, u32[]{:S(2)}) collective-permute-start(f32[5,8,128]{2,1,0:T(8,128)S(1)} %get-tuple-element.26.before_ref), channel_id=1, source_target_pairs={{0,1},{1,0},{2,3},{3,2},{4,5},{5,4},{6,7},{7,6},{8,9},{9,8},{10,11... | collective-permute-start | bytes 61448 | tf_op jit(solution)/shard_map/ppermute | solution.py:592
  10.0 2.3 %collective-permute-start.3 = (f32[4,8,128]{2,1,0:T(8,128)S(1)}, f32[4,8,128]{2,1,0:T(8,128)S(1)}, u32[]{:S(2)}, u32[]{:S(2)}) collective-permute-start(f32[4,8,128]{2,1,0:T(8,128)S(1)} %get-tuple-element.27), channel_id=1, source_target_pairs={{0,4},{1,2},{2,1},{3,7},{4,0},{5,6},{6,5},{7,3},{8,12},{9,10},{10,... | collective-permute-start | bytes 49160 | tf_op jit(solution)/shard_map/ppermute | solution.py:592
  11.1 4.0 %collective-permute-start.5 = (f32[8,8,128]{2,1,0:T(8,128)S(1)}, f32[8,8,128]{2,1,0:T(8,128)S(1)}, u32[]{:S(2)}, u32[]{:S(2)}) collective-permute-start(f32[8,8,128]{2,1,0:T(8,128)S(1)} %sum.1.own_ref), channel_id=1, source_target_pairs={{0,8},{1,9},{2,10},{3,11},{4,12},{5,13},{6,14},{7,15},{8,0},{9,1},... | collective-permute-start | bytes 98312 | tf_op jit(solution)/shard_map/ppermute | solution.py:592
  13.5 6.4 %collective-permute-start.7 = (f32[64,8,128]{2,1,0:T(8,128)S(1)}, f32[64,8,128]{2,1,0:T(8,128)S(1)}, u32[]{:S(2)}, u32[]{:S(2)}) collective-permute-start(f32[64,8,128]{2,1,0:T(8,128)S(1)} %get-tuple-element.37), channel_id=1, source_target_pairs={{0,16},{1,17},{2,18},{3,19},{4,8},{5,9},{6,10},{7,11},{8,4},{9,5},... | collective-permute-start | bytes 786440 | tf_op jit(solution)/shard_map/ppermute | solution.py:592
  15.1 4.8 %collective-permute-start.6 = (f32[64,8,128]{2,1,0:T(8,128)S(1)}, f32[64,8,128]{2,1,0:T(8,128)S(1)}, u32[]{:S(2)}, u32[]{:S(2)}) collective-permute-start(f32[64,8,128]{2,1,0:T(8,128)S(1)} %get-tuple-element.36), channel_id=1, source_target_pairs={{0,4},{1,5},{2,6},{3,7},{4,0},{5,1},{6,2},{7,3},{8,12},{9,13},{10,... | collective-permute-start | bytes 786440 | tf_op jit(solution)/shard_map/ppermute | solution.py:592
  15.2 3.9 %collective-permute-start.8 = (f32[7,8,128]{2,1,0:T(8,128)S(1)}, f32[7,8,128]{2,1,0:T(8,128)S(1)}, u32[]{:S(2)}, u32[]{:S(2)}) collective-permute-start(f32[7,8,128]{2,1,0:T(8,128)S(1)} %get-tuple-element.38), channel_id=1, source_target_pairs={{0,1},{1,0},{2,3},{3,2},{4,5},{5,4},{6,7},{7,6},{8,9},{9,8},{10,11... | collective-permute-start | bytes 86024 | tf_op jit(solution)/shard_map/ppermute | solution.py:592
  16.8 2.7 %collective-permute-start.9 = (f32[4,8,128]{2,1,0:T(8,128)S(1)}, f32[4,8,128]{2,1,0:T(8,128)S(1)}, u32[]{:S(2)}, u32[]{:S(2)}) collective-permute-start(f32[4,8,128]{2,1,0:T(8,128)S(1)} %get-tuple-element.39), channel_id=1, source_target_pairs={{0,4},{1,2},{2,1},{3,7},{4,0},{5,6},{6,5},{7,3},{8,12},{9,10},{10,... | collective-permute-start | bytes 49160 | tf_op jit(solution)/shard_map/ppermute | solution.py:592
